TPU v7x, 256 devices: a whole 4x4x8 slice. The times are simulated.
256 devices in a mesh: lon: 16 (over x_hi, y, core), lat: 16 (over z, x_lo).
Axes of the slice: x: 4 (x_hi: 2, x_lo: 2; x = x_hi * 2 + x_lo), y: 4, z: 8, core: 2. Of those that a mesh axis runs over, the one named last changes fastest.
Arguments:
- background: bfloat16 [2, 128, 256, 2048], P(None, None, 'lat', 'lon'), may hold values from -6 to 6
- obs_cell: int32 [16, 16, 1024], P('lat', 'lon'), may hold values from 0 to 2047, as said below
- obs_count: int32 [16, 16], P('lat', 'lon'), may hold values from 128 to 1024, as said below
- obs_value: bfloat16 [16, 16, 1024], P('lat', 'lon'), may hold values from -6 to 6
- obs_err: float32 [16, 16, 1024], P('lat', 'lon'), may hold values from 0.5 to 2
- land: int32 [256, 2048], P('lat', 'lon'), may hold values 0 or 1
Outputs:
- analysis: bfloat16 [2, 128, 256, 2048], P(None, None, 'lat', 'lon')
Inputs may be any that keep to these rules, and one draw needn't show every extreme that they name: `obs_cell`: the 1024 cells named by one tile are distinct; a cell is numbered row * 128 + column within its tile. `obs_count`: some tile uses all its slots.
All inputs are finite; a program needn't handle non-finite values. No bound on the sum of `land` on one device may be relied on, other than what follows from the above.
Results may differ from a plain program's by a relative error of at most 0.0052.
Values may be sent and summed in bfloat16 or wider, within the bound.
No kernel may reach another device: no remote copies, remote signals or barrier semaphores. Data moves between devices by JAX's collectives and lax.ppermute only.
A program may use at most 64 MiB of HBM per device.

v0:
```python
import jax
import jax.numpy as jnp
import numpy as np
from jax import lax
from jax.experimental import pallas as pl
from jax.experimental.pallas import tpu as pltpu
from jax.sharding import PartitionSpec as P

MEMBERS = 128
PATCH = 16
RADIUS = 15
NS_ITERS = 5
ROWS = 16
COLS = 128
PATCHES = COLS // PATCH
CELLS = PATCH * PATCH
EXTRA = 16
CHANNELS = MEMBERS + EXTRA
PACKED = (PATCHES // 2) * MEMBERS + 16
NT = (((1,), (1,)), ((), ()))
VMEM_LIMIT = 48 * 1024 * 1024
F32 = jnp.float32
BF16 = jnp.bfloat16


def taper_table():
    line = np.arange(PATCH, dtype=np.float32)
    span = np.float32(2.0 * (RADIUS + PATCH / 2.0))
    half = np.float32((PATCH - 1) / 2.0)
    ahead = np.where(line >= 1, 1 - (PATCH + half - line) / span, 0)
    inside = 1 - np.abs(line - half) / span
    behind = np.where(line <= PATCH - 2, 1 - (line + PATCH - half) / span, 0)
    lon = np.stack([ahead, inside, behind])
    lat = np.stack([behind, inside, ahead])
    table = lat[:, None, :, None] * lon[None, :, None, :]
    full = np.zeros((8, 3 * CELLS), np.float32)
    full[:3] = table.reshape(3, 3 * CELLS)
    return full


def stencil_tables():
    rows, cols = np.divmod(np.arange(CELLS), PATCH)
    near = np.abs(rows[:, None] - rows[None, :]) <= 1
    main, rim = [], []
    for side in (-1, 0, 1):
        beside = np.abs(side * PATCH + cols[:, None] - cols[None, :]) <= 1
        main.append(near & beside)
        edge = np.zeros((COLS, CELLS), bool)
        column = np.arange(PATCH)
        reach = np.abs(side * PATCH + column[:, None] - cols[None, :]) <= 1
        edge[:PATCH] = reach & (rows == 0)[None, :]
        edge[PATCH : 2 * PATCH] = reach & (rows == ROWS - 1)[None, :]
        rim.append(edge)
    return np.concatenate(main, 0), np.concatenate(rim, 0)


def swap_groups(arrays):
    lane = lax.broadcasted_iota(jnp.int32, arrays[0].shape, 1)
    for step in (1, 2, 4):
        width = PATCH * step
        high = (lane & width) != 0
        mixed = list(arrays)
        for i in range(8):
            if i & step == 0:
                first, second = arrays[i], arrays[i + step]
                mixed[i] = jnp.where(high, pltpu.roll(second, width, 1), first)
                mixed[i + step] = jnp.where(high, second, pltpu.roll(first, COLS - width, 1))
        arrays = mixed
    return arrays


def to_blocks(field_ref, index, out_ref, scratch):
    for m in range(MEMBERS // 16):
        piece = field_ref[index, pl.ds(m * 16, 16)].astype(F32)
        scratch[pl.ds(m * 256, 256), :] = piece.reshape(256, COLS)
    for m in range(MEMBERS // 16):
        halves = []
        for g in range(2):
            lines = [
                scratch[pl.ds(m * 256 + g * 8 + r, 16, stride=16), :] for r in range(8)
            ]
            halves.append(swap_groups(lines))
        for b in range(PATCHES):
            both = jnp.concatenate([halves[0][b], halves[1][b]], axis=1)
            out_ref[pl.ds(m * 16, 16), pl.ds(b * CELLS, CELLS)] = both.astype(BF16)


def layout_kernel(field_ref, cell_ref, count_ref, value_ref, err_ref, land_ref, blocks_ref, mask_ref, scratch):
    to_blocks(field_ref, 0, blocks_ref, scratch)
    land = land_ref[...].astype(F32)
    halves = []
    for g in range(2):
        lines = [jnp.broadcast_to(land[g * 8 + r : g * 8 + r + 1], (8, COLS)) for r in range(8)]
        halves.append(swap_groups(lines))
    which = lax.broadcasted_iota(jnp.int32, (8, CELLS), 0)
    mask = jnp.zeros((8, CELLS), F32)
    for b in range(PATCHES):
        mask = jnp.where(which == b, jnp.concatenate([halves[0][b], halves[1][b]], axis=1), mask)
    mask_ref[...] = mask
    cell = cell_ref[...]
    slots = cell.shape[1]
    used = lax.broadcasted_iota(jnp.int32, (1, slots), 1) < count_ref[0, 0]
    err = err_ref[...]
    inverse = jnp.where(used, 1.0 / (err * err), 0.0)
    value = jnp.where(used, value_ref[...].astype(F32), 0.0)
    column = cell & (COLS - 1)
    block = column >> 4
    place = ((cell >> 7) << 4) + (column & (PATCH - 1))
    slot_block = lax.broadcasted_iota(jnp.int32, (16, slots), 0)
    chosen = (slot_block & 7) == block
    amount = jnp.where(slot_block < 8, inverse, value)
    left = jnp.where(chosen, amount, 0.0).astype(BF16)
    spot = lax.broadcasted_iota(jnp.int32, (CELLS, slots), 0) == place
    right = jnp.where(spot, 1.0, 0.0).astype(BF16)
    grids = lax.dot_general(left, right, NT, preferred_element_type=F32)
    precision = grids[:8] * mask
    observed = grids[8:]
    row = lax.broadcasted_iota(jnp.int32, (EXTRA, CELLS), 0)
    for b in range(PATCHES):
        tail = jnp.where(row == 0, precision[b : b + 1], jnp.where(row == 1, observed[b : b + 1], 0.0))
        blocks_ref[pl.ds(MEMBERS, EXTRA), pl.ds(b * CELLS, CELLS)] = tail.astype(BF16)


def rim_kernel(first_ref, second_ref, blocks_ref, rim_ref, even_ref, odd_ref):
    lat_odd = (lax.axis_index("lat") & 1) == 1
    lon_odd = (lax.axis_index("lon") & 1) == 1
    first = first_ref[...].astype(F32)
    second = second_ref[...].astype(F32)
    above = jnp.where(lat_odd, first, second)
    below = jnp.where(lat_odd, second, first)
    lane = lax.broadcasted_iota(jnp.int32, (MEMBERS, COLS), 1)
    for b in range(PATCHES):
        top = pltpu.roll(above, (COLS - PATCH * b) % COLS, 1)
        low = pltpu.roll(below, (COLS - PATCH * b + PATCH) % COLS, 1)
        edge = jnp.where(lane < PATCH, top, jnp.where(lane < 2 * PATCH, low, 0.0)).astype(BF16)
        rim_ref[:, pl.ds(b * COLS, COLS)] = edge
        if b == 0:
            west_rim = edge
        if b == PATCHES - 1:
            east_rim = edge
    west = blocks_ref[:, pl.ds(0, CELLS)]
    east = blocks_ref[:, pl.ds((PATCHES - 1) * CELLS, CELLS)]
    even_ref[:, pl.ds(0, CELLS)] = jnp.where(lon_odd, west, east)
    odd_ref[:, pl.ds(0, CELLS)] = jnp.where(lon_odd, east, west)
    even_ref[pl.ds(0, MEMBERS), pl.ds(CELLS, COLS)] = jnp.where(lon_odd, west_rim, east_rim)
    odd_ref[pl.ds(0, MEMBERS), pl.ds(CELLS, COLS)] = jnp.where(lon_odd, east_rim, west_rim)
    blank = jnp.zeros((EXTRA, COLS), BF16)
    even_ref[pl.ds(MEMBERS, EXTRA), pl.ds(CELLS, COLS)] = blank
    odd_ref[pl.ds(MEMBERS, EXTRA), pl.ds(CELLS, COLS)] = blank


def gram_kernel(
    blocks_ref, rim_ref, first_ref, second_ref, taper_ref, main_ref, edge_ref,
    even_ref, odd_ref, gram_ref, force_ref, wide, wide_rim, pert,
):
    lat = lax.axis_index("lat")
    lat_odd = (lat & 1) == 1
    lon_odd = (lax.axis_index("lon") & 1) == 1
    span = PATCHES * CELLS
    wide[:, pl.ds(0, CELLS)] = jnp.zeros((CHANNELS, CELLS), BF16)
    wide[:, pl.ds(span + 3 * CELLS, CELLS)] = jnp.zeros((CHANNELS, CELLS), BF16)
    wide[:, pl.ds(2 * CELLS, span)] = blocks_ref[...]
    one = first_ref[:, pl.ds(0, CELLS)]
    two = second_ref[:, pl.ds(0, CELLS)]
    wide[:, pl.ds(CELLS, CELLS)] = jnp.where(lon_odd, one, two)
    wide[:, pl.ds(span + 2 * CELLS, CELLS)] = jnp.where(lon_odd, two, one)
    rim_span = PATCHES * COLS
    blank = jnp.zeros((MEMBERS, COLS), BF16)
    wide_rim[:, pl.ds(0, COLS)] = blank
    wide_rim[:, pl.ds(rim_span + 3 * COLS, COLS)] = blank
    wide_rim[:, pl.ds(2 * COLS, rim_span)] = rim_ref[...]
    one = first_ref[pl.ds(0, MEMBERS), pl.ds(CELLS, COLS)]
    two = second_ref[pl.ds(0, MEMBERS), pl.ds(CELLS, COLS)]
    wide_rim[:, pl.ds(COLS, COLS)] = jnp.where(lon_odd, one, two)
    wide_rim[:, pl.ds(rim_span + 2 * COLS, COLS)] = jnp.where(lon_odd, two, one)

    lane = lax.broadcasted_iota(jnp.int32, (1, CELLS), 1)
    row = lane >> 4
    last = lax.axis_size("lat") - 1
    short = ((row == 0) & (lat == 0)) | ((row == ROWS - 1) & (lat == last))
    share = jnp.where(short, 1.0 / 6.0, 1.0 / 9.0)
    tail_row = lax.broadcasted_iota(jnp.int32, (EXTRA, CELLS), 0)
    for e in range(PATCHES + 2):
        summed = jnp.dot(
            wide[pl.ds(0, MEMBERS), pl.ds(e * CELLS, 3 * CELLS)], main_ref[...], preferred_element_type=F32
        )
        summed = summed + jnp.dot(
            wide_rim[:, pl.ds(e * COLS, 3 * COLS)], edge_ref[...], preferred_element_type=F32
        )
        mean = summed * share
        average = jnp.sum(mean, axis=0, keepdims=True) * (1.0 / MEMBERS)
        pert[pl.ds(0, MEMBERS), pl.ds(e * CELLS, CELLS)] = (mean - average).astype(BF16)
        tail = wide[pl.ds(MEMBERS, EXTRA), pl.ds((e + 1) * CELLS, CELLS)].astype(F32)
        innovation = tail[1:2] - average
        pert[pl.ds(MEMBERS, EXTRA), pl.ds(e * CELLS, CELLS)] = jnp.where(
            tail_row == 0, innovation, 0.0
        ).astype(BF16)

    r = lax.broadcasted_iota(jnp.int32, (MEMBERS, MEMBERS), 0)
    c = lax.broadcasted_iota(jnp.int32, (MEMBERS, MEMBERS), 1)
    lower = r >= c
    same = r == c
    base = (PATCHES // 2) * MEMBERS
    tails = [[], [], []]
    diagonals = [[], [], []]
    for pair in range(PATCHES // 2):
        kept = [None, None, None]
        for p in (2 * pair, 2 * pair + 1):
            window = pert[:, pl.ds(p * CELLS, 3 * CELLS)]
            members = window[:MEMBERS].astype(F32)
            precision = wide[pl.ds(MEMBERS, EXTRA), pl.ds((p + 1) * CELLS, 3 * CELLS)].astype(F32)[0:1]
            for s in range(3):
                weight = precision * taper_ref[s : s + 1, :]
                scaled = (members * weight).astype(BF16)
                full = lax.dot_general(scaled, window, NT, preferred_element_type=F32)
                gram = full[:, :MEMBERS]
                forcing = jnp.sum(jnp.where(same, full[:, MEMBERS : MEMBERS + 1], 0.0), axis=0, keepdims=True)
                tails[s].append(forcing)
                if s == 1:
                    gram_ref[p] = gram
                elif p == 2 * pair:
                    kept[s] = gram
                else:
                    diagonals[s].append(jnp.sum(jnp.where(same, gram, 0.0), axis=0, keepdims=True))
                    kept[s] = jnp.where(lower, kept[s], gram)
        even_ref[pl.ds(pair * MEMBERS, MEMBERS), :] = jnp.where(lat_odd, kept[0], kept[2]).astype(BF16)
        odd_ref[pl.ds(pair * MEMBERS, MEMBERS), :] = jnp.where(lat_odd, kept[2], kept[0]).astype(BF16)
    force_ref[...] = jnp.concatenate(tails[1], axis=0)
    gap = [jnp.zeros((4, MEMBERS), F32)]
    up = jnp.concatenate(tails[0] + diagonals[0] + gap, axis=0)
    down = jnp.concatenate(tails[2] + diagonals[2] + gap, axis=0)
    even_ref[pl.ds(base, 16), :] = jnp.where(lat_odd, up, down).astype(BF16)
    odd_ref[pl.ds(base, 16), :] = jnp.where(lat_odd, down, up).astype(BF16)


def split(a):
    high = a.astype(BF16)
    return high, (a - high.astype(F32)).astype(BF16)


def product(a, b):
    a_high, a_low = split(a)
    b_high, b_low = split(b)
    wide = jnp.concatenate([b_high, b_low], axis=1)
    out = jnp.dot(
        jnp.concatenate([a_high, a_low], axis=1),
        jnp.concatenate([wide, wide], axis=0),
        preferred_element_type=F32,
    )
    return out[:, :MEMBERS] + out[:, MEMBERS:]


def solve_kernel(first_ref, second_ref, gram_ref, force_ref, field_ref, blocks_ref, mask_ref, out_ref,
                 upper, lower_ref, soil, scratch, spread):
    to_blocks(field_ref, 0, soil, scratch)
    r = lax.broadcasted_iota(jnp.int32, (MEMBERS, MEMBERS), 0)
    c = lax.broadcasted_iota(jnp.int32, (MEMBERS, MEMBERS), 1)
    eye = jnp.where(r == c, 1.0, 0.0)
    base = (PATCHES // 2) * MEMBERS
    tail = first_ref[pl.ds(base, 16), :].astype(F32) + second_ref[pl.ds(base, 16), :].astype(F32)
    norms = []
    for pair in range(PATCHES // 2):
        rows = pl.ds(pair * MEMBERS, MEMBERS)
        mixed = first_ref[rows, :].astype(F32) + second_ref[rows, :].astype(F32)
        turned = mixed.T
        diagonal = tail[8 + pair : 9 + pair]
        gains = (
            jnp.where(r >= c, mixed, turned),
            jnp.where(r > c, turned, jnp.where(r < c, mixed, diagonal)),
        )
        for k in range(2):
            p = 2 * pair + k
            system = (MEMBERS - 1.0) * eye + (gram_ref[p] + gains[k])
            total = jnp.sum(jnp.sum(system * system, axis=0, keepdims=True), axis=1, keepdims=True)
            norm = jnp.sqrt(total)
            norms.append(norm)
            scaled = system * (1.0 / norm)
            upper[p] = 1.5 * scaled - 0.5 * product(scaled, scaled)
            lower_ref[p] = 1.5 * eye - 0.5 * scaled

    def sweep(_, carry):
        middles = [1.5 * eye - 0.5 * product(lower_ref[p], upper[p]) for p in range(PATCHES)]
        for p in range(PATCHES):
            both = product(jnp.concatenate([upper[p], lower_ref[p]], axis=0), middles[p])
            upper[p] = both[:MEMBERS]
            lower_ref[p] = both[MEMBERS:]
        return carry

    lax.fori_loop(0, NS_ITERS - 2, sweep, 0)
    for p in range(PATCHES):
        middle = 1.5 * eye - 0.5 * product(lower_ref[p], upper[p])
        lower = product(lower_ref[p], middle)
        forcing = jnp.broadcast_to(force_ref[p : p + 1] + tail[p : p + 1], (16, MEMBERS))
        mean_weight = product(product(forcing, lower), lower)[0:1] * (1.0 / norms[p])
        scale = jnp.sqrt(MEMBERS - 1.0) / jnp.sqrt(norms[p])
        transform = (lower * scale + mean_weight).astype(BF16)
        cells = pl.ds(p * CELLS, CELLS)
        raw = jnp.concatenate([blocks_ref[pl.ds(0, MEMBERS), cells], soil[:, cells]], axis=1).astype(F32)
        mean = jnp.sum(raw, axis=0, keepdims=True) * (1.0 / MEMBERS)
        departure = (raw - mean).astype(BF16)
        updated = mean + jnp.dot(transform, departure, preferred_element_type=F32)
        land = mask_ref[p : p + 1, :]
        keep = jnp.concatenate([land, land], axis=1) != 0.0
        spread[:, pl.ds(p * 2 * CELLS, 2 * CELLS)] = jnp.where(keep, updated, raw)

    for v in range(2):
        for m in range(MEMBERS // 16):
            rows = pl.ds(m * 16, 16)
            for g in range(2):
                groups = [
                    spread[rows, pl.ds(b * 2 * CELLS + v * CELLS + g * COLS, COLS)] for b in range(PATCHES)
                ]
                lines = swap_groups(groups)
                for k in range(8):
                    scratch[pl.ds(m * 256 + g * 8 + k, 16, stride=16), :] = lines[k]
            out_ref[v, rows] = scratch[pl.ds(m * 256, 256), :].reshape(16, ROWS, COLS).astype(BF16)


def call(kernel, out_shape, scratch, flops, moved, *operands, in_specs=None):
    vmem = pl.BlockSpec(memory_space=pltpu.VMEM)
    return pl.pallas_call(
        kernel,
        out_shape=out_shape,
        grid=(1,),
        in_specs=in_specs or [vmem] * len(operands),
        out_specs=[vmem] * len(out_shape),
        scratch_shapes=scratch,
        compiler_params=pltpu.CompilerParams(vmem_limit_bytes=VMEM_LIMIT),
        cost_estimate=pl.CostEstimate(flops=flops, bytes_accessed=moved, transcendentals=0),
    )(*operands)


def pairs_inside(size):
    return [(i, i ^ 1) for i in range(size)]


def pairs_across(size, wrap):
    pairs = []
    for i in range(1, size - 1, 2):
        pairs += [(i, i + 1), (i + 1, i)]
    if wrap:
        pairs += [(size - 1, 0), (0, size - 1)]
    return pairs


def exchange(even, odd, axis, wrap):
    size = lax.axis_size(axis)
    return (
        lax.ppermute(even, axis, pairs_inside(size)),
        lax.ppermute(odd, axis, pairs_across(size, wrap)),
    )


def body(background, obs_cell, obs_count, obs_value, obs_err, land):
    vmem = pl.BlockSpec(memory_space=pltpu.VMEM)
    smem = pl.BlockSpec(memory_space=pltpu.SMEM)
    slots = obs_cell.shape[-1]
    span = PATCHES * CELLS
    shape = jax.ShapeDtypeStruct
    lat_odd = (lax.axis_index("lat") & 1) == 1
    top, bottom = background[0, :, 0], background[0, :, ROWS - 1]
    rows = exchange(
        jnp.where(lat_odd, top, bottom), jnp.where(lat_odd, bottom, top), "lat", False
    )
    blocks, mask = call(
        layout_kernel,
        [shape((CHANNELS, span), BF16), shape((8, CELLS), F32)],
        [pltpu.VMEM((MEMBERS * ROWS, COLS), F32)],
        10**7, 2 * 10**6,
        background, obs_cell.reshape(1, slots), obs_count, obs_value.reshape(1, slots),
        obs_err.reshape(1, slots), land,
        in_specs=[pl.BlockSpec((1, MEMBERS, ROWS, COLS), lambda i: (0, 0, 0, 0)), vmem, smem, vmem, vmem, vmem],
    )
    rim, even, odd = call(
        rim_kernel,
        [shape((MEMBERS, PATCHES * COLS), BF16)] + [shape((CHANNELS, CELLS + COLS), BF16)] * 2,
        [], 10**6, 10**6, *rows, blocks,
    )
    sides = exchange(even, odd, "lon", True)
    main, edge = stencil_tables()
    even, odd, gram, force = call(
        gram_kernel,
        [shape((PACKED, MEMBERS), BF16)] * 2
        + [shape((PATCHES, MEMBERS, MEMBERS), F32), shape((PATCHES, MEMBERS), F32)],
        [
            pltpu.VMEM((CHANNELS, span + 4 * CELLS), BF16),
            pltpu.VMEM((MEMBERS, (PATCHES + 4) * COLS), BF16),
            pltpu.VMEM((CHANNELS, span + 2 * CELLS), BF16),
        ],
        10**9, 3 * 10**6,
        blocks, rim, *sides, jnp.asarray(taper_table()), jnp.asarray(main, BF16), jnp.asarray(edge, BF16),
    )
    packed = exchange(even, odd, "lat", False)
    (analysis,) = call(
        solve_kernel,
        [shape(background.shape, BF16)],
        [
            pltpu.VMEM((PATCHES, MEMBERS, MEMBERS), F32),
            pltpu.VMEM((PATCHES, MEMBERS, MEMBERS), F32),
            pltpu.VMEM((MEMBERS, span), BF16),
            pltpu.VMEM((MEMBERS * ROWS, COLS), F32),
            pltpu.VMEM((MEMBERS, 2 * span), F32),
        ],
        2 * 10**9, 5 * 10**6,
        *packed, gram, force, background, blocks, mask,
        in_specs=[vmem] * 4 + [pl.BlockSpec((1, MEMBERS, ROWS, COLS), lambda i: (1, 0, 0, 0)), vmem, vmem],
    )
    return analysis


def solution(mesh):
    return jax.shard_map(
        body,
        mesh=mesh,
        in_specs=(
            P(None, None, "lat", "lon"),
            P("lat", "lon", None),
            P("lat", "lon"),
            P("lat", "lon", None),
            P("lat", "lon", None),
            P("lat", "lon"),
        ),
        out_specs=P(None, None, "lat", "lon"),
        check_vma=False,
    )
```

profile of v0, /device:TPU:102, one launch (start us, length us, event | category | flops | bytes accessed | tf_op | source)
XLA Modules:
  0.0 44.0 jit_solution(5058410519851608217)
XLA Ops:
  0.0 1.1 %fusion = (bf16[1,128,1,128]{3,2,1,0:T(2,128)(2,1)S(1)}, bf16[1,128,1,128]{3,2,1,0:T(2,128)(2,1)S(1)}) fusion(bf16[2,128,16,128]{3,2,1,0:T(8,128)(2,1)} %field_ref.3), kind=kLoop, calls=%fused_computation.2 | loop fusion | bytes 131072 | tf_op jit(solution)/shard_map/slice | solution.py:361
  1.1 0.0 copy-start.3
  1.1 0.0 copy-start.4
  1.2 0.0 copy-start.5
  1.2 0.0 copy-start.2
  1.2 5.3 %collective-permute-start.1 = (bf16[128,128]{1,0:T(8,128)(2,1)S(1)}, bf16[128,128]{1,0:T(8,128)(2,1)S(1)}, u32[]{:S(2)}, u32[]{:S(2)}) collective-permute-start(bf16[128,128]{1,0:T(8,128)(2,1)S(1)} %get-tuple-element.25), channel_id=1, source_target_pairs={{1,2},{2,1},{3,4},{4,3},{5,6},{6,5},{7,8},{8,7},{9,10},{10,9},{11,... | collective-permute-start | bytes 98312 | tf_op jit(solution)/shard_map/ppermute | solution.py:350
  6.5 0.1 collective-permute-start
  7.3 0.0 copy-done.3
  7.3 0.0 copy-done.4
  7.3 0.0 copy-done.5
  7.3 0.0 copy-done.2
  7.3 0.0 copy-start
  7.3 1.2 %copy-done = bf16[2,128,16,128]{3,2,1,0:T(8,128)(2,1)S(1)} copy-done((bf16[2,128,16,128]{3,2,1,0:T(8,128)(2,1)S(1)}, bf16[2,128,16,128]{3,2,1,0:T(8,128)(2,1)}, u32[]{:S(2)}) %copy-start) | copy-done | bytes 1048600
  8.5 2.0 %shard_map.91 = (bf16[144,2048]{1,0:T(8,128)(2,1)S(1)}, f32[8,256]{1,0:T(8,128)S(1)}) custom-call(bf16[2,128,16,128]{3,2,1,0:T(8,128)(2,1)S(1)} %copy-done, s32[1,1024]{1,0:T(1,128)S(1)} %bitcast.7, s32[1,1]{1,0:T(1,128)S(6)} %copy.18.count_ref, bf16[1,1024]{1,0:T(2,128)(2,1)S(1)} %bitcast.8, f32[1,1024]{1,0:T(1,128)S(1)} %bitcast.9, s32[16,128]{1,0:T(8,128)S(1)} %copy-done.2), custom_call_target="tpu_custom_call" | custom-call | flops 10000000 | bytes 2000000 | tf_op jit(solution)/shard_map/pallas_call | solution.py:321
  10.5 0.0 copy-start.6
  10.5 0.0 collective-permute-done.1.second_ref
  10.6 0.0 collective-permute-done.first_ref
  10.6 0.0 copy-start.7
  10.6 0.0 copy-start.8
  10.6 0.2 shard_map.92
  10.8 0.1 collective-permute-start.2
  10.9 3.7 %collective-permute-start.3 = (bf16[144,384]{1,0:T(8,128)(2,1)S(1)}, bf16[144,384]{1,0:T(8,128)(2,1)S(1)}, u32[]{:S(2)}, u32[]{:S(2)}) collective-permute-start(bf16[144,384]{1,0:T(8,128)(2,1)S(1)} %get-tuple-element.17), channel_id=1, source_target_pairs={{16,32},{32,16},{48,64},{64,48},{80,96},{96,80},{112,128},{128,112... | collective-permute-start | bytes 331784 | tf_op jit(solution)/shard_map/ppermute | solution.py:350
  14.6 0.0 collective-permute-done.2.first_ref
  14.6 4.2 %collective-permute-done.3.second_ref = bf16[144,384]{1,0:T(8,128)(2,1)S(1)} collective-permute-done((bf16[144,384]{1,0:T(8,128)(2,1)S(1)}, bf16[144,384]{1,0:T(8,128)(2,1)S(1)}, u32[]{:S(2)}, u32[]{:S(2)}) %collective-permute-start.3) | collective-permute-done | bytes 110624 | tf_op jit(solution)/shard_map/ppermute | solution.py:350
  18.8 0.0 copy-done.6
  18.8 0.0 copy-done.7
  18.8 0.0 copy-done.8
  18.8 0.0 copy-start.1
  18.8 2.6 %shard_map.93 = (bf16[528,128]{1,0:T(8,128)(2,1)S(1)}, bf16[528,128]{1,0:T(8,128)(2,1)S(1)}, f32[8,128,128]{2,1,0:T(8,128)S(1)}, f32[8,128]{1,0:T(8,128)S(1)}) custom-call(bf16[144,2048]{1,0:T(8,128)(2,1)S(1)} %get-tuple-element.14.blocks_ref, bf16[128,1024]{1,0:T(8,128)(2,1)S(1)} %get-tuple-element.15.rim_ref, ...), custom_call_target="tpu_custom_call" | custom-call | flops 1000000000 | bytes 3000000 | tf_op jit(solution)/shard_map/pallas_call | solution.py:321
  21.4 2.1 %collective-permute-start.4 = (bf16[528,128]{1,0:T(8,128)(2,1)S(1)}, bf16[528,128]{1,0:T(8,128)(2,1)S(1)}, u32[]{:S(2)}, u32[]{:S(2)}) collective-permute-start(bf16[528,128]{1,0:T(8,128)(2,1)S(1)} %get-tuple-element.18), channel_id=1, source_target_pairs={{0,1},{1,0},{2,3},{3,2},{4,5},{5,4},{6,7},{7,6},{8,9},{9,8},{10,11... | collective-permute-start | bytes 405512 | tf_op jit(solution)/shard_map/ppermute | solution.py:349
  23.5 2.6 %collective-permute-start.5 = (bf16[528,128]{1,0:T(8,128)(2,1)S(1)}, bf16[528,128]{1,0:T(8,128)(2,1)S(1)}, u32[]{:S(2)}, u32[]{:S(2)}) collective-permute-start(bf16[528,128]{1,0:T(8,128)(2,1)S(1)} %get-tuple-element.19), channel_id=1, source_target_pairs={{1,2},{2,1},{3,4},{4,3},{5,6},{6,5},{7,8},{8,7},{9,10},{10,9},{11,... | collective-permute-start | bytes 405512 | tf_op jit(solution)/shard_map/ppermute | solution.py:350
  26.2 0.3 collective-permute-done.4.first_ref
  26.5 6.0 %collective-permute-done.5.second_ref = bf16[528,128]{1,0:T(8,128)(2,1)S(1)} collective-permute-done((bf16[528,128]{1,0:T(8,128)(2,1)S(1)}, bf16[528,128]{1,0:T(8,128)(2,1)S(1)}, u32[]{:S(2)}, u32[]{:S(2)}) %collective-permute-start.5) | collective-permute-done | bytes 135200 | tf_op jit(solution)/shard_map/ppermute | solution.py:350
  32.5 0.0 copy-done.1
  32.5 11.5 %shard_map.94 = bf16[2,128,16,128]{3,2,1,0:T(8,128)(2,1)} custom-call(bf16[528,128]{1,0:T(8,128)(2,1)S(1)} %collective-permute-done.4.first_ref, bf16[528,128]{1,0:T(8,128)(2,1)S(1)} %collective-permute-done.5.second_ref, f32[8,128,128]{2,1,0:T(8,128)S(1)} %get-tuple-element.20.gram_ref, f32[8,128]{1,0:T(8,128)S(1)} %get-tuple-element.21.force_ref, ...), custom_call_target="tpu_custom_call" | custom-call | flops 2000000000 | bytes 5000000 | tf_op jit(solution)/shard_map/pallas_call | solution.py:321
  (1 shorter events, 0.0 us)
Async XLA Ops:
  1.1 6.1 %copy-start.3 = (s32[1,1,1024]{2,1,0:T(1,128)S(1)}, s32[1,1,1024]{2,1,0:T(1,128)}, u32[]{:S(2)}) copy-start(s32[1,1,1024]{2,1,0:T(1,128)} %param.10) | copy-start | bytes 12292
  1.1 6.1 %copy-start.4 = (bf16[1,1,1024]{2,1,0:T(2,128)(2,1)S(1)}, bf16[1,1,1024]{2,1,0:T(2,128)(2,1)}, u32[]{:S(2)}) copy-start(bf16[1,1,1024]{2,1,0:T(2,128)(2,1)} %param.12) | copy-start | bytes 6148
  1.2 6.1 %copy-start.5 = (f32[1,1,1024]{2,1,0:T(1,128)S(1)}, f32[1,1,1024]{2,1,0:T(1,128)}, u32[]{:S(2)}) copy-start(f32[1,1,1024]{2,1,0:T(1,128)} %param.13) | copy-start | bytes 12292
  1.2 6.1 %copy-start.2 = (s32[16,128]{1,0:T(8,128)S(1)}, s32[16,128]{1,0:T(8,128)}, u32[]{:S(2)}) copy-start(s32[16,128]{1,0:T(8,128)} %land_ref.1) | copy-start | bytes 24580
  1.2 9.3 %collective-permute-start.1 = (bf16[128,128]{1,0:T(8,128)(2,1)S(1)}, bf16[128,128]{1,0:T(8,128)(2,1)S(1)}, u32[]{:S(2)}, u32[]{:S(2)}) collective-permute-start(bf16[128,128]{1,0:T(8,128)(2,1)S(1)} %get-tuple-element.25), channel_id=1, source_target_pairs={{1,2},{2,1},{3,4},{4,3},{5,6},{6,5},{7,8},{8,7},{9,10},{10,9},{11,... | collective-permute-start | bytes 98312 | tf_op jit(solution)/shard_map/ppermute | solution.py:350
  6.5 4.0 %collective-permute-start = (bf16[128,128]{1,0:T(8,128)(2,1)S(1)}, bf16[128,128]{1,0:T(8,128)(2,1)S(1)}, u32[]{:S(2)}, u32[]{:S(2)}) collective-permute-start(bf16[128,128]{1,0:T(8,128)(2,1)S(1)} %get-tuple-element.26), channel_id=1, source_target_pairs={{0,1},{1,0},{2,3},{3,2},{4,5},{5,4},{6,7},{7,6},{8,9},{9,8},{10,11... | collective-permute-start | bytes 98312 | tf_op jit(solution)/shard_map/ppermute | solution.py:349
  7.3 1.2 %copy-start = (bf16[2,128,16,128]{3,2,1,0:T(8,128)(2,1)S(1)}, bf16[2,128,16,128]{3,2,1,0:T(8,128)(2,1)}, u32[]{:S(2)}) copy-start(bf16[2,128,16,128]{3,2,1,0:T(8,128)(2,1)} %field_ref.3) | copy-start | bytes 3145732
  10.5 8.2 %copy-start.6 = (bf16[768,256]{1,0:T(8,128)(2,1)S(1)}, bf16[768,256]{1,0:T(8,128)(2,1)}, u32[]{:S(2)}) copy-start(bf16[768,256]{1,0:T(8,128)(2,1)} %constant.13.clone.main_ref) | copy-start | bytes 1179652
  10.6 8.2 %copy-start.7 = (bf16[384,256]{1,0:T(8,128)(2,1)S(1)}, bf16[384,256]{1,0:T(8,128)(2,1)}, u32[]{:S(2)}) copy-start(bf16[384,256]{1,0:T(8,128)(2,1)} %constant.14.clone.edge_ref) | copy-start | bytes 589828
  10.6 8.2 %copy-start.8 = (f32[8,768]{1,0:T(8,128)S(1)}, f32[8,768]{1,0:T(8,128)}, u32[]{:S(2)}) copy-start(f32[8,768]{1,0:T(8,128)} %constant.12.clone.taper_ref) | copy-start | bytes 73732
  10.8 3.8 %collective-permute-start.2 = (bf16[144,384]{1,0:T(8,128)(2,1)S(1)}, bf16[144,384]{1,0:T(8,128)(2,1)S(1)}, u32[]{:S(2)}, u32[]{:S(2)}) collective-permute-start(bf16[144,384]{1,0:T(8,128)(2,1)S(1)} %get-tuple-element.16), channel_id=1, source_target_pairs={{0,16},{16,0},{32,48},{48,32},{64,80},{80,64},{96,112},{112,96},{1... | collective-permute-start | bytes 331784 | tf_op jit(solution)/shard_map/ppermute | solution.py:349
  10.9 7.9 %collective-permute-start.3 = (bf16[144,384]{1,0:T(8,128)(2,1)S(1)}, bf16[144,384]{1,0:T(8,128)(2,1)S(1)}, u32[]{:S(2)}, u32[]{:S(2)}) collective-permute-start(bf16[144,384]{1,0:T(8,128)(2,1)S(1)} %get-tuple-element.17), channel_id=1, source_target_pairs={{16,32},{32,16},{48,64},{64,48},{80,96},{96,80},{112,128},{128,112... | collective-permute-start | bytes 331784 | tf_op jit(solution)/shard_map/ppermute | solution.py:350
  18.8 13.7 %copy-start.1 = (bf16[2,128,16,128]{3,2,1,0:T(8,128)(2,1)S(1)}, bf16[2,128,16,128]{3,2,1,0:T(8,128)(2,1)}, u32[]{:S(2)}) copy-start(bf16[2,128,16,128]{3,2,1,0:T(8,128)(2,1)} %field_ref.3) | copy-start | bytes 3145732
  21.4 5.1 %collective-permute-start.4 = (bf16[528,128]{1,0:T(8,128)(2,1)S(1)}, bf16[528,128]{1,0:T(8,128)(2,1)S(1)}, u32[]{:S(2)}, u32[]{:S(2)}) collective-permute-start(bf16[528,128]{1,0:T(8,128)(2,1)S(1)} %get-tuple-element.18), channel_id=1, source_target_pairs={{0,1},{1,0},{2,3},{3,2},{4,5},{5,4},{6,7},{7,6},{8,9},{9,8},{10,11... | collective-permute-start | bytes 405512 | tf_op jit(solution)/shard_map/ppermute | solution.py:349
  23.5 9.0 %collective-permute-start.5 = (bf16[528,128]{1,0:T(8,128)(2,1)S(1)}, bf16[528,128]{1,0:T(8,128)(2,1)S(1)}, u32[]{:S(2)}, u32[]{:S(2)}) collective-permute-start(bf16[528,128]{1,0:T(8,128)(2,1)S(1)} %get-tuple-element.19), channel_id=1, source_target_pairs={{1,2},{2,1},{3,4},{4,3},{5,6},{6,5},{7,8},{8,7},{9,10},{10,9},{11,... | collective-permute-start | bytes 405512 | tf_op jit(solution)/shard_map/ppermute | solution.py:350
where the time goes:
time: 44.2 us; the launch traced here: 44 us
  Pallas kernels  16.3 us (37%)
  starting transfers between devices  13.9 us (31%)
  waiting for transfers between devices  10.6 us (24%)
  local copies, waits for them, and re-layouts  2.41 us (5%)
  between operations  0.84 us (2%)
    pallas_call x4, Pallas kernels, call(): pl.pallas_call(kernel, out_shape=out_shape, grid=(1,), in_specs=in_specs...  16.3 us
    ppermute x3, starting transfers between devices, exchange(): lax.ppermute(odd, axis, pairs_across(size, wrap))  11.6 us
    ppermute x3, waiting for transfers between devices, exchange(): lax.ppermute(odd, axis, pairs_across(size, wrap))  10.2 us
    ppermute x3, starting transfers between devices, exchange(): lax.ppermute(even, axis, pairs_inside(size))  2.28 us
    unnamed x18, local copies, waits for them, and re-layouts  1.27 us
    slice x1, local copies, waits for them, and re-layouts, body(): top, bottom = (background[0, :, 0], background[0, :, ROWS - 1])  1.13 us
  transfers between devices with their start and end apart: 6, of which 3 were waited for; matrix products, arithmetic and copies ran while one was open for 0% of the time, Pallas kernels for 5%

commit v1 on v0

v1 whole, which is shorter than its diff:
```python
import jax
import jax.numpy as jnp
import numpy as np
from jax import lax
from jax.experimental import pallas as pl
from jax.experimental.pallas import tpu as pltpu
from jax.sharding import PartitionSpec as P

MEMBERS = 128
PATCH = 16
RADIUS = 15
NS_ITERS = 5
ROWS = 16
COLS = 128
PATCHES = COLS // PATCH
CELLS = PATCH * PATCH
EXTRA = 16
CHANNELS = MEMBERS + EXTRA
PACKED = (PATCHES // 2) * MEMBERS + 16
NT = (((1,), (1,)), ((), ()))
PARTS = 4
VMEM_LIMIT = 48 * 1024 * 1024
F32 = jnp.float32
BF16 = jnp.bfloat16


def tapers():
    lane = lax.broadcasted_iota(jnp.int32, (1, 3 * CELLS), 1)
    side = lane >> 8
    row, column = (lane >> 4) & (PATCH - 1), lane & (PATCH - 1)
    span = 2.0 * (RADIUS + PATCH / 2.0)
    half = (PATCH - 1) / 2.0

    def line(place, shift):
        offset = jnp.abs(place.astype(F32) + (PATCH * shift - half))
        return jnp.where(offset < RADIUS + PATCH / 2.0, 1.0 - offset / span, 0.0)

    lon = jnp.where(side == 0, line(column, -1), jnp.where(side == 1, line(column, 0), line(column, 1)))
    return [line(row, shift) * lon for shift in (1, 0, -1)]


def stencil_rows(first):
    cell = first + lax.broadcasted_iota(jnp.int32, (COLS, CELLS), 0)
    lane = lax.broadcasted_iota(jnp.int32, (COLS, CELLS), 1)
    row, column = lane >> 4, lane & (PATCH - 1)
    if first < 3 * CELLS:
        side = first // CELLS - 1
        place = ((cell & (CELLS - 1)) >> 4) - row
        near = jnp.abs(place) <= 1
    else:
        side = (first - 3 * CELLS) // COLS - 1
        slot = (cell & (COLS - 1)) >> 4
        near = ((slot == 0) & (row == 0)) | ((slot == 1) & (row == ROWS - 1))
    beside = jnp.abs(side * PATCH + (cell & (PATCH - 1)) - column) <= 1
    return jnp.where(near & beside, 1.0, 0.0).astype(BF16)


def swap_groups(arrays):
    lane = lax.broadcasted_iota(jnp.int32, arrays[0].shape, 1)
    for step in (1, 2, 4):
        width = PATCH * step
        high = (lane & width) != 0
        mixed = list(arrays)
        for i in range(8):
            if i & step == 0:
                first, second = arrays[i], arrays[i + step]
                mixed[i] = jnp.where(high, pltpu.roll(second, width, 1), first)
                mixed[i + step] = jnp.where(high, second, pltpu.roll(first, COLS - width, 1))
        arrays = mixed
    return arrays


def fetch(source, target, sem):
    copy = pltpu.make_async_copy(source, target, sem)
    copy.start()
    return copy


def fetch_field(background_ref, variable, held, sems):
    part = MEMBERS // PARTS
    return [
        fetch(
            background_ref.at[variable, pl.ds(k * part, part)], held.at[pl.ds(k * part, part)], sems.at[k]
        )
        for k in range(PARTS)
    ]


def widen_lines(copies, held, lines):
    part = MEMBERS // PARTS
    for k in range(PARTS):
        if copies:
            copies[k].wait()
        for m in range(k * part // 16, (k + 1) * part // 16):
            piece = held[pl.ds(m * 16, 16)].astype(F32)
            lines[pl.ds(m * 256, 256), :] = piece.reshape(256, COLS)


def to_blocks(lines, out_ref):
    for m in range(MEMBERS // 16):
        halves = []
        for g in range(2):
            rows = [lines[pl.ds(m * 256 + g * 8 + r, 16, stride=16), :] for r in range(8)]
            halves.append(swap_groups(rows))
        for b in range(PATCHES):
            both = jnp.concatenate([halves[0][b], halves[1][b]], axis=1)
            out_ref[pl.ds(m * 16, 16), pl.ds(b * CELLS, CELLS)] = both.astype(BF16)


def strip_kernel(background_ref, pack_ref, land_ref, held, sides_ref, tails_ref, mask_ref, lines, sems):
    copies = fetch_field(background_ref, 0, held, sems)
    land = land_ref[...].astype(F32)
    halves = []
    for g in range(2):
        rows = [jnp.broadcast_to(land[g * 8 + r : g * 8 + r + 1], (8, COLS)) for r in range(8)]
        halves.append(swap_groups(rows))
    which = lax.broadcasted_iota(jnp.int32, (8, CELLS), 0)
    mask = jnp.zeros((8, CELLS), F32)
    for b in range(PATCHES):
        mask = jnp.where(which == b, jnp.concatenate([halves[0][b], halves[1][b]], axis=1), mask)
    mask_ref[...] = mask
    pack = pack_ref[...]
    slots = pack.shape[1]
    cell, value, err, count = (pack[k : k + 1] for k in range(4))
    cell = cell.astype(jnp.int32)
    used = lax.broadcasted_iota(jnp.int32, (1, slots), 1) < count.astype(jnp.int32)
    inverse = jnp.where(used, 1.0 / (err * err), 0.0)
    value = jnp.where(used, value, 0.0)
    column = cell & (COLS - 1)
    block = column >> 4
    place = ((cell >> 7) << 4) + (column & (PATCH - 1))
    slot_block = lax.broadcasted_iota(jnp.int32, (16, value.shape[1]), 0)
    chosen = (slot_block & 7) == block
    amount = jnp.where(slot_block < 8, inverse, value)
    left = jnp.where(chosen, amount, 0.0).astype(BF16)
    spot = lax.broadcasted_iota(jnp.int32, (CELLS, value.shape[1]), 0) == place
    right = jnp.where(spot, 1.0, 0.0).astype(BF16)
    grids = lax.dot_general(left, right, NT, preferred_element_type=F32)
    precision = grids[:8] * mask
    observed = grids[8:]
    channel = lax.broadcasted_iota(jnp.int32, (EXTRA, CELLS), 0)
    for b in range(PATCHES):
        tail = jnp.where(
            channel == 0, precision[b : b + 1], jnp.where(channel == 1, observed[b : b + 1], 0.0)
        ).astype(BF16)
        tails_ref[:, pl.ds(b * CELLS, CELLS)] = tail
        if b == 0:
            sides_ref[pl.ds(MEMBERS, EXTRA), pl.ds(0, CELLS)] = tail
        if b == PATCHES - 1:
            sides_ref[pl.ds(MEMBERS, EXTRA), pl.ds(CELLS, CELLS)] = tail

    widen_lines(copies, held, lines)
    group = lax.broadcasted_iota(jnp.int32, (16, COLS), 1) >> 4
    for m in range(MEMBERS // 16):
        for g in range(2):
            west = jnp.zeros((16, COLS), F32)
            east = west
            for r in range(8):
                row = lines[pl.ds(m * 256 + g * 8 + r, 16, stride=16), :]
                here = group == r
                west = jnp.where(here, pltpu.roll(row, PATCH * r, 1) if r else row, west)
                east = jnp.where(here, pltpu.roll(row, PATCH * (r + 1), 1) if r < 7 else row, east)
            sides_ref[pl.ds(m * 16, 16), pl.ds(g * COLS, COLS)] = west.astype(BF16)
            sides_ref[pl.ds(m * 16, 16), pl.ds(CELLS + g * COLS, COLS)] = east.astype(BF16)


def block_kernel(held, tails_ref, blocks_ref, table_ref, lines):
    for first in range(0, 3 * (CELLS + COLS), COLS):
        table_ref[pl.ds(first, COLS), :] = stencil_rows(first)
    widen_lines((), held, lines)
    to_blocks(lines, blocks_ref)
    blocks_ref[pl.ds(MEMBERS, EXTRA), :] = tails_ref[...]


def rim_kernel(first_ref, second_ref, sides_ref, rim_ref, even_ref, odd_ref):
    lat_odd = (lax.axis_index("lat") & 1) == 1
    lon_odd = (lax.axis_index("lon") & 1) == 1
    first = first_ref[...].astype(F32)
    second = second_ref[...].astype(F32)
    above = jnp.where(lat_odd, first, second)
    below = jnp.where(lat_odd, second, first)
    lane = lax.broadcasted_iota(jnp.int32, (MEMBERS, COLS), 1)
    for b in range(PATCHES):
        top = pltpu.roll(above, (COLS - PATCH * b) % COLS, 1)
        low = pltpu.roll(below, (COLS - PATCH * b + PATCH) % COLS, 1)
        edge = jnp.where(lane < PATCH, top, jnp.where(lane < 2 * PATCH, low, 0.0)).astype(BF16)
        rim_ref[:, pl.ds(b * COLS, COLS)] = edge
        if b == 0:
            west_rim = edge
        if b == PATCHES - 1:
            east_rim = edge
    west = sides_ref[:, pl.ds(0, CELLS)]
    east = sides_ref[:, pl.ds(CELLS, CELLS)]
    even_ref[:, pl.ds(0, CELLS)] = jnp.where(lon_odd, west, east)
    odd_ref[:, pl.ds(0, CELLS)] = jnp.where(lon_odd, east, west)
    even_ref[pl.ds(0, MEMBERS), pl.ds(CELLS, COLS)] = jnp.where(lon_odd, west_rim, east_rim)
    odd_ref[pl.ds(0, MEMBERS), pl.ds(CELLS, COLS)] = jnp.where(lon_odd, east_rim, west_rim)
    blank = jnp.zeros((EXTRA, COLS), BF16)
    even_ref[pl.ds(MEMBERS, EXTRA), pl.ds(CELLS, COLS)] = blank
    odd_ref[pl.ds(MEMBERS, EXTRA), pl.ds(CELLS, COLS)] = blank


def gram_kernel(
    blocks_ref, rim_ref, first_ref, second_ref, table_ref,
    even_ref, odd_ref, pert, wide, wide_rim,
):
    lat = lax.axis_index("lat")
    lat_odd = (lat & 1) == 1
    lon_odd = (lax.axis_index("lon") & 1) == 1
    span = PATCHES * CELLS
    wide[:, pl.ds(0, CELLS)] = jnp.zeros((CHANNELS, CELLS), BF16)
    wide[:, pl.ds(span + 3 * CELLS, CELLS)] = jnp.zeros((CHANNELS, CELLS), BF16)
    wide[:, pl.ds(2 * CELLS, span)] = blocks_ref[...]
    one = first_ref[:, pl.ds(0, CELLS)]
    two = second_ref[:, pl.ds(0, CELLS)]
    wide[:, pl.ds(CELLS, CELLS)] = jnp.where(lon_odd, one, two)
    wide[:, pl.ds(span + 2 * CELLS, CELLS)] = jnp.where(lon_odd, two, one)
    rim_span = PATCHES * COLS
    blank = jnp.zeros((MEMBERS, COLS), BF16)
    wide_rim[:, pl.ds(0, COLS)] = blank
    wide_rim[:, pl.ds(rim_span + 3 * COLS, COLS)] = blank
    wide_rim[:, pl.ds(2 * COLS, rim_span)] = rim_ref[...]
    one = first_ref[pl.ds(0, MEMBERS), pl.ds(CELLS, COLS)]
    two = second_ref[pl.ds(0, MEMBERS), pl.ds(CELLS, COLS)]
    wide_rim[:, pl.ds(COLS, COLS)] = jnp.where(lon_odd, one, two)
    wide_rim[:, pl.ds(rim_span + 2 * COLS, COLS)] = jnp.where(lon_odd, two, one)

    lane = lax.broadcasted_iota(jnp.int32, (1, CELLS), 1)
    row = lane >> 4
    last = lax.axis_size("lat") - 1
    short = ((row == 0) & (lat == 0)) | ((row == ROWS - 1) & (lat == last))
    share = jnp.where(short, 1.0 / 6.0, 1.0 / 9.0)
    tail_row = lax.broadcasted_iota(jnp.int32, (EXTRA, CELLS), 0)
    for e in range(PATCHES + 2):
        summed = jnp.dot(
            wide[pl.ds(0, MEMBERS), pl.ds(e * CELLS, 3 * CELLS)], table_ref[pl.ds(0, 3 * CELLS), :], preferred_element_type=F32
        )
        summed = summed + jnp.dot(
            wide_rim[:, pl.ds(e * COLS, 3 * COLS)], table_ref[pl.ds(3 * CELLS, 3 * COLS), :], preferred_element_type=F32
        )
        mean = summed * share
        average = jnp.sum(mean, axis=0, keepdims=True) * (1.0 / MEMBERS)
        pert[pl.ds(0, MEMBERS), pl.ds(e * CELLS, CELLS)] = (mean - average).astype(BF16)
        tail = wide[pl.ds(MEMBERS, EXTRA), pl.ds((e + 1) * CELLS, CELLS)].astype(F32)
        innovation = tail[1:2] - average
        pert[pl.ds(MEMBERS, EXTRA), pl.ds(e * CELLS, CELLS)] = jnp.where(
            tail_row == 0, innovation, jnp.where(tail_row == 1, tail[0:1], 0.0)
        ).astype(BF16)

    r = lax.broadcasted_iota(jnp.int32, (MEMBERS, MEMBERS), 0)
    c = lax.broadcasted_iota(jnp.int32, (MEMBERS, MEMBERS), 1)
    lower = r >= c
    same = r == c
    base = (PATCHES // 2) * MEMBERS
    above, _, below = tapers()
    for out_ref, near, far in ((even_ref, above, below), (odd_ref, below, above)):
        taper = jnp.where(lat_odd, near, far)
        forcings, diagonals = [], []
        for pair in range(PATCHES // 2):
            first, forcing = patch_gram(pert, 2 * pair, taper, same)
            forcings.append(forcing)
            second, forcing = patch_gram(pert, 2 * pair + 1, taper, same)
            forcings.append(forcing)
            diagonals.append(jnp.sum(jnp.where(same, second, 0.0), axis=0, keepdims=True))
            out_ref[pl.ds(pair * MEMBERS, MEMBERS), :] = jnp.where(lower, first, second).astype(BF16)
        tail = forcings + diagonals + [jnp.zeros((4, MEMBERS), F32)]
        out_ref[pl.ds(base, 16), :] = jnp.concatenate(tail, axis=0).astype(BF16)


def patch_gram(pert, p, taper, same):
    window = pert[:, pl.ds(p * CELLS, 3 * CELLS)]
    precision = window[MEMBERS:].astype(F32)[1:2]
    scaled = (window[:MEMBERS].astype(F32) * (precision * taper)).astype(BF16)
    full = lax.dot_general(scaled, window, NT, preferred_element_type=F32)
    forcing = jnp.sum(jnp.where(same, full[:, MEMBERS : MEMBERS + 1], 0.0), axis=0, keepdims=True)
    return full[:, :MEMBERS], forcing


def centre_kernel(pert, blocks_ref, background_ref, mask_ref,
                  gram_ref, force_ref, departure_ref, base_ref, soil, held, lines, sems):
    copies = fetch_field(background_ref, 1, held, sems)
    r = lax.broadcasted_iota(jnp.int32, (MEMBERS, MEMBERS), 0)
    c = lax.broadcasted_iota(jnp.int32, (MEMBERS, MEMBERS), 1)
    same = r == c
    taper = tapers()[1]
    forcings = []
    for p in range(PATCHES):
        gram, forcing = patch_gram(pert, p, taper, same)
        gram_ref[p] = gram + jnp.where(same, MEMBERS - 1.0, 0.0)
        forcings.append(forcing)
    force_ref[...] = jnp.concatenate(forcings, axis=0)
    widen_lines(copies, held, lines)
    to_blocks(lines, soil)
    for p in range(PATCHES):
        cells = pl.ds(p * CELLS, CELLS)
        land = mask_ref[p : p + 1, :] != 0.0
        for v, raw in enumerate((blocks_ref[pl.ds(0, MEMBERS), cells], soil[:, cells])):
            raw = raw.astype(F32)
            mean = jnp.sum(raw, axis=0, keepdims=True) * (1.0 / MEMBERS)
            place = pl.ds((2 * p + v) * CELLS, CELLS)
            departure_ref[:, place] = jnp.where(land, raw - mean, 0.0).astype(BF16)
            base_ref[:, place] = jnp.where(land, mean, raw)


def split(a):
    high = a.astype(BF16)
    return high, (a - high.astype(F32)).astype(BF16)


def product(a, b):
    a_high, a_low = split(a)
    b_high, b_low = split(b)
    wide = jnp.concatenate([b_high, b_low], axis=1)
    out = jnp.dot(
        jnp.concatenate([a_high, a_low], axis=1),
        jnp.concatenate([wide, wide], axis=0),
        preferred_element_type=F32,
    )
    return out[:, :MEMBERS] + out[:, MEMBERS:]


def halves(a):
    return jnp.concatenate(split(a), axis=1)


def product(a, b):
    out = jnp.dot(a, jnp.concatenate([b, b], axis=0), preferred_element_type=F32)
    return out[:, :MEMBERS] + out[:, MEMBERS:]


def solve_kernel(first_ref, second_ref, gram_ref, force_ref, departure_ref, base_ref, out_ref,
                 pair_ref, scratch, spread, held, sems):
    r = lax.broadcasted_iota(jnp.int32, (MEMBERS, MEMBERS), 0)
    c = lax.broadcasted_iota(jnp.int32, (MEMBERS, MEMBERS), 1)
    eye = jnp.where(r == c, 1.0, 0.0)
    base = (PATCHES // 2) * MEMBERS
    tail = first_ref[pl.ds(base, 16), :].astype(F32) + second_ref[pl.ds(base, 16), :].astype(F32)
    norms = []
    for pair in range(PATCHES // 2):
        rows = pl.ds(pair * MEMBERS, MEMBERS)
        mixed = first_ref[rows, :].astype(F32) + second_ref[rows, :].astype(F32)
        turned = mixed.T
        diagonal = tail[8 + pair : 9 + pair]
        gains = (
            jnp.where(r >= c, mixed, turned),
            jnp.where(r > c, turned, jnp.where(r < c, mixed, diagonal)),
        )
        for k in range(2):
            p = 2 * pair + k
            system = gram_ref[p] + gains[k]
            total = jnp.sum(jnp.sum(system * system, axis=0, keepdims=True), axis=1, keepdims=True)
            norm = jnp.sqrt(total)
            norms.append(norm)
            scaled = system * (1.0 / norm)
            split_scaled = halves(scaled)
            pair_ref[p, :MEMBERS] = halves(1.5 * scaled - 0.5 * product(split_scaled, split_scaled))
            pair_ref[p, MEMBERS:] = halves(1.5 * eye - 0.5 * scaled)

    def sweep(_, carry):
        middles = [
            halves(1.5 * eye - 0.5 * product(pair_ref[p, MEMBERS:], pair_ref[p, :MEMBERS]))
            for p in range(PATCHES)
        ]
        for p in range(PATCHES):
            pair_ref[p] = halves(product(pair_ref[p], middles[p]))
        return carry

    lax.fori_loop(0, NS_ITERS - 2, sweep, 0)
    middles = [
        halves(1.5 * eye - 0.5 * product(pair_ref[p, MEMBERS:], pair_ref[p, :MEMBERS]))
        for p in range(PATCHES)
    ]
    for p in range(PATCHES):
        lower = product(pair_ref[p, MEMBERS:], middles[p])
        split_lower = halves(lower)
        forcing = jnp.broadcast_to(force_ref[p : p + 1] + tail[p : p + 1], (16, MEMBERS))
        once = product(halves(forcing), split_lower)
        mean_weight = product(halves(once), split_lower)[0:1] * (1.0 / norms[p])
        scale = jnp.sqrt(MEMBERS - 1.0) / jnp.sqrt(norms[p])
        transform = (lower * scale + mean_weight).astype(BF16)
        cells = pl.ds(p * 2 * CELLS, 2 * CELLS)
        spread[:, cells] = base_ref[:, cells] + jnp.dot(
            transform, departure_ref[:, cells], preferred_element_type=F32
        )

    copies = []
    for v in range(2):
        for m in range(MEMBERS // 16):
            rows = pl.ds(m * 16, 16)
            for g in range(2):
                groups = [
                    spread[rows, pl.ds(b * 2 * CELLS + v * CELLS + g * COLS, COLS)] for b in range(PATCHES)
                ]
                lines = swap_groups(groups)
                for k in range(8):
                    scratch[pl.ds(m * 256 + g * 8 + k, 16, stride=16), :] = lines[k]
            held[v, rows] = scratch[pl.ds(m * 256, 256), :].reshape(16, ROWS, COLS).astype(BF16)
            copies.append(fetch(held.at[v, rows], out_ref.at[v, rows], sems.at[v * (MEMBERS // 16) + m]))
    for copy in copies:
        copy.wait()


LIMITS = {strip_kernel: 53 * 1024 * 1024}


def call(kernel, out_shape, scratch, flops, moved, *operands, far=(), scalars=(), out_far=False):
    vmem = pl.BlockSpec(memory_space=pltpu.VMEM)
    smem = pl.BlockSpec(memory_space=pltpu.SMEM)
    anywhere = pl.BlockSpec(memory_space=pltpu.HBM)
    return pl.pallas_call(
        kernel,
        out_shape=out_shape,
        in_specs=[
            anywhere if i in far else smem if i in scalars else vmem for i in range(len(operands))
        ],
        out_specs=[anywhere if out_far else vmem] * len(out_shape),
        scratch_shapes=scratch,
        compiler_params=pltpu.CompilerParams(vmem_limit_bytes=LIMITS.get(kernel, VMEM_LIMIT)),
        cost_estimate=pl.CostEstimate(flops=flops, bytes_accessed=moved, transcendentals=0),
    )(*operands)


def pairs_inside(size):
    return [(i, i ^ 1) for i in range(size)]


def pairs_across(size, wrap):
    pairs = []
    for i in range(1, size - 1, 2):
        pairs += [(i, i + 1), (i + 1, i)]
    if wrap:
        pairs += [(size - 1, 0), (0, size - 1)]
    return pairs


def exchange(even, odd, axis, wrap):
    size = lax.axis_size(axis)
    return (
        lax.ppermute(even, axis, pairs_inside(size)),
        lax.ppermute(odd, axis, pairs_across(size, wrap)),
    )


def body(background, obs_cell, obs_count, obs_value, obs_err, land):
    slots = obs_cell.shape[-1]
    span = PATCHES * CELLS
    shape = jax.ShapeDtypeStruct
    field = pltpu.VMEM((MEMBERS, ROWS, COLS), BF16)
    lines_shape = (MEMBERS * ROWS, COLS)
    copies = pltpu.SemaphoreType.DMA
    lat_odd = (lax.axis_index("lat") & 1) == 1
    line = lax.broadcasted_iota(jnp.int32, (8, slots), 0)
    pack = jnp.zeros((8, slots), F32)
    for k, array in enumerate((obs_cell, obs_value, obs_err, obs_count)):
        pack = jnp.where(line == k, array.reshape(1, -1).astype(F32), pack)
    top, bottom = background[0, :, 0], background[0, :, ROWS - 1]
    rows = exchange(
        jnp.where(lat_odd, top, bottom), jnp.where(lat_odd, bottom, top), "lat", False
    )
    held, sides, tails, mask = call(
        strip_kernel,
        [
            shape((MEMBERS, ROWS, COLS), BF16),
            shape((CHANNELS, 2 * CELLS), BF16),
            shape((EXTRA, span), BF16),
            shape((8, CELLS), F32),
        ],
        [pltpu.VMEM(lines_shape, F32), copies((PARTS,))],
        10**7, 2 * 10**6,
        background, pack, land,
        far=(0,),
    )
    rim, even, odd = call(
        rim_kernel,
        [shape((MEMBERS, PATCHES * COLS), BF16)] + [shape((CHANNELS, CELLS + COLS), BF16)] * 2,
        [], 10**6, 10**6, *rows, sides,
    )
    neighbours = exchange(even, odd, "lon", True)
    blocks, table = call(
        block_kernel,
        [shape((CHANNELS, span), BF16), shape((3 * (CELLS + COLS), CELLS), BF16)],
        [pltpu.VMEM(lines_shape, F32)],
        10**8, 4 * 10**6,
        held, tails,
    )
    even, odd, pert = call(
        gram_kernel,
        [shape((PACKED, MEMBERS), BF16)] * 2 + [shape((CHANNELS, span + 2 * CELLS), BF16)],
        [
            pltpu.VMEM((CHANNELS, span + 4 * CELLS), BF16),
            pltpu.VMEM((MEMBERS, (PATCHES + 4) * COLS), BF16),
        ],
        10**9, 3 * 10**6,
        blocks, rim, *neighbours, table,
    )
    packed = exchange(even, odd, "lat", False)
    gram, force, departure, base = call(
        centre_kernel,
        [
            shape((PATCHES, MEMBERS, MEMBERS), F32),
            shape((PATCHES, MEMBERS), F32),
            shape((MEMBERS, 2 * span), BF16),
            shape((MEMBERS, 2 * span), F32),
        ],
        [pltpu.VMEM((MEMBERS, span), BF16), field, pltpu.VMEM(lines_shape, F32), copies((PARTS,))],
        10**9, 5 * 10**6,
        pert, blocks, background, mask,
        far=(2,),
    )
    (analysis,) = call(
        solve_kernel,
        [shape(background.shape, BF16)],
        [
            pltpu.VMEM((PATCHES, 2 * MEMBERS, 2 * MEMBERS), BF16),
            pltpu.VMEM(lines_shape, F32),
            pltpu.VMEM((MEMBERS, 2 * span), F32),
            pltpu.VMEM(background.shape, BF16),
            copies((2 * MEMBERS // 16,)),
        ],
        2 * 10**9, 5 * 10**6,
        *packed, gram, force, departure, base,
        out_far=True,
    )
    return analysis


def solution(mesh):
    return jax.shard_map(
        body,
        mesh=mesh,
        in_specs=(
            P(None, None, "lat", "lon"),
            P("lat", "lon", None),
            P("lat", "lon"),
            P("lat", "lon", None),
            P("lat", "lon", None),
            P("lat", "lon"),
        ),
        out_specs=P(None, None, "lat", "lon"),
        check_vma=False,
    )
```

time: 44.2 us -> 42.4 us (0.959)
  waiting for transfers between devices: 10.6 us -> 4.19 us
  Pallas kernels: 16.3 us -> 18.8 us
  other arithmetic: 0.02 us -> 2.18 us
  local copies, waits for them, and re-layouts: 2.41 us -> 1.83 us
    ppermute x3, waiting for transfers between devices: 10.2 us -> 4.18 us  [exchange(): lax.ppermute(odd, axis, pairs_across(size, wrap))]
    pallas_call x4 -> x6, Pallas kernels: 16.3 us -> 18.8 us  [call(): pl.pallas_call(kernel, out_shape=out_shape, in_specs=[anywhere if i in fa...]
    convert_element_type x0 -> x2, other arithmetic: none -> 1.38 us  [body(): pack = jnp.where(line == k, array.reshape(1, -1).astype(F32), pack)]
    select_n x0 -> x1, other arithmetic: none -> 0.76 us  [body(): pack = jnp.where(line == k, array.reshape(1, -1).astype(F32), pack)]
    unnamed x18 -> x4, local copies, waits for them, and re-layouts: 1.27 us -> 0.7 us
  transfers between devices with their start and end apart: 6 -> 6, of which waited for: 3 -> 2; matrix products, arithmetic and copies ran while one was open for 0% -> 5% of each run, Pallas kernels for 5% -> 18%
where the time goes in v1:
time: 42.4 us; the launch traced here: 42 us
  Pallas kernels  18.8 us (44%)
  starting transfers between devices  14.1 us (33%)
  waiting for transfers between devices  4.19 us (10%)
  other arithmetic  2.18 us (5%)
  local copies, waits for them, and re-layouts  1.83 us (4%)
  between operations  0.95 us (2%)
    pallas_call x6, Pallas kernels, call(): pl.pallas_call(kernel, out_shape=out_shape, in_specs=[anywhere if i in fa...  18.8 us
    ppermute x3, starting transfers between devices, exchange(): lax.ppermute(odd, axis, pairs_across(size, wrap))  11.8 us
    ppermute x3, waiting for transfers between devices, exchange(): lax.ppermute(odd, axis, pairs_across(size, wrap))  4.18 us
    ppermute x3, starting transfers between devices, exchange(): lax.ppermute(even, axis, pairs_inside(size))  2.27 us
    convert_element_type x2, other arithmetic, body(): pack = jnp.where(line == k, array.reshape(1, -1).astype(F32), pack)  1.38 us
    slice x1, local copies, waits for them, and re-layouts, body(): top, bottom = (background[0, :, 0], background[0, :, ROWS - 1])  1.13 us
  transfers between devices with their start and end apart: 6, of which 2 were waited for; matrix products, arithmetic and copies ran while one was open for 5% of the time, Pallas kernels for 18%

profile of v1, /device:TPU:102, one launch (start us, length us, event | category | flops | bytes accessed | tf_op | source)
XLA Modules:
  0.0 42.0 jit_solution(12733547427398953253)
XLA Ops:
  0.0 1.1 %fusion = (bf16[1,128,1,128]{3,2,1,0:T(2,128)(2,1)S(1)}, bf16[1,128,1,128]{3,2,1,0:T(2,128)(2,1)S(1)}) fusion(bf16[2,128,16,128]{3,2,1,0:T(8,128)(2,1)} %background_ref.3), kind=kLoop, calls=%fused_computation.7 | loop fusion | bytes 131072 | tf_op jit(solution)/shard_map/slice | solution.py:456
  1.2 5.3 %collective-permute-start.1 = (bf16[128,128]{1,0:T(8,128)(2,1)S(1)}, bf16[128,128]{1,0:T(8,128)(2,1)S(1)}, u32[]{:S(2)}, u32[]{:S(2)}) collective-permute-start(bf16[128,128]{1,0:T(8,128)(2,1)S(1)} %get-tuple-element.39), channel_id=1, source_target_pairs={{1,2},{2,1},{3,4},{4,3},{5,6},{6,5},{7,8},{8,7},{9,10},{10,9},{11,... | collective-permute-start | bytes 98312 | tf_op jit(solution)/shard_map/ppermute | solution.py:440
  6.5 0.1 collective-permute-start
  7.2 0.7 %convert_element_type.28 = f32[1,1,1024]{2,1,0:T(1,128)S(1)} convert(s32[1,1,1024]{2,1,0:T(1,128)} %param.7) | non-fusion elementwise | flops 1024 | bytes 8192 | tf_op jit(solution)/shard_map/convert_element_type | solution.py:455
  7.9 0.7 %convert_element_type.30 = f32[1,1,1024]{2,1,0:T(1,128)S(1)} convert(bf16[1,1,1024]{2,1,0:T(2,128)(2,1)} %param.9) | non-fusion elementwise | flops 1024 | bytes 6144 | tf_op jit(solution)/shard_map/convert_element_type | solution.py:455
  8.6 0.8 %select_select_fusion.pack_ref = f32[8,1024]{1,0:T(8,128)S(1)} fusion(f32[1024]{0:T(1024)S(1)} %bitcast.8, f32[1024]{0:T(1024)S(1)} %bitcast.9, f32[1024]{0:T(1024)} %bitcast.10, f32[]{:T(128)} %bitcast, pred[8]{0:T(512)(128)(4,1)S(1)} %get-tuple-element.41, pred[8]{0:T(512)(128)(4,1)S(1)} %get-tuple-element.42, pred[8]{0:T(512)(128)(4,1)S(1)} %get-tuple-element.43, ...), kind=kLoop, calls=%fused_computation.2 | loop fusion | flops 32768 | bytes 45092 | tf_op jit(solution)/shard_map/jit(_where)/select_n | solution.py:455
  9.4 0.0 copy-start.1
  9.4 0.7 %copy-done.1 = s32[16,128]{1,0:T(8,128)S(1)} copy-done((s32[16,128]{1,0:T(8,128)S(1)}, s32[16,128]{1,0:T(8,128)}, u32[]{:S(2)}) %copy-start.1) | copy-done | bytes 8216
  10.1 1.5 %shard_map.64 = (bf16[128,16,128]{2,1,0:T(8,128)(2,1)S(1)}, bf16[144,512]{1,0:T(8,128)(2,1)S(1)}, bf16[16,2048]{1,0:T(8,128)(2,1)S(1)}, f32[8,256]{1,0:T(8,128)S(1)}) custom-call(bf16[2,128,16,128]{3,2,1,0:T(8,128)(2,1)} %background_ref.3, f32[8,1024]{1,0:T(8,128)S(1)} %select_select_fusion.pack_ref, s32[16,128]{1,0:T(8,128)S(1)} %copy-done.1), custom_call_target="tpu_custom_call" | custom-call | flops 10000000 | bytes 2000000 | tf_op jit(solution)/shard_map/pallas_call | solution.py:410
  11.6 0.0 collective-permute-done.1.second_ref
  11.6 0.0 collective-permute-done.first_ref
  11.6 0.2 shard_map.66
  11.8 0.1 collective-permute-start.2
  11.9 3.7 %collective-permute-start.3 = (bf16[144,384]{1,0:T(8,128)(2,1)S(1)}, bf16[144,384]{1,0:T(8,128)(2,1)S(1)}, u32[]{:S(2)}, u32[]{:S(2)}) collective-permute-start(bf16[144,384]{1,0:T(8,128)(2,1)S(1)} %get-tuple-element.27), channel_id=1, source_target_pairs={{16,32},{32,16},{48,64},{64,48},{80,96},{96,80},{112,128},{128,112... | collective-permute-start | bytes 331784 | tf_op jit(solution)/shard_map/ppermute | solution.py:440
  15.6 0.0 copy-start
  15.6 2.4 %shard_map.65 = (bf16[144,2048]{1,0:T(8,128)(2,1)S(1)}, bf16[1152,256]{1,0:T(8,128)(2,1)S(1)}) custom-call(bf16[128,16,128]{2,1,0:T(8,128)(2,1)S(1)} %get-tuple-element.21.held, bf16[16,2048]{1,0:T(8,128)(2,1)S(1)} %get-tuple-element.22.tails_ref), custom_call_target="tpu_custom_call" | custom-call | flops 100000000 | bytes 4000000 | tf_op jit(solution)/shard_map/pallas_call | solution.py:410
  18.0 0.0 collective-permute-done.2.first_ref
  18.0 1.8 %collective-permute-done.3.second_ref = bf16[144,384]{1,0:T(8,128)(2,1)S(1)} collective-permute-done((bf16[144,384]{1,0:T(8,128)(2,1)S(1)}, bf16[144,384]{1,0:T(8,128)(2,1)S(1)}, u32[]{:S(2)}, u32[]{:S(2)}) %collective-permute-start.3) | collective-permute-done | bytes 110624 | tf_op jit(solution)/shard_map/ppermute | solution.py:440
  19.8 2.3 %shard_map.67 = (bf16[528,128]{1,0:T(8,128)(2,1)S(1)}, bf16[528,128]{1,0:T(8,128)(2,1)S(1)}, bf16[144,2560]{1,0:T(8,128)(2,1)S(1)}) custom-call(bf16[144,2048]{1,0:T(8,128)(2,1)S(1)} %get-tuple-element.23.blocks_ref, bf16[128,1024]{1,0:T(8,128)(2,1)S(1)} %get-tuple-element.25.rim_ref, bf16[144,384]{1,0:T(8,128)(2,1)S(1)} %collective-permute-done.2.first_ref, ...), custom_call_target="tpu_custom_call" | custom-call | flops 1000000000 | bytes 3000000 | tf_op jit(solution)/shard_map/pallas_call | solution.py:410
  22.1 2.1 %collective-permute-start.4 = (bf16[528,128]{1,0:T(8,128)(2,1)S(1)}, bf16[528,128]{1,0:T(8,128)(2,1)S(1)}, u32[]{:S(2)}, u32[]{:S(2)}) collective-permute-start(bf16[528,128]{1,0:T(8,128)(2,1)S(1)} %get-tuple-element.29), channel_id=1, source_target_pairs={{0,1},{1,0},{2,3},{3,2},{4,5},{5,4},{6,7},{7,6},{8,9},{9,8},{10,11... | collective-permute-start | bytes 405512 | tf_op jit(solution)/shard_map/ppermute | solution.py:439
  24.2 2.8 %collective-permute-start.5 = (bf16[528,128]{1,0:T(8,128)(2,1)S(1)}, bf16[528,128]{1,0:T(8,128)(2,1)S(1)}, u32[]{:S(2)}, u32[]{:S(2)}) collective-permute-start(bf16[528,128]{1,0:T(8,128)(2,1)S(1)} %get-tuple-element.30), channel_id=1, source_target_pairs={{1,2},{2,1},{3,4},{4,3},{5,6},{6,5},{7,8},{8,7},{9,10},{10,9},{11,... | collective-permute-start | bytes 405512 | tf_op jit(solution)/shard_map/ppermute | solution.py:440
  27.0 0.0 copy-done
  27.0 3.8 %shard_map.68 = (f32[8,128,128]{2,1,0:T(8,128)S(1)}, f32[8,128]{1,0:T(8,128)S(1)}, bf16[128,4096]{1,0:T(8,128)(2,1)S(1)}, f32[128,4096]{1,0:T(8,128)S(1)}) custom-call(bf16[144,2560]{1,0:T(8,128)(2,1)S(1)} %get-tuple-element.31.pert, bf16[144,2048]{1,0:T(8,128)(2,1)S(1)} %get-tuple-element.23.blocks_ref, bf16[2,128,16,128]{3,2,1,0:T(8,128)(2,1)S(1)} %copy-done, ...), custom_call_target="tpu_custom_call" | custom-call | flops 1000000000 | bytes 5000000 | tf_op jit(solution)/shard_map/pallas_call | solution.py:410
  30.8 0.0 collective-permute-done.4.first_ref
  30.8 2.4 %collective-permute-done.5.second_ref = bf16[528,128]{1,0:T(8,128)(2,1)S(1)} collective-permute-done((bf16[528,128]{1,0:T(8,128)(2,1)S(1)}, bf16[528,128]{1,0:T(8,128)(2,1)S(1)}, u32[]{:S(2)}, u32[]{:S(2)}) %collective-permute-start.5) | collective-permute-done | bytes 135200 | tf_op jit(solution)/shard_map/ppermute | solution.py:440
  33.2 8.7 %shard_map.69 = bf16[2,128,16,128]{3,2,1,0:T(8,128)(2,1)} custom-call(bf16[528,128]{1,0:T(8,128)(2,1)S(1)} %collective-permute-done.4.first_ref, bf16[528,128]{1,0:T(8,128)(2,1)S(1)} %collective-permute-done.5.second_ref, f32[8,128,128]{2,1,0:T(8,128)S(1)} %get-tuple-element.33.gram_ref, f32[8,128]{1,0:T(8,128)S(1)} %get-tuple-element.34.force_ref, ...), custom_call_target="tpu_custom_call" | custom-call | flops 2000000000 | bytes 5000000 | tf_op jit(solution)/shard_map/pallas_call | solution.py:410
  (3 shorter events, 0.0 us)
Async XLA Ops:
  1.2 10.4 %collective-permute-start.1 = (bf16[128,128]{1,0:T(8,128)(2,1)S(1)}, bf16[128,128]{1,0:T(8,128)(2,1)S(1)}, u32[]{:S(2)}, u32[]{:S(2)}) collective-permute-start(bf16[128,128]{1,0:T(8,128)(2,1)S(1)} %get-tuple-element.39), channel_id=1, source_target_pairs={{1,2},{2,1},{3,4},{4,3},{5,6},{6,5},{7,8},{8,7},{9,10},{10,9},{11,... | collective-permute-start | bytes 98312 | tf_op jit(solution)/shard_map/ppermute | solution.py:440
  6.5 5.1 %collective-permute-start = (bf16[128,128]{1,0:T(8,128)(2,1)S(1)}, bf16[128,128]{1,0:T(8,128)(2,1)S(1)}, u32[]{:S(2)}, u32[]{:S(2)}) collective-permute-start(bf16[128,128]{1,0:T(8,128)(2,1)S(1)} %get-tuple-element.40), channel_id=1, source_target_pairs={{0,1},{1,0},{2,3},{3,2},{4,5},{5,4},{6,7},{7,6},{8,9},{9,8},{10,11... | collective-permute-start | bytes 98312 | tf_op jit(solution)/shard_map/ppermute | solution.py:439
  9.4 0.7 %copy-start.1 = (s32[16,128]{1,0:T(8,128)S(1)}, s32[16,128]{1,0:T(8,128)}, u32[]{:S(2)}) copy-start(s32[16,128]{1,0:T(8,128)} %land_ref.1) | copy-start | bytes 24580
  11.8 6.2 %collective-permute-start.2 = (bf16[144,384]{1,0:T(8,128)(2,1)S(1)}, bf16[144,384]{1,0:T(8,128)(2,1)S(1)}, u32[]{:S(2)}, u32[]{:S(2)}) collective-permute-start(bf16[144,384]{1,0:T(8,128)(2,1)S(1)} %get-tuple-element.26), channel_id=1, source_target_pairs={{0,16},{16,0},{32,48},{48,32},{64,80},{80,64},{96,112},{112,96},{1... | collective-permute-start | bytes 331784 | tf_op jit(solution)/shard_map/ppermute | solution.py:439
  11.9 7.9 %collective-permute-start.3 = (bf16[144,384]{1,0:T(8,128)(2,1)S(1)}, bf16[144,384]{1,0:T(8,128)(2,1)S(1)}, u32[]{:S(2)}, u32[]{:S(2)}) collective-permute-start(bf16[144,384]{1,0:T(8,128)(2,1)S(1)} %get-tuple-element.27), channel_id=1, source_target_pairs={{16,32},{32,16},{48,64},{64,48},{80,96},{96,80},{112,128},{128,112... | collective-permute-start | bytes 331784 | tf_op jit(solution)/shard_map/ppermute | solution.py:440
  15.6 11.4 %copy-start = (bf16[2,128,16,128]{3,2,1,0:T(8,128)(2,1)S(1)}, bf16[2,128,16,128]{3,2,1,0:T(8,128)(2,1)}, u32[]{:S(2)}) copy-start(bf16[2,128,16,128]{3,2,1,0:T(8,128)(2,1)} %background_ref.3) | copy-start | bytes 3145732
  22.1 8.7 %collective-permute-start.4 = (bf16[528,128]{1,0:T(8,128)(2,1)S(1)}, bf16[528,128]{1,0:T(8,128)(2,1)S(1)}, u32[]{:S(2)}, u32[]{:S(2)}) collective-permute-start(bf16[528,128]{1,0:T(8,128)(2,1)S(1)} %get-tuple-element.29), channel_id=1, source_target_pairs={{0,1},{1,0},{2,3},{3,2},{4,5},{5,4},{6,7},{7,6},{8,9},{9,8},{10,11... | collective-permute-start | bytes 405512 | tf_op jit(solution)/shard_map/ppermute | solution.py:439
  24.2 9.0 %collective-permute-start.5 = (bf16[528,128]{1,0:T(8,128)(2,1)S(1)}, bf16[528,128]{1,0:T(8,128)(2,1)S(1)}, u32[]{:S(2)}, u32[]{:S(2)}) collective-permute-start(bf16[528,128]{1,0:T(8,128)(2,1)S(1)} %get-tuple-element.30), channel_id=1, source_target_pairs={{1,2},{2,1},{3,4},{4,3},{5,6},{6,5},{7,8},{8,7},{9,10},{10,9},{11,... | collective-permute-start | bytes 405512 | tf_op jit(solution)/shard_map/ppermute | solution.py:440

commit v2 on v1

--- a/solution.py
+++ b/solution.py
@@ -100,32 +100,31 @@
     for m in range(MEMBERS // 16):
         halves = []
         for g in range(2):
-            rows = [lines[pl.ds(m * 256 + g * 8 + r, 16, stride=16), :] for r in range(8)]
+            rows = [lines[pl.ds(m * 256 + g * 8 + r, 16, stride=16), :].astype(BF16) for r in range(8)]
             halves.append(swap_groups(rows))
         for b in range(PATCHES):
             both = jnp.concatenate([halves[0][b], halves[1][b]], axis=1)
-            out_ref[pl.ds(m * 16, 16), pl.ds(b * CELLS, CELLS)] = both.astype(BF16)
-
-
-def strip_kernel(background_ref, pack_ref, land_ref, held, sides_ref, tails_ref, mask_ref, lines, sems):
+            out_ref[pl.ds(m * 16, 16), pl.ds(b * CELLS, CELLS)] = both
+
+
+def strip_kernel(background_ref, pack_ref, held, sides_ref, tails_ref, mask_ref, lines, sems):
     copies = fetch_field(background_ref, 0, held, sems)
-    land = land_ref[...].astype(F32)
+    slots = (pack_ref.shape[1] - ROWS * COLS) // 3
     halves = []
     for g in range(2):
-        rows = [jnp.broadcast_to(land[g * 8 + r : g * 8 + r + 1], (8, COLS)) for r in range(8)]
+        rows = [
+            jnp.broadcast_to(pack_ref[:, pl.ds(3 * slots + (g * 8 + r) * COLS, COLS)], (8, COLS))
+            for r in range(8)
+        ]
         halves.append(swap_groups(rows))
     which = lax.broadcasted_iota(jnp.int32, (8, CELLS), 0)
     mask = jnp.zeros((8, CELLS), F32)
     for b in range(PATCHES):
         mask = jnp.where(which == b, jnp.concatenate([halves[0][b], halves[1][b]], axis=1), mask)
     mask_ref[...] = mask
-    pack = pack_ref[...]
-    slots = pack.shape[1]
-    cell, value, err, count = (pack[k : k + 1] for k in range(4))
-    cell = cell.astype(jnp.int32)
-    used = lax.broadcasted_iota(jnp.int32, (1, slots), 1) < count.astype(jnp.int32)
-    inverse = jnp.where(used, 1.0 / (err * err), 0.0)
-    value = jnp.where(used, value, 0.0)
+    cell = pack_ref[:, pl.ds(0, slots)].astype(jnp.int32)
+    inverse = pack_ref[:, pl.ds(slots, slots)]
+    value = pack_ref[:, pl.ds(2 * slots, slots)]
     column = cell & (COLS - 1)
     block = column >> 4
     place = ((cell >> 7) << 4) + (column & (PATCH - 1))
@@ -153,15 +152,15 @@
     group = lax.broadcasted_iota(jnp.int32, (16, COLS), 1) >> 4
     for m in range(MEMBERS // 16):
         for g in range(2):
-            west = jnp.zeros((16, COLS), F32)
+            west = jnp.zeros((16, COLS), BF16)
             east = west
             for r in range(8):
-                row = lines[pl.ds(m * 256 + g * 8 + r, 16, stride=16), :]
+                row = lines[pl.ds(m * 256 + g * 8 + r, 16, stride=16), :].astype(BF16)
                 here = group == r
                 west = jnp.where(here, pltpu.roll(row, PATCH * r, 1) if r else row, west)
                 east = jnp.where(here, pltpu.roll(row, PATCH * (r + 1), 1) if r < 7 else row, east)
-            sides_ref[pl.ds(m * 16, 16), pl.ds(g * COLS, COLS)] = west.astype(BF16)
-            sides_ref[pl.ds(m * 16, 16), pl.ds(CELLS + g * COLS, COLS)] = east.astype(BF16)
+            sides_ref[pl.ds(m * 16, 16), pl.ds(g * COLS, COLS)] = west
+            sides_ref[pl.ds(m * 16, 16), pl.ds(CELLS + g * COLS, COLS)] = east
 
 
 def block_kernel(held, tails_ref, blocks_ref, table_ref, lines):
@@ -277,7 +276,7 @@
 
 
 def centre_kernel(pert, blocks_ref, background_ref, mask_ref,
-                  gram_ref, force_ref, departure_ref, base_ref, soil, held, lines, sems):
+                  gram_ref, force_ref, departure_ref, base_ref, rest_ref, soil, held, lines, sems):
     copies = fetch_field(background_ref, 1, held, sems)
     r = lax.broadcasted_iota(jnp.int32, (MEMBERS, MEMBERS), 0)
     c = lax.broadcasted_iota(jnp.int32, (MEMBERS, MEMBERS), 1)
@@ -298,8 +297,10 @@
             raw = raw.astype(F32)
             mean = jnp.sum(raw, axis=0, keepdims=True) * (1.0 / MEMBERS)
             place = pl.ds((2 * p + v) * CELLS, CELLS)
+            coarse = mean.astype(BF16).astype(F32)
             departure_ref[:, place] = jnp.where(land, raw - mean, 0.0).astype(BF16)
-            base_ref[:, place] = jnp.where(land, mean, raw)
+            base_ref[:, place] = jnp.where(land, coarse, raw).astype(BF16)
+            rest_ref[:, place] = jnp.broadcast_to(jnp.where(land, mean - coarse, 0.0), (8, CELLS))
 
 
 def split(a):
@@ -328,11 +329,12 @@
     return out[:, :MEMBERS] + out[:, MEMBERS:]
 
 
-def solve_kernel(first_ref, second_ref, gram_ref, force_ref, departure_ref, base_ref, out_ref,
+def solve_kernel(first_ref, second_ref, gram_ref, force_ref, departure_ref, base_ref, rest_ref, out_ref,
                  pair_ref, scratch, spread, held, sems):
     r = lax.broadcasted_iota(jnp.int32, (MEMBERS, MEMBERS), 0)
     c = lax.broadcasted_iota(jnp.int32, (MEMBERS, MEMBERS), 1)
     eye = jnp.where(r == c, 1.0, 0.0)
+    unit = eye.astype(BF16)
     base = (PATCHES // 2) * MEMBERS
     tail = first_ref[pl.ds(base, 16), :].astype(F32) + second_ref[pl.ds(base, 16), :].astype(F32)
     norms = []
@@ -356,45 +358,49 @@
             pair_ref[p, :MEMBERS] = halves(1.5 * scaled - 0.5 * product(split_scaled, split_scaled))
             pair_ref[p, MEMBERS:] = halves(1.5 * eye - 0.5 * scaled)
 
-    def sweep(_, carry):
+    def sweep():
         middles = [
             halves(1.5 * eye - 0.5 * product(pair_ref[p, MEMBERS:], pair_ref[p, :MEMBERS]))
             for p in range(PATCHES)
         ]
         for p in range(PATCHES):
             pair_ref[p] = halves(product(pair_ref[p], middles[p]))
-        return carry
-
-    lax.fori_loop(0, NS_ITERS - 2, sweep, 0)
+
+    for _ in range(NS_ITERS - 2):
+        sweep()
     middles = [
         halves(1.5 * eye - 0.5 * product(pair_ref[p, MEMBERS:], pair_ref[p, :MEMBERS]))
         for p in range(PATCHES)
     ]
+    transforms = []
     for p in range(PATCHES):
         lower = product(pair_ref[p, MEMBERS:], middles[p])
-        split_lower = halves(lower)
-        forcing = jnp.broadcast_to(force_ref[p : p + 1] + tail[p : p + 1], (16, MEMBERS))
-        once = product(halves(forcing), split_lower)
-        mean_weight = product(halves(once), split_lower)[0:1] * (1.0 / norms[p])
+        forcing = force_ref[p : p + 1] + tail[p : p + 1]
+        once = jnp.sum(lower * forcing, axis=1, keepdims=True)
+        mean_weight = jnp.sum(lower * once, axis=0, keepdims=True) * (1.0 / norms[p])
         scale = jnp.sqrt(MEMBERS - 1.0) / jnp.sqrt(norms[p])
         transform = (lower * scale + mean_weight).astype(BF16)
-        cells = pl.ds(p * 2 * CELLS, 2 * CELLS)
-        spread[:, cells] = base_ref[:, cells] + jnp.dot(
-            transform, departure_ref[:, cells], preferred_element_type=F32
-        )
+        transforms.append(jnp.concatenate([transform, unit], axis=1))
 
     copies = []
     for v in range(2):
+        for p in range(PATCHES):
+            cells = pl.ds((2 * p + v) * CELLS, CELLS)
+            updated = jnp.dot(
+                transforms[p],
+                jnp.concatenate([departure_ref[:, cells], base_ref[:, cells]], axis=0),
+                preferred_element_type=F32,
+            )
+            spread[v, :, pl.ds(p * CELLS, CELLS)] = updated + rest_ref[0:1, cells]
         for m in range(MEMBERS // 16):
             rows = pl.ds(m * 16, 16)
             for g in range(2):
-                groups = [
-                    spread[rows, pl.ds(b * 2 * CELLS + v * CELLS + g * COLS, COLS)] for b in range(PATCHES)
-                ]
-                lines = swap_groups(groups)
+                lines = swap_groups(
+                    [spread[v, rows, pl.ds(b * CELLS + g * COLS, COLS)] for b in range(PATCHES)]
+                )
                 for k in range(8):
-                    scratch[pl.ds(m * 256 + g * 8 + k, 16, stride=16), :] = lines[k]
-            held[v, rows] = scratch[pl.ds(m * 256, 256), :].reshape(16, ROWS, COLS).astype(BF16)
+                    scratch[v, pl.ds(m * 256 + g * 8 + k, 16, stride=16), :] = lines[k]
+            held[v, rows] = scratch[v, pl.ds(m * 256, 256), :].reshape(16, ROWS, COLS).astype(BF16)
             copies.append(fetch(held.at[v, rows], out_ref.at[v, rows], sems.at[v * (MEMBERS // 16) + m]))
     for copy in copies:
         copy.wait()
@@ -449,10 +455,15 @@
     lines_shape = (MEMBERS * ROWS, COLS)
     copies = pltpu.SemaphoreType.DMA
     lat_odd = (lax.axis_index("lat") & 1) == 1
-    line = lax.broadcasted_iota(jnp.int32, (8, slots), 0)
-    pack = jnp.zeros((8, slots), F32)
-    for k, array in enumerate((obs_cell, obs_value, obs_err, obs_count)):
-        pack = jnp.where(line == k, array.reshape(1, -1).astype(F32), pack)
+    cell, value, err = (array.reshape(1, slots).astype(F32) for array in (obs_cell, obs_value, obs_err))
+    used = lax.broadcasted_iota(jnp.int32, (1, slots), 1) < obs_count
+    parts = [cell, jnp.where(used, 1.0 / (err * err), 0.0), jnp.where(used, value, 0.0)]
+    parts.append(land.reshape(1, ROWS * COLS).astype(F32))
+    room = sum(part.shape[1] for part in parts)
+    pack, start = 0.0, 0
+    for part in parts:
+        pack = pack + jnp.pad(part, ((0, 0), (start, room - start - part.shape[1])))
+        start += part.shape[1]
     top, bottom = background[0, :, 0], background[0, :, ROWS - 1]
     rows = exchange(
         jnp.where(lat_odd, top, bottom), jnp.where(lat_odd, bottom, top), "lat", False
@@ -467,7 +478,7 @@
         ],
         [pltpu.VMEM(lines_shape, F32), copies((PARTS,))],
         10**7, 2 * 10**6,
-        background, pack, land,
+        background, pack,
         far=(0,),
     )
     rim, even, odd = call(
@@ -494,13 +505,14 @@
         blocks, rim, *neighbours, table,
     )
     packed = exchange(even, odd, "lat", False)
-    gram, force, departure, base = call(
+    gram, force, departure, base, rest = call(
         centre_kernel,
         [
             shape((PATCHES, MEMBERS, MEMBERS), F32),
             shape((PATCHES, MEMBERS), F32),
             shape((MEMBERS, 2 * span), BF16),
-            shape((MEMBERS, 2 * span), F32),
+            shape((MEMBERS, 2 * span), BF16),
+            shape((8, 2 * span), F32),
         ],
         [pltpu.VMEM((MEMBERS, span), BF16), field, pltpu.VMEM(lines_shape, F32), copies((PARTS,))],
         10**9, 5 * 10**6,
@@ -512,13 +524,13 @@
         [shape(background.shape, BF16)],
         [
             pltpu.VMEM((PATCHES, 2 * MEMBERS, 2 * MEMBERS), BF16),
-            pltpu.VMEM(lines_shape, F32),
-            pltpu.VMEM((MEMBERS, 2 * span), F32),
+            pltpu.VMEM((2,) + lines_shape, F32),
+            pltpu.VMEM((2, MEMBERS, span), F32),
             pltpu.VMEM(background.shape, BF16),
             copies((2 * MEMBERS // 16,)),
         ],
         2 * 10**9, 5 * 10**6,
-        *packed, gram, force, departure, base,
+        *packed, gram, force, departure, base, rest,
         out_far=True,
     )
     return analysis

time: 42.4 us -> 37 us (0.87)
  Pallas kernels: 18.8 us -> 14.9 us
  other arithmetic: 2.18 us -> 0.05 us
  waiting for transfers between devices: 4.19 us -> 5.19 us
    pallas_call x6, Pallas kernels: 18.8 us -> 14.9 us  [call(): pl.pallas_call(kernel, out_shape=out_shape, in_specs=[anywhere if i in fa...]
    convert_element_type x2, other arithmetic: 1.38 us -> 0.01 us  [the longest x1 0.01 us: body(): array.reshape(1, slots).astype(F32)]
    ppermute x3, waiting for transfers between devices: 0.01 us -> 0.95 us  [exchange(): lax.ppermute(even, axis, pairs_inside(size))]
    ppermute x3, starting transfers between devices: 2.27 us -> 1.36 us  [exchange(): lax.ppermute(even, axis, pairs_inside(size))]
    select_n x1, other arithmetic: 0.76 us -> 0.02 us  [body(): jnp.where(used, value, 0.0)]
    ppermute x3, starting transfers between devices: 11.8 us -> 12.4 us  [exchange(): lax.ppermute(odd, axis, pairs_across(size, wrap))]
  transfers between devices with their start and end apart: 6 -> 6, of which waited for: 2 -> 3; matrix products, arithmetic and copies ran while one was open for 5% -> 0% of each run, Pallas kernels for 18% -> 19%
where the time goes in v2:
time: 37 us; the launch traced here: 36.8 us
  Pallas kernels  14.9 us (40%)
  starting transfers between devices  13.8 us (37%)
  waiting for transfers between devices  5.19 us (14%)
  local copies, waits for them, and re-layouts  1.83 us (5%)
  between operations  1 us (3%)
    pallas_call x6, Pallas kernels, call(): pl.pallas_call(kernel, out_shape=out_shape, in_specs=[anywhere if i in fa...  14.9 us
    ppermute x3, starting transfers between devices, exchange(): lax.ppermute(odd, axis, pairs_across(size, wrap))  12.4 us
    ppermute x3, waiting for transfers between devices, exchange(): lax.ppermute(odd, axis, pairs_across(size, wrap))  4.24 us
    ppermute x3, starting transfers between devices, exchange(): lax.ppermute(even, axis, pairs_inside(size))  1.36 us
    slice x1, local copies, waits for them, and re-layouts, body(): top, bottom = (background[0, :, 0], background[0, :, ROWS - 1])  1.13 us
    ppermute x3, waiting for transfers between devices, exchange(): lax.ppermute(even, axis, pairs_inside(size))  0.95 us
  transfers between devices with their start and end apart: 6, of which 3 were waited for; matrix products, arithmetic and copies ran while one was open for 0% of the time, Pallas kernels for 19%

profile of v2, /device:TPU:102, one launch (start us, length us, event | category | flops | bytes accessed | tf_op | source)
XLA Modules:
  0.0 36.8 jit_solution(16151084224368591334)
XLA Ops:
  0.0 1.1 %fusion = (bf16[1,128,1,128]{3,2,1,0:T(2,128)(2,1)S(1)}, bf16[1,128,1,128]{3,2,1,0:T(2,128)(2,1)S(1)}) fusion(bf16[2,128,16,128]{3,2,1,0:T(8,128)(2,1)} %background_ref.3), kind=kLoop, calls=%fused_computation.6 | loop fusion | bytes 131072 | tf_op jit(solution)/shard_map/slice | solution.py:467
  1.1 0.0 copy-start.2
  1.2 0.0 copy-start.1
  1.2 5.3 %collective-permute-start.1 = (bf16[128,128]{1,0:T(8,128)(2,1)S(1)}, bf16[128,128]{1,0:T(8,128)(2,1)S(1)}, u32[]{:S(2)}, u32[]{:S(2)}) collective-permute-start(bf16[128,128]{1,0:T(8,128)(2,1)S(1)} %get-tuple-element.41), channel_id=1, source_target_pairs={{1,2},{2,1},{3,4},{4,3},{5,6},{6,5},{7,8},{8,7},{9,10},{10,9},{11,... | collective-permute-start | bytes 98312 | tf_op jit(solution)/shard_map/ppermute | solution.py:446
  6.5 0.1 collective-permute-start
  7.2 0.0 copy-done.2
  7.3 0.0 copy-done.1
  7.3 0.0 copy-start.3
  7.3 0.0 copy-start.4
  7.3 0.7 %copy-done.3 = bf16[1,1,1024]{2,1,0:T(2,128)(2,1)S(1)} copy-done((bf16[1,1,1024]{2,1,0:T(2,128)(2,1)S(1)}, bf16[1,1,1024]{2,1,0:T(2,128)(2,1)}, u32[]{:S(2)}) %copy-start.3) | copy-done | bytes 2072
  8.0 0.0 copy-done.4
  8.0 1.5 %shard_map.64 = (bf16[128,16,128]{2,1,0:T(8,128)(2,1)S(1)}, bf16[144,512]{1,0:T(8,128)(2,1)S(1)}, bf16[16,2048]{1,0:T(8,128)(2,1)S(1)}, f32[8,256]{1,0:T(8,128)S(1)}) custom-call(bf16[2,128,16,128]{3,2,1,0:T(8,128)(2,1)} %background_ref.3, f32[1,5120]{1,0:T(1,128)S(1)} %pad_add_fusion.pack_ref), custom_call_target="tpu_custom_call" | custom-call | flops 10000000 | bytes 2000000 | tf_op jit(solution)/shard_map/pallas_call | solution.py:416
  9.5 0.0 collective-permute-done.1.second_ref
  9.6 0.9 %collective-permute-done.first_ref = bf16[128,128]{1,0:T(8,128)(2,1)S(1)} collective-permute-done((bf16[128,128]{1,0:T(8,128)(2,1)S(1)}, bf16[128,128]{1,0:T(8,128)(2,1)S(1)}, u32[]{:S(2)}, u32[]{:S(2)}) %collective-permute-start) | collective-permute-done | bytes 32800 | tf_op jit(solution)/shard_map/ppermute | solution.py:445
  10.5 0.2 shard_map.66
  10.7 0.1 collective-permute-start.2
  10.8 3.7 %collective-permute-start.3 = (bf16[144,384]{1,0:T(8,128)(2,1)S(1)}, bf16[144,384]{1,0:T(8,128)(2,1)S(1)}, u32[]{:S(2)}, u32[]{:S(2)}) collective-permute-start(bf16[144,384]{1,0:T(8,128)(2,1)S(1)} %get-tuple-element.28), channel_id=1, source_target_pairs={{16,32},{32,16},{48,64},{64,48},{80,96},{96,80},{112,128},{128,112... | collective-permute-start | bytes 331784 | tf_op jit(solution)/shard_map/ppermute | solution.py:446
  14.5 2.1 %shard_map.65 = (bf16[144,2048]{1,0:T(8,128)(2,1)S(1)}, bf16[1152,256]{1,0:T(8,128)(2,1)S(1)}) custom-call(bf16[128,16,128]{2,1,0:T(8,128)(2,1)S(1)} %get-tuple-element.22.held, bf16[16,2048]{1,0:T(8,128)(2,1)S(1)} %get-tuple-element.23.tails_ref), custom_call_target="tpu_custom_call" | custom-call | flops 100000000 | bytes 4000000 | tf_op jit(solution)/shard_map/pallas_call | solution.py:416
  16.5 0.0 collective-permute-done.2.first_ref
  16.6 2.1 %collective-permute-done.3.second_ref = bf16[144,384]{1,0:T(8,128)(2,1)S(1)} collective-permute-done((bf16[144,384]{1,0:T(8,128)(2,1)S(1)}, bf16[144,384]{1,0:T(8,128)(2,1)S(1)}, u32[]{:S(2)}, u32[]{:S(2)}) %collective-permute-start.3) | collective-permute-done | bytes 110624 | tf_op jit(solution)/shard_map/ppermute | solution.py:446
  18.7 0.0 copy-start
  18.7 2.3 %shard_map.67 = (bf16[528,128]{1,0:T(8,128)(2,1)S(1)}, bf16[528,128]{1,0:T(8,128)(2,1)S(1)}, bf16[144,2560]{1,0:T(8,128)(2,1)S(1)}) custom-call(bf16[144,2048]{1,0:T(8,128)(2,1)S(1)} %get-tuple-element.24.blocks_ref, bf16[128,1024]{1,0:T(8,128)(2,1)S(1)} %get-tuple-element.26.rim_ref, bf16[144,384]{1,0:T(8,128)(2,1)S(1)} %collective-permute-done.2.first_ref, ...), custom_call_target="tpu_custom_call" | custom-call | flops 1000000000 | bytes 3000000 | tf_op jit(solution)/shard_map/pallas_call | solution.py:416
  20.9 1.2 %collective-permute-start.4 = (bf16[528,128]{1,0:T(8,128)(2,1)S(1)}, bf16[528,128]{1,0:T(8,128)(2,1)S(1)}, u32[]{:S(2)}, u32[]{:S(2)}) collective-permute-start(bf16[528,128]{1,0:T(8,128)(2,1)S(1)} %get-tuple-element.30), channel_id=1, source_target_pairs={{0,1},{1,0},{2,3},{3,2},{4,5},{5,4},{6,7},{7,6},{8,9},{9,8},{10,11... | collective-permute-start | bytes 405512 | tf_op jit(solution)/shard_map/ppermute | solution.py:445
  22.1 3.5 %collective-permute-start.5 = (bf16[528,128]{1,0:T(8,128)(2,1)S(1)}, bf16[528,128]{1,0:T(8,128)(2,1)S(1)}, u32[]{:S(2)}, u32[]{:S(2)}) collective-permute-start(bf16[528,128]{1,0:T(8,128)(2,1)S(1)} %get-tuple-element.31), channel_id=1, source_target_pairs={{1,2},{2,1},{3,4},{4,3},{5,6},{6,5},{7,8},{8,7},{9,10},{10,9},{11,... | collective-permute-start | bytes 405512 | tf_op jit(solution)/shard_map/ppermute | solution.py:446
  25.6 0.0 copy-done
  25.6 3.4 %shard_map.68 = (f32[8,128,128]{2,1,0:T(8,128)S(1)}, f32[8,128]{1,0:T(8,128)S(1)}, bf16[128,4096]{1,0:T(8,128)(2,1)S(1)}, bf16[128,4096]{1,0:T(8,128)(2,1)S(1)}, f32[8,4096]{1,0:T(8,128)S(1)}) custom-call(bf16[144,2560]{1,0:T(8,128)(2,1)S(1)} %get-tuple-element.32.pert, bf16[144,2048]{1,0:T(8,128)(2,1)S(1)} %get-tuple-element.24.blocks_ref, ...), custom_call_target="tpu_custom_call" | custom-call | flops 1000000000 | bytes 5000000 | tf_op jit(solution)/shard_map/pallas_call | solution.py:416
  29.0 0.0 collective-permute-done.4.first_ref
  29.0 2.1 %collective-permute-done.5.second_ref = bf16[528,128]{1,0:T(8,128)(2,1)S(1)} collective-permute-done((bf16[528,128]{1,0:T(8,128)(2,1)S(1)}, bf16[528,128]{1,0:T(8,128)(2,1)S(1)}, u32[]{:S(2)}, u32[]{:S(2)}) %collective-permute-start.5) | collective-permute-done | bytes 135200 | tf_op jit(solution)/shard_map/ppermute | solution.py:446
  31.1 5.5 %shard_map.69 = bf16[2,128,16,128]{3,2,1,0:T(8,128)(2,1)} custom-call(bf16[528,128]{1,0:T(8,128)(2,1)S(1)} %collective-permute-done.4.first_ref, bf16[528,128]{1,0:T(8,128)(2,1)S(1)} %collective-permute-done.5.second_ref, f32[8,128,128]{2,1,0:T(8,128)S(1)} %get-tuple-element.34.gram_ref, f32[8,128]{1,0:T(8,128)S(1)} %get-tuple-element.35.force_ref, ...), custom_call_target="tpu_custom_call" | custom-call | flops 2000000000 | bytes 5000000 | tf_op jit(solution)/shard_map/pallas_call | solution.py:416
  (5 shorter events, 0.0 us)
Async XLA Ops:
  1.1 6.1 %copy-start.2 = (s32[1,1,1024]{2,1,0:T(1,128)S(1)}, s32[1,1,1024]{2,1,0:T(1,128)}, u32[]{:S(2)}) copy-start(s32[1,1,1024]{2,1,0:T(1,128)} %param.7) | copy-start | bytes 12292
  1.2 6.1 %copy-start.1 = (s32[16,128]{1,0:T(8,128)S(1)}, s32[16,128]{1,0:T(8,128)}, u32[]{:S(2)}) copy-start(s32[16,128]{1,0:T(8,128)} %param.11) | copy-start | bytes 24580
  1.2 8.4 %collective-permute-start.1 = (bf16[128,128]{1,0:T(8,128)(2,1)S(1)}, bf16[128,128]{1,0:T(8,128)(2,1)S(1)}, u32[]{:S(2)}, u32[]{:S(2)}) collective-permute-start(bf16[128,128]{1,0:T(8,128)(2,1)S(1)} %get-tuple-element.41), channel_id=1, source_target_pairs={{1,2},{2,1},{3,4},{4,3},{5,6},{6,5},{7,8},{8,7},{9,10},{10,9},{11,... | collective-permute-start | bytes 98312 | tf_op jit(solution)/shard_map/ppermute | solution.py:446
  6.5 4.0 %collective-permute-start = (bf16[128,128]{1,0:T(8,128)(2,1)S(1)}, bf16[128,128]{1,0:T(8,128)(2,1)S(1)}, u32[]{:S(2)}, u32[]{:S(2)}) collective-permute-start(bf16[128,128]{1,0:T(8,128)(2,1)S(1)} %get-tuple-element.42), channel_id=1, source_target_pairs={{0,1},{1,0},{2,3},{3,2},{4,5},{5,4},{6,7},{7,6},{8,9},{9,8},{10,11... | collective-permute-start | bytes 98312 | tf_op jit(solution)/shard_map/ppermute | solution.py:445
  7.3 0.7 %copy-start.3 = (bf16[1,1,1024]{2,1,0:T(2,128)(2,1)S(1)}, bf16[1,1,1024]{2,1,0:T(2,128)(2,1)}, u32[]{:S(2)}) copy-start(bf16[1,1,1024]{2,1,0:T(2,128)(2,1)} %param.9) | copy-start | bytes 6148
  7.3 0.7 %copy-start.4 = (f32[1,1,1024]{2,1,0:T(1,128)S(1)}, f32[1,1,1024]{2,1,0:T(1,128)}, u32[]{:S(2)}) copy-start(f32[1,1,1024]{2,1,0:T(1,128)} %param.10) | copy-start | bytes 12292
  10.7 5.8 %collective-permute-start.2 = (bf16[144,384]{1,0:T(8,128)(2,1)S(1)}, bf16[144,384]{1,0:T(8,128)(2,1)S(1)}, u32[]{:S(2)}, u32[]{:S(2)}) collective-permute-start(bf16[144,384]{1,0:T(8,128)(2,1)S(1)} %get-tuple-element.27), channel_id=1, source_target_pairs={{0,16},{16,0},{32,48},{48,32},{64,80},{80,64},{96,112},{112,96},{1... | collective-permute-start | bytes 331784 | tf_op jit(solution)/shard_map/ppermute | solution.py:445
  10.8 7.9 %collective-permute-start.3 = (bf16[144,384]{1,0:T(8,128)(2,1)S(1)}, bf16[144,384]{1,0:T(8,128)(2,1)S(1)}, u32[]{:S(2)}, u32[]{:S(2)}) collective-permute-start(bf16[144,384]{1,0:T(8,128)(2,1)S(1)} %get-tuple-element.28), channel_id=1, source_target_pairs={{16,32},{32,16},{48,64},{64,48},{80,96},{96,80},{112,128},{128,112... | collective-permute-start | bytes 331784 | tf_op jit(solution)/shard_map/ppermute | solution.py:446
  18.7 6.9 %copy-start = (bf16[2,128,16,128]{3,2,1,0:T(8,128)(2,1)S(1)}, bf16[2,128,16,128]{3,2,1,0:T(8,128)(2,1)}, u32[]{:S(2)}) copy-start(bf16[2,128,16,128]{3,2,1,0:T(8,128)(2,1)} %background_ref.3) | copy-start | bytes 3145732
  20.9 8.1 %collective-permute-start.4 = (bf16[528,128]{1,0:T(8,128)(2,1)S(1)}, bf16[528,128]{1,0:T(8,128)(2,1)S(1)}, u32[]{:S(2)}, u32[]{:S(2)}) collective-permute-start(bf16[528,128]{1,0:T(8,128)(2,1)S(1)} %get-tuple-element.30), channel_id=1, source_target_pairs={{0,1},{1,0},{2,3},{3,2},{4,5},{5,4},{6,7},{7,6},{8,9},{9,8},{10,11... | collective-permute-start | bytes 405512 | tf_op jit(solution)/shard_map/ppermute | solution.py:445
  22.1 9.0 %collective-permute-start.5 = (bf16[528,128]{1,0:T(8,128)(2,1)S(1)}, bf16[528,128]{1,0:T(8,128)(2,1)S(1)}, u32[]{:S(2)}, u32[]{:S(2)}) collective-permute-start(bf16[528,128]{1,0:T(8,128)(2,1)S(1)} %get-tuple-element.31), channel_id=1, source_target_pairs={{1,2},{2,1},{3,4},{4,3},{5,6},{6,5},{7,8},{8,7},{9,10},{10,9},{11,... | collective-permute-start | bytes 405512 | tf_op jit(solution)/shard_map/ppermute | solution.py:446

commit v3 on v2

--- a/solution.py
+++ b/solution.py
@@ -16,7 +16,8 @@
 CELLS = PATCH * PATCH
 EXTRA = 16
 CHANNELS = MEMBERS + EXTRA
-PACKED = (PATCHES // 2) * MEMBERS + 16
+RIMS = (PATCHES // 2) * MEMBERS + 16
+PACKED = RIMS + 2 * MEMBERS + MEMBERS // 2 + EXTRA
 NT = (((1,), (1,)), ((), ()))
 PARTS = 4
 VMEM_LIMIT = 48 * 1024 * 1024
@@ -36,23 +37,39 @@
         return jnp.where(offset < RADIUS + PATCH / 2.0, 1.0 - offset / span, 0.0)
 
     lon = jnp.where(side == 0, line(column, -1), jnp.where(side == 1, line(column, 0), line(column, 1)))
-    return [line(row, shift) * lon for shift in (1, 0, -1)]
+    inner = (row > 0) & (row < ROWS - 1)
+    return [jnp.where(inner, line(row, shift) * lon, 0.0) for shift in (1, 0, -1)]
+
+
+def rim_taper(first):
+    lane = lax.broadcasted_iota(jnp.int32, (1, 2 * COLS), 1)
+    side = (lane >> 6) - first - 1
+    row, column = (lane >> 4) & 3, lane & (PATCH - 1)
+    span = 2.0 * (RADIUS + PATCH / 2.0)
+    half = (PATCH - 1) / 2.0
+    across = jnp.where((row == 0) | (row == 3), 1.0 - (half + 1.0) / span, 1.0 - half / span)
+    offset = jnp.abs(column.astype(F32) + side.astype(F32) * PATCH - half)
+    along = jnp.where(offset < RADIUS + PATCH / 2.0, 1.0 - offset / span, 0.0)
+    return across * along
 
 
 def stencil_rows(first):
     cell = first + lax.broadcasted_iota(jnp.int32, (COLS, CELLS), 0)
     lane = lax.broadcasted_iota(jnp.int32, (COLS, CELLS), 1)
-    row, column = lane >> 4, lane & (PATCH - 1)
-    if first < 3 * CELLS:
-        side = first // CELLS - 1
-        place = ((cell & (CELLS - 1)) >> 4) - row
-        near = jnp.abs(place) <= 1
-    else:
-        side = (first - 3 * CELLS) // COLS - 1
-        slot = (cell & (COLS - 1)) >> 4
-        near = ((slot == 0) & (row == 0)) | ((slot == 1) & (row == ROWS - 1))
-    beside = jnp.abs(side * PATCH + (cell & (PATCH - 1)) - column) <= 1
+    side = first // CELLS - 1
+    near = jnp.abs(((cell & (CELLS - 1)) >> 4) - (lane >> 4)) <= 1
+    beside = jnp.abs(side * PATCH + (cell & (PATCH - 1)) - (lane & (PATCH - 1))) <= 1
     return jnp.where(near & beside, 1.0, 0.0).astype(BF16)
+
+
+def rim_stencil_rows(place):
+    cell = lax.broadcasted_iota(jnp.int32, (COLS, COLS), 0)
+    lane = lax.broadcasted_iota(jnp.int32, (COLS, COLS), 1)
+    row = (lane >> 4) & 3
+    step = (cell >> 4) - jnp.where(row < 2, row, row + 2)
+    side = place - 1 - (lane >> 6)
+    beside = jnp.abs(side * PATCH + (cell & (PATCH - 1)) - (lane & (PATCH - 1))) <= 1
+    return jnp.where((step >= 0) & (step <= 2) & beside, 1.0, 0.0).astype(BF16)
 
 
 def swap_groups(arrays):
@@ -107,9 +124,10 @@
             out_ref[pl.ds(m * 16, 16), pl.ds(b * CELLS, CELLS)] = both
 
 
-def strip_kernel(background_ref, pack_ref, held, sides_ref, tails_ref, mask_ref, lines, sems):
+def strip_kernel(background_ref, pack_ref, held, even_ref, odd_ref, tails_ref, mask_ref, lines, sems):
+    lon_odd = (lax.axis_index("lon") & 1) == 1
     copies = fetch_field(background_ref, 0, held, sems)
-    slots = (pack_ref.shape[1] - ROWS * COLS) // 3
+    slots = (pack_ref.shape[1] - (ROWS + 1) * COLS) // 3
     halves = []
     for g in range(2):
         rows = [
@@ -123,8 +141,11 @@
         mask = jnp.where(which == b, jnp.concatenate([halves[0][b], halves[1][b]], axis=1), mask)
     mask_ref[...] = mask
     cell = pack_ref[:, pl.ds(0, slots)].astype(jnp.int32)
-    inverse = pack_ref[:, pl.ds(slots, slots)]
-    value = pack_ref[:, pl.ds(2 * slots, slots)]
+    count = pack_ref[:, pl.ds(3 * slots + ROWS * COLS, COLS)][:, 0:1].astype(jnp.int32)
+    used = lax.broadcasted_iota(jnp.int32, (1, slots), 1) < count
+    err = pack_ref[:, pl.ds(2 * slots, slots)]
+    inverse = jnp.where(used, 1.0 / (err * err), 0.0)
+    value = jnp.where(used, pack_ref[:, pl.ds(slots, slots)], 0.0)
     column = cell & (COLS - 1)
     block = column >> 4
     place = ((cell >> 7) << 4) + (column & (PATCH - 1))
@@ -144,9 +165,9 @@
         ).astype(BF16)
         tails_ref[:, pl.ds(b * CELLS, CELLS)] = tail
         if b == 0:
-            sides_ref[pl.ds(MEMBERS, EXTRA), pl.ds(0, CELLS)] = tail
-        if b == PATCHES - 1:
-            sides_ref[pl.ds(MEMBERS, EXTRA), pl.ds(CELLS, CELLS)] = tail
+            west = tail
+    even_ref[pl.ds(MEMBERS, EXTRA), :] = jnp.where(lon_odd, west, tail)
+    odd_ref[pl.ds(MEMBERS, EXTRA), :] = jnp.where(lon_odd, tail, west)
 
     widen_lines(copies, held, lines)
     group = lax.broadcasted_iota(jnp.int32, (16, COLS), 1) >> 4
@@ -159,85 +180,46 @@
                 here = group == r
                 west = jnp.where(here, pltpu.roll(row, PATCH * r, 1) if r else row, west)
                 east = jnp.where(here, pltpu.roll(row, PATCH * (r + 1), 1) if r < 7 else row, east)
-            sides_ref[pl.ds(m * 16, 16), pl.ds(g * COLS, COLS)] = west
-            sides_ref[pl.ds(m * 16, 16), pl.ds(CELLS + g * COLS, COLS)] = east
+            even_ref[pl.ds(m * 16, 16), pl.ds(g * COLS, COLS)] = jnp.where(lon_odd, west, east)
+            odd_ref[pl.ds(m * 16, 16), pl.ds(g * COLS, COLS)] = jnp.where(lon_odd, east, west)
 
 
 def block_kernel(held, tails_ref, blocks_ref, table_ref, lines):
-    for first in range(0, 3 * (CELLS + COLS), COLS):
+    for first in range(0, 3 * CELLS, COLS):
         table_ref[pl.ds(first, COLS), :] = stencil_rows(first)
     widen_lines((), held, lines)
     to_blocks(lines, blocks_ref)
     blocks_ref[pl.ds(MEMBERS, EXTRA), :] = tails_ref[...]
 
 
-def rim_kernel(first_ref, second_ref, sides_ref, rim_ref, even_ref, odd_ref):
+def shift(piece, lanes):
+    return pltpu.roll(piece, lanes % COLS, 1) if lanes % COLS else piece
+
+
+def quarters(pieces, offset, lane):
+    tile = shift(pieces[0], -offset)
+    for q in range(1, len(pieces)):
+        tile = jnp.where((lane >> 5) == q, shift(pieces[q], 32 * q - offset), tile)
+    return tile
+
+
+def gram_kernel(blocks_ref, first_ref, second_ref, table_ref, even_ref, odd_ref, pert, wide):
     lat_odd = (lax.axis_index("lat") & 1) == 1
-    lon_odd = (lax.axis_index("lon") & 1) == 1
-    first = first_ref[...].astype(F32)
-    second = second_ref[...].astype(F32)
-    above = jnp.where(lat_odd, first, second)
-    below = jnp.where(lat_odd, second, first)
-    lane = lax.broadcasted_iota(jnp.int32, (MEMBERS, COLS), 1)
-    for b in range(PATCHES):
-        top = pltpu.roll(above, (COLS - PATCH * b) % COLS, 1)
-        low = pltpu.roll(below, (COLS - PATCH * b + PATCH) % COLS, 1)
-        edge = jnp.where(lane < PATCH, top, jnp.where(lane < 2 * PATCH, low, 0.0)).astype(BF16)
-        rim_ref[:, pl.ds(b * COLS, COLS)] = edge
-        if b == 0:
-            west_rim = edge
-        if b == PATCHES - 1:
-            east_rim = edge
-    west = sides_ref[:, pl.ds(0, CELLS)]
-    east = sides_ref[:, pl.ds(CELLS, CELLS)]
-    even_ref[:, pl.ds(0, CELLS)] = jnp.where(lon_odd, west, east)
-    odd_ref[:, pl.ds(0, CELLS)] = jnp.where(lon_odd, east, west)
-    even_ref[pl.ds(0, MEMBERS), pl.ds(CELLS, COLS)] = jnp.where(lon_odd, west_rim, east_rim)
-    odd_ref[pl.ds(0, MEMBERS), pl.ds(CELLS, COLS)] = jnp.where(lon_odd, east_rim, west_rim)
-    blank = jnp.zeros((EXTRA, COLS), BF16)
-    even_ref[pl.ds(MEMBERS, EXTRA), pl.ds(CELLS, COLS)] = blank
-    odd_ref[pl.ds(MEMBERS, EXTRA), pl.ds(CELLS, COLS)] = blank
-
-
-def gram_kernel(
-    blocks_ref, rim_ref, first_ref, second_ref, table_ref,
-    even_ref, odd_ref, pert, wide, wide_rim,
-):
-    lat = lax.axis_index("lat")
-    lat_odd = (lat & 1) == 1
     lon_odd = (lax.axis_index("lon") & 1) == 1
     span = PATCHES * CELLS
     wide[:, pl.ds(0, CELLS)] = jnp.zeros((CHANNELS, CELLS), BF16)
     wide[:, pl.ds(span + 3 * CELLS, CELLS)] = jnp.zeros((CHANNELS, CELLS), BF16)
     wide[:, pl.ds(2 * CELLS, span)] = blocks_ref[...]
-    one = first_ref[:, pl.ds(0, CELLS)]
-    two = second_ref[:, pl.ds(0, CELLS)]
+    one, two = first_ref[...], second_ref[...]
     wide[:, pl.ds(CELLS, CELLS)] = jnp.where(lon_odd, one, two)
     wide[:, pl.ds(span + 2 * CELLS, CELLS)] = jnp.where(lon_odd, two, one)
-    rim_span = PATCHES * COLS
-    blank = jnp.zeros((MEMBERS, COLS), BF16)
-    wide_rim[:, pl.ds(0, COLS)] = blank
-    wide_rim[:, pl.ds(rim_span + 3 * COLS, COLS)] = blank
-    wide_rim[:, pl.ds(2 * COLS, rim_span)] = rim_ref[...]
-    one = first_ref[pl.ds(0, MEMBERS), pl.ds(CELLS, COLS)]
-    two = second_ref[pl.ds(0, MEMBERS), pl.ds(CELLS, COLS)]
-    wide_rim[:, pl.ds(COLS, COLS)] = jnp.where(lon_odd, one, two)
-    wide_rim[:, pl.ds(rim_span + 2 * COLS, COLS)] = jnp.where(lon_odd, two, one)
-
-    lane = lax.broadcasted_iota(jnp.int32, (1, CELLS), 1)
-    row = lane >> 4
-    last = lax.axis_size("lat") - 1
-    short = ((row == 0) & (lat == 0)) | ((row == ROWS - 1) & (lat == last))
-    share = jnp.where(short, 1.0 / 6.0, 1.0 / 9.0)
+
     tail_row = lax.broadcasted_iota(jnp.int32, (EXTRA, CELLS), 0)
     for e in range(PATCHES + 2):
         summed = jnp.dot(
-            wide[pl.ds(0, MEMBERS), pl.ds(e * CELLS, 3 * CELLS)], table_ref[pl.ds(0, 3 * CELLS), :], preferred_element_type=F32
+            wide[pl.ds(0, MEMBERS), pl.ds(e * CELLS, 3 * CELLS)], table_ref[...], preferred_element_type=F32
         )
-        summed = summed + jnp.dot(
-            wide_rim[:, pl.ds(e * COLS, 3 * COLS)], table_ref[pl.ds(3 * CELLS, 3 * COLS), :], preferred_element_type=F32
-        )
-        mean = summed * share
+        mean = summed * (1.0 / 9.0)
         average = jnp.sum(mean, axis=0, keepdims=True) * (1.0 / MEMBERS)
         pert[pl.ds(0, MEMBERS), pl.ds(e * CELLS, CELLS)] = (mean - average).astype(BF16)
         tail = wide[pl.ds(MEMBERS, EXTRA), pl.ds((e + 1) * CELLS, CELLS)].astype(F32)
@@ -245,6 +227,30 @@
         pert[pl.ds(MEMBERS, EXTRA), pl.ds(e * CELLS, CELLS)] = jnp.where(
             tail_row == 0, innovation, jnp.where(tail_row == 1, tail[0:1], 0.0)
         ).astype(BF16)
+
+    lane = lax.broadcasted_iota(jnp.int32, (MEMBERS, COLS), 1)
+    tail_lane = lax.broadcasted_iota(jnp.int32, (EXTRA, COLS), 1)
+    rims, rim_tails = [], []
+    for part, offset in ((0, 0), (1, COLS - 32)):
+        tiles, tails = [], []
+        for t in range(3):
+            some = range(4 * t, min(4 * t + 4, PATCHES + 2))
+            places = [pl.ds((e + 1) * CELLS + part * COLS, COLS) for e in some]
+            tiles.append(quarters([wide[pl.ds(0, MEMBERS), place] for place in places], offset, lane))
+            tail = [wide[pl.ds(MEMBERS, EXTRA), place].astype(F32) for place in places]
+            tails.append(quarters(tail, offset, tail_lane)[0:2])
+        half = MEMBERS // 2
+        tiles[2] = jnp.where(lane[:half] < 64, tiles[2][:half], shift(tiles[2][half:], 64))
+        rims.append(tiles)
+        rim_tails.append(jnp.concatenate(tails + [jnp.zeros((EXTRA - 6, COLS), F32)], axis=0).astype(BF16))
+    start = RIMS
+    for t in range(3):
+        size = rims[0][t].shape[0]
+        even_ref[pl.ds(start, size), :] = jnp.where(lat_odd, rims[0][t], rims[1][t])
+        odd_ref[pl.ds(start, size), :] = jnp.where(lat_odd, rims[1][t], rims[0][t])
+        start += size
+    even_ref[pl.ds(start, EXTRA), :] = jnp.where(lat_odd, rim_tails[0], rim_tails[1])
+    odd_ref[pl.ds(start, EXTRA), :] = jnp.where(lat_odd, rim_tails[1], rim_tails[0])
 
     r = lax.broadcasted_iota(jnp.int32, (MEMBERS, MEMBERS), 0)
     c = lax.broadcasted_iota(jnp.int32, (MEMBERS, MEMBERS), 1)
@@ -256,9 +262,9 @@
         taper = jnp.where(lat_odd, near, far)
         forcings, diagonals = [], []
         for pair in range(PATCHES // 2):
-            first, forcing = patch_gram(pert, 2 * pair, taper, same)
+            first, forcing = patch_gram(pert, window_of(2 * pair), taper, same)
             forcings.append(forcing)
-            second, forcing = patch_gram(pert, 2 * pair + 1, taper, same)
+            second, forcing = patch_gram(pert, window_of(2 * pair + 1), taper, same)
             forcings.append(forcing)
             diagonals.append(jnp.sum(jnp.where(same, second, 0.0), axis=0, keepdims=True))
             out_ref[pl.ds(pair * MEMBERS, MEMBERS), :] = jnp.where(lower, first, second).astype(BF16)
@@ -266,8 +272,8 @@
         out_ref[pl.ds(base, 16), :] = jnp.concatenate(tail, axis=0).astype(BF16)
 
 
-def patch_gram(pert, p, taper, same):
-    window = pert[:, pl.ds(p * CELLS, 3 * CELLS)]
+def patch_gram(pert, lanes, taper, same):
+    window = pert[:, lanes]
     precision = window[MEMBERS:].astype(F32)[1:2]
     scaled = (window[:MEMBERS].astype(F32) * (precision * taper)).astype(BF16)
     full = lax.dot_general(scaled, window, NT, preferred_element_type=F32)
@@ -275,8 +281,13 @@
     return full[:, :MEMBERS], forcing
 
 
-def centre_kernel(pert, blocks_ref, background_ref, mask_ref,
-                  gram_ref, force_ref, departure_ref, base_ref, rest_ref, soil, held, lines, sems):
+def window_of(p):
+    return pl.ds(p * CELLS, 3 * CELLS)
+
+
+def centre_kernel(pert, wide, blocks_ref, background_ref, mask_ref,
+                  gram_ref, force_ref, departure_ref, base_ref, rest_ref, rim_ref, rim_table_ref,
+                  soil, held, lines, sems):
     copies = fetch_field(background_ref, 1, held, sems)
     r = lax.broadcasted_iota(jnp.int32, (MEMBERS, MEMBERS), 0)
     c = lax.broadcasted_iota(jnp.int32, (MEMBERS, MEMBERS), 1)
@@ -284,10 +295,17 @@
     taper = tapers()[1]
     forcings = []
     for p in range(PATCHES):
-        gram, forcing = patch_gram(pert, p, taper, same)
+        gram, forcing = patch_gram(pert, window_of(p), taper, same)
         gram_ref[p] = gram + jnp.where(same, MEMBERS - 1.0, 0.0)
         forcings.append(forcing)
     force_ref[...] = jnp.concatenate(forcings, axis=0)
+    for place in range(4):
+        rim_table_ref[pl.ds(place * COLS, COLS), :] = rim_stencil_rows(place)
+    lane = lax.broadcasted_iota(jnp.int32, (CHANNELS, COLS), 1)
+    for e in range(PATCHES + 4):
+        upper = shift(wide[:, pl.ds(e * CELLS, COLS)], 32)
+        lower = shift(wide[:, pl.ds(e * CELLS + COLS, COLS)], -32)
+        rim_ref[:, pl.ds(e * COLS, COLS)] = jnp.where(lane < 64, upper, lower)
     widen_lines(copies, held, lines)
     to_blocks(lines, soil)
     for p in range(PATCHES):
@@ -329,15 +347,81 @@
     return out[:, :MEMBERS] + out[:, MEMBERS:]
 
 
-def solve_kernel(first_ref, second_ref, gram_ref, force_ref, departure_ref, base_ref, rest_ref, out_ref,
-                 pair_ref, scratch, spread, held, sems):
+def rim_perts(first_ref, second_ref, rim_ref, rim_table_ref, wide_rim, pert):
+    lat = lax.axis_index("lat")
+    lat_odd = (lat & 1) == 1
+    last = lax.axis_size("lat") - 1
+    half = MEMBERS // 2
+
+    def tiles_of(source):
+        folded = source(RIMS + 2 * MEMBERS, half)
+        tails = source(RIMS + 2 * MEMBERS + half, EXTRA).astype(F32)
+        tiles = [source(RIMS, MEMBERS), source(RIMS + MEMBERS, MEMBERS)]
+        return tiles + [jnp.concatenate([folded, shift(folded, 64)], axis=0)], tails
+
+    def above(start, size):
+        rows = pl.ds(start, size)
+        return jnp.where(lat_odd, first_ref[rows, :], second_ref[rows, :])
+
+    def below(start, size):
+        rows = pl.ds(start, size)
+        return jnp.where(lat_odd, second_ref[rows, :], first_ref[rows, :])
+
+    top, top_tails = tiles_of(above)
+    low, low_tails = tiles_of(below)
+    lane = lax.broadcasted_iota(jnp.int32, (MEMBERS, COLS), 1)
+    tail_lane = lax.broadcasted_iota(jnp.int32, (8, COLS), 1)
+    wide_rim[:, pl.ds(0, COLS)] = jnp.zeros((MEMBERS, COLS), BF16)
+    wide_rim[:, pl.ds((PATCHES + 3) * COLS, COLS)] = jnp.zeros((MEMBERS, COLS), BF16)
+    tails = []
+    for e in range(PATCHES + 2):
+        t, q = divmod(e, 4)
+        place = pl.ds((e + 1) * COLS, COLS)
+        own = rim_ref[pl.ds(0, MEMBERS), place]
+        mixed = jnp.where(lane < 32, shift(top[t], -32 * q), jnp.where(lane < 96, own, shift(low[t], 96 - 32 * q)))
+        wide_rim[:, place] = mixed
+        own = rim_ref[pl.ds(MEMBERS, EXTRA), place].astype(F32)[:8]
+        row = jnp.zeros((6, COLS), F32)
+        upper = shift(jnp.concatenate([top_tails[2 * t : 2 * t + 2], row], axis=0), -32 * q)
+        lower = shift(jnp.concatenate([low_tails[2 * t : 2 * t + 2], row], axis=0), 96 - 32 * q)
+        tails.append(jnp.where(tail_lane < 32, upper, jnp.where(tail_lane < 96, own, lower)))
+    line = lax.broadcasted_iota(jnp.int32, (1, COLS), 1)
+    row = (line >> 4) & 3
+    short = ((row == 1) & (lat == 0)) | ((row == 2) & (lat == last))
+    share = jnp.where(short, 1.0 / 6.0, 1.0 / 9.0)
+    tail_row = lax.broadcasted_iota(jnp.int32, (EXTRA, COLS), 0)
+    for t in range(PATCHES // 2 + 1):
+        place = pl.ds(t * COLS, COLS)
+        summed = jnp.dot(
+            wide_rim[:, pl.ds(2 * t * COLS, 4 * COLS)], rim_table_ref[...], preferred_element_type=F32
+        )
+        mean = summed * share
+        average = jnp.sum(mean, axis=0, keepdims=True) * (1.0 / MEMBERS)
+        pert[pl.ds(0, MEMBERS), place] = (mean - average).astype(BF16)
+        left, right = tails[2 * t], tails[2 * t + 1]
+        group = tail_lane >> 5
+        tail = jnp.where(
+            group == 0,
+            shift(left, -16),
+            jnp.where(group == 1, shift(left, -48), jnp.where(group == 2, shift(right, 48), shift(right, 16))),
+        )
+        innovation = tail[1:2] - average
+        pert[pl.ds(MEMBERS, EXTRA), place] = jnp.where(
+            tail_row == 0, innovation, jnp.where(tail_row == 1, tail[0:1], 0.0)
+        ).astype(BF16)
+
+
+def solve_kernel(first_ref, second_ref, gram_ref, force_ref, departure_ref, base_ref, rest_ref,
+                 rim_ref, rim_table_ref, out_ref,
+                 pair_ref, scratch, spread, held, wide_rim, pert, sems):
+    rim_perts(first_ref, second_ref, rim_ref, rim_table_ref, wide_rim, pert)
     r = lax.broadcasted_iota(jnp.int32, (MEMBERS, MEMBERS), 0)
     c = lax.broadcasted_iota(jnp.int32, (MEMBERS, MEMBERS), 1)
     eye = jnp.where(r == c, 1.0, 0.0)
     unit = eye.astype(BF16)
     base = (PATCHES // 2) * MEMBERS
     tail = first_ref[pl.ds(base, 16), :].astype(F32) + second_ref[pl.ds(base, 16), :].astype(F32)
-    norms = []
+    norms, rim_forcings = [], []
     for pair in range(PATCHES // 2):
         rows = pl.ds(pair * MEMBERS, MEMBERS)
         mixed = first_ref[rows, :].astype(F32) + second_ref[rows, :].astype(F32)
@@ -349,7 +433,10 @@
         )
         for k in range(2):
             p = 2 * pair + k
-            system = gram_ref[p] + gains[k]
+            lanes = pl.ds((p - k) // 2 * COLS, 2 * COLS)
+            rim_gram, rim_forcing = patch_gram(pert, lanes, rim_taper(k), r == c)
+            rim_forcings.append(rim_forcing)
+            system = gram_ref[p] + gains[k] + rim_gram
             total = jnp.sum(jnp.sum(system * system, axis=0, keepdims=True), axis=1, keepdims=True)
             norm = jnp.sqrt(total)
             norms.append(norm)
@@ -375,7 +462,7 @@
     transforms = []
     for p in range(PATCHES):
         lower = product(pair_ref[p, MEMBERS:], middles[p])
-        forcing = force_ref[p : p + 1] + tail[p : p + 1]
+        forcing = force_ref[p : p + 1] + tail[p : p + 1] + rim_forcings[p]
         once = jnp.sum(lower * forcing, axis=1, keepdims=True)
         mean_weight = jnp.sum(lower * once, axis=0, keepdims=True) * (1.0 / norms[p])
         scale = jnp.sqrt(MEMBERS - 1.0) / jnp.sqrt(norms[p])
@@ -454,25 +541,18 @@
     field = pltpu.VMEM((MEMBERS, ROWS, COLS), BF16)
     lines_shape = (MEMBERS * ROWS, COLS)
     copies = pltpu.SemaphoreType.DMA
-    lat_odd = (lax.axis_index("lat") & 1) == 1
-    cell, value, err = (array.reshape(1, slots).astype(F32) for array in (obs_cell, obs_value, obs_err))
-    used = lax.broadcasted_iota(jnp.int32, (1, slots), 1) < obs_count
-    parts = [cell, jnp.where(used, 1.0 / (err * err), 0.0), jnp.where(used, value, 0.0)]
-    parts.append(land.reshape(1, ROWS * COLS).astype(F32))
-    room = sum(part.shape[1] for part in parts)
+    parts = [array.reshape(1, -1).astype(F32) for array in (obs_cell, obs_value, obs_err, land, obs_count)]
+    room = 3 * slots + (ROWS + 1) * COLS
     pack, start = 0.0, 0
     for part in parts:
         pack = pack + jnp.pad(part, ((0, 0), (start, room - start - part.shape[1])))
         start += part.shape[1]
-    top, bottom = background[0, :, 0], background[0, :, ROWS - 1]
-    rows = exchange(
-        jnp.where(lat_odd, top, bottom), jnp.where(lat_odd, bottom, top), "lat", False
-    )
-    held, sides, tails, mask = call(
+    held, even, odd, tails, mask = call(
         strip_kernel,
         [
             shape((MEMBERS, ROWS, COLS), BF16),
-            shape((CHANNELS, 2 * CELLS), BF16),
+            shape((CHANNELS, CELLS), BF16),
+            shape((CHANNELS, CELLS), BF16),
             shape((EXTRA, span), BF16),
             shape((8, CELLS), F32),
         ],
@@ -481,31 +561,24 @@
         background, pack,
         far=(0,),
     )
-    rim, even, odd = call(
-        rim_kernel,
-        [shape((MEMBERS, PATCHES * COLS), BF16)] + [shape((CHANNELS, CELLS + COLS), BF16)] * 2,
-        [], 10**6, 10**6, *rows, sides,
-    )
     neighbours = exchange(even, odd, "lon", True)
     blocks, table = call(
         block_kernel,
-        [shape((CHANNELS, span), BF16), shape((3 * (CELLS + COLS), CELLS), BF16)],
+        [shape((CHANNELS, span), BF16), shape((3 * CELLS, CELLS), BF16)],
         [pltpu.VMEM(lines_shape, F32)],
         10**8, 4 * 10**6,
         held, tails,
     )
-    even, odd, pert = call(
+    even, odd, pert, wide = call(
         gram_kernel,
-        [shape((PACKED, MEMBERS), BF16)] * 2 + [shape((CHANNELS, span + 2 * CELLS), BF16)],
-        [
-            pltpu.VMEM((CHANNELS, span + 4 * CELLS), BF16),
-            pltpu.VMEM((MEMBERS, (PATCHES + 4) * COLS), BF16),
-        ],
+        [shape((PACKED, MEMBERS), BF16)] * 2
+        + [shape((CHANNELS, span + 2 * CELLS), BF16), shape((CHANNELS, span + 4 * CELLS), BF16)],
+        [],
         10**9, 3 * 10**6,
-        blocks, rim, *neighbours, table,
+        blocks, *neighbours, table,
     )
     packed = exchange(even, odd, "lat", False)
-    gram, force, departure, base, rest = call(
+    gram, force, departure, base, rest, rim, rim_table = call(
         centre_kernel,
         [
             shape((PATCHES, MEMBERS, MEMBERS), F32),
@@ -513,11 +586,13 @@
             shape((MEMBERS, 2 * span), BF16),
             shape((MEMBERS, 2 * span), BF16),
             shape((8, 2 * span), F32),
+            shape((CHANNELS, (PATCHES + 4) * COLS), BF16),
+            shape((4 * COLS, COLS), BF16),
         ],
         [pltpu.VMEM((MEMBERS, span), BF16), field, pltpu.VMEM(lines_shape, F32), copies((PARTS,))],
         10**9, 5 * 10**6,
-        pert, blocks, background, mask,
-        far=(2,),
+        pert, wide, blocks, background, mask,
+        far=(3,),
     )
     (analysis,) = call(
         solve_kernel,
@@ -527,10 +602,12 @@
             pltpu.VMEM((2,) + lines_shape, F32),
             pltpu.VMEM((2, MEMBERS, span), F32),
             pltpu.VMEM(background.shape, BF16),
+            pltpu.VMEM((MEMBERS, (PATCHES + 4) * COLS), BF16),
+            pltpu.VMEM((CHANNELS, (PATCHES // 2 + 1) * COLS), BF16),
             copies((2 * MEMBERS // 16,)),
         ],
         2 * 10**9, 5 * 10**6,
-        *packed, gram, force, departure, base, rest,
+        *packed, gram, force, departure, base, rest, rim, rim_table,
         out_far=True,
     )
     return analysis

time: 37 us -> 32.9 us (0.89)
  the two profiles are of different devices: /device:TPU:102 before, /device:TPU:128 now
where the time goes in v3:
time: 32.9 us; the launch traced here: 32.6 us
  Pallas kernels  17 us (52%)
  starting transfers between devices  9.39 us (29%)
  waiting for transfers between devices  3.98 us (12%)
  between operations  0.9 us (3%)
  other arithmetic  0.7 us (2%)
  local copies, waits for them, and re-layouts  0.69 us (2%)
    pallas_call x5, Pallas kernels, call(): pl.pallas_call(kernel, out_shape=out_shape, in_specs=[anywhere if i in fa...  17 us
    ppermute x2, starting transfers between devices, exchange(): lax.ppermute(odd, axis, pairs_across(size, wrap))  7.86 us
    ppermute x2, waiting for transfers between devices, exchange(): lax.ppermute(odd, axis, pairs_across(size, wrap))  3.16 us
    ppermute x2, starting transfers between devices, exchange(): lax.ppermute(even, axis, pairs_inside(size))  1.53 us
    ppermute x2, waiting for transfers between devices, exchange(): lax.ppermute(even, axis, pairs_inside(size))  0.82 us
    convert_element_type x2, other arithmetic, body(): array.reshape(1, -1).astype(F32)  0.69 us
    unnamed x6, local copies, waits for them, and re-layouts  0.69 us
  transfers between devices with their start and end apart: 4, of which 3 were waited for; matrix products, arithmetic and copies ran while one was open for 0% of the time, Pallas kernels for 17%

profile of v3, /device:TPU:128, one launch (start us, length us, event | category | flops | bytes accessed | tf_op | source)
XLA Modules:
  0.0 32.6 jit_solution(4692165299476414705)
XLA Ops:
  0.0 0.0 copy-start
  0.7 0.7 %convert_bitcast_fusion = f32[1,1024]{1,0:T(1,128)S(1)} fusion(s32[1,1,1024]{2,1,0:T(1,128)} %param.7), kind=kLoop, calls=%fused_computation.1 | loop fusion | flops 1024 | bytes 8192 | tf_op jit(solution)/shard_map/convert_element_type | solution.py:544
  1.4 0.0 copy-done
  1.4 0.0 copy-start.2
  1.4 0.0 copy-start.1
  1.4 0.7 %copy-done.2 = bf16[1,1,1024]{2,1,0:T(2,128)(2,1)S(1)} copy-done((bf16[1,1,1024]{2,1,0:T(2,128)(2,1)S(1)}, bf16[1,1,1024]{2,1,0:T(2,128)(2,1)}, u32[]{:S(2)}) %copy-start.2) | copy-done | bytes 2072
  2.1 0.0 copy-done.1
  2.1 1.5 %shard_map.64 = (bf16[128,16,128]{2,1,0:T(8,128)(2,1)S(1)}, bf16[144,256]{1,0:T(8,128)(2,1)S(1)}, bf16[144,256]{1,0:T(8,128)(2,1)S(1)}, bf16[16,2048]{1,0:T(8,128)(2,1)S(1)}, f32[8,256]{1,0:T(8,128)S(1)}) custom-call(bf16[2,128,16,128]{3,2,1,0:T(8,128)(2,1)} %background_ref.3, f32[1,5248]{1,0:T(1,128)S(1)} %pad_add_fusion.pack_ref), custom_call_target="tpu_custom_call" | custom-call | flops 10000000 | bytes 2000000 | tf_op jit(solution)/shard_map/pallas_call | solution.py:503
  3.6 0.1 collective-permute-start
  3.7 5.6 %collective-permute-start.1 = (bf16[144,256]{1,0:T(8,128)(2,1)S(1)}, bf16[144,256]{1,0:T(8,128)(2,1)S(1)}, u32[]{:S(2)}, u32[]{:S(2)}) collective-permute-start(bf16[144,256]{1,0:T(8,128)(2,1)S(1)} %get-tuple-element.27), channel_id=1, source_target_pairs={{16,32},{32,16},{48,64},{64,48},{80,96},{96,80},{112,128},{128,112... | collective-permute-start | bytes 221192 | tf_op jit(solution)/shard_map/ppermute | solution.py:533
  9.3 1.8 %shard_map.65 = (bf16[144,2048]{1,0:T(8,128)(2,1)S(1)}, bf16[768,256]{1,0:T(8,128)(2,1)S(1)}) custom-call(bf16[128,16,128]{2,1,0:T(8,128)(2,1)S(1)} %get-tuple-element.23.held, bf16[16,2048]{1,0:T(8,128)(2,1)S(1)} %get-tuple-element.24.tails_ref), custom_call_target="tpu_custom_call" | custom-call | flops 100000000 | bytes 4000000 | tf_op jit(solution)/shard_map/pallas_call | solution.py:503
  11.1 0.0 collective-permute-done.first_ref
  11.1 0.2 collective-permute-done.1.second_ref
  11.3 2.0 %shard_map.66 = (bf16[864,128]{1,0:T(8,128)(2,1)S(1)}, bf16[864,128]{1,0:T(8,128)(2,1)S(1)}, bf16[144,2560]{1,0:T(8,128)(2,1)S(1)}, bf16[144,3072]{1,0:T(8,128)(2,1)S(1)}) custom-call(bf16[144,2048]{1,0:T(8,128)(2,1)S(1)} %get-tuple-element.25.blocks_ref, bf16[144,256]{1,0:T(8,128)(2,1)S(1)} %collective-permute-done.first_ref, ...), custom_call_target="tpu_custom_call" | custom-call | flops 1000000000 | bytes 3000000 | tf_op jit(solution)/shard_map/pallas_call | solution.py:503
  13.4 1.4 %collective-permute-start.2 = (bf16[864,128]{1,0:T(8,128)(2,1)S(1)}, bf16[864,128]{1,0:T(8,128)(2,1)S(1)}, u32[]{:S(2)}, u32[]{:S(2)}) collective-permute-start(bf16[864,128]{1,0:T(8,128)(2,1)S(1)} %get-tuple-element.29), channel_id=1, source_target_pairs={{0,1},{1,0},{2,3},{3,2},{4,5},{5,4},{6,7},{7,6},{8,9},{9,8},{10,11... | collective-permute-start | bytes 663560 | tf_op jit(solution)/shard_map/ppermute | solution.py:532
  14.8 2.3 %collective-permute-start.3 = (bf16[864,128]{1,0:T(8,128)(2,1)S(1)}, bf16[864,128]{1,0:T(8,128)(2,1)S(1)}, u32[]{:S(2)}, u32[]{:S(2)}) collective-permute-start(bf16[864,128]{1,0:T(8,128)(2,1)S(1)} %get-tuple-element.30), channel_id=1, source_target_pairs={{1,2},{2,1},{3,4},{4,3},{5,6},{6,5},{7,8},{8,7},{9,10},{10,9},{11,... | collective-permute-start | bytes 663560 | tf_op jit(solution)/shard_map/ppermute | solution.py:533
  17.1 3.8 %shard_map.67 = (f32[8,128,128]{2,1,0:T(8,128)S(1)}, f32[8,128]{1,0:T(8,128)S(1)}, bf16[128,4096]{1,0:T(8,128)(2,1)S(1)}, bf16[128,4096]{1,0:T(8,128)(2,1)S(1)},...) custom-call(bf16[144,2560]{1,0:T(8,128)(2,1)S(1)} %get-tuple-element.31.pert, ...), custom_call_target="tpu_custom_call" | custom-call | flops 1000000000 | bytes 5000000 | tf_op jit(solution)/shard_map/pallas_call | solution.py:503
  20.9 0.8 %collective-permute-done.2.first_ref = bf16[864,128]{1,0:T(8,128)(2,1)S(1)} collective-permute-done((bf16[864,128]{1,0:T(8,128)(2,1)S(1)}, bf16[864,128]{1,0:T(8,128)(2,1)S(1)}, u32[]{:S(2)}, u32[]{:S(2)}) %collective-permute-start.2) | collective-permute-done | bytes 221216 | tf_op jit(solution)/shard_map/ppermute | solution.py:532
  21.8 3.0 %collective-permute-done.3.second_ref = bf16[864,128]{1,0:T(8,128)(2,1)S(1)} collective-permute-done((bf16[864,128]{1,0:T(8,128)(2,1)S(1)}, bf16[864,128]{1,0:T(8,128)(2,1)S(1)}, u32[]{:S(2)}, u32[]{:S(2)}) %collective-permute-start.3) | collective-permute-done | bytes 221216 | tf_op jit(solution)/shard_map/ppermute | solution.py:533
  24.7 7.7 %shard_map.68 = bf16[2,128,16,128]{3,2,1,0:T(8,128)(2,1)} custom-call(bf16[864,128]{1,0:T(8,128)(2,1)S(1)} %collective-permute-done.2.first_ref, bf16[864,128]{1,0:T(8,128)(2,1)S(1)} %collective-permute-done.3.second_ref, f32[8,128,128]{2,1,0:T(8,128)S(1)} %get-tuple-element.34.gram_ref, f32[8,128]{1,0:T(8,128)S(1)} %get-tuple-element.35.force_ref, ...), custom_call_target="tpu_custom_call" | custom-call | flops 2000000000 | bytes 5000000 | tf_op jit(solution)/shard_map/pallas_call | solution.py:503
  (2 shorter events, 0.0 us)
Async XLA Ops:
  0.0 1.4 %copy-start = (s32[16,128]{1,0:T(8,128)S(1)}, s32[16,128]{1,0:T(8,128)}, u32[]{:S(2)}) copy-start(s32[16,128]{1,0:T(8,128)} %param.11) | copy-start | bytes 24580
  1.4 0.7 %copy-start.2 = (bf16[1,1,1024]{2,1,0:T(2,128)(2,1)S(1)}, bf16[1,1,1024]{2,1,0:T(2,128)(2,1)}, u32[]{:S(2)}) copy-start(bf16[1,1,1024]{2,1,0:T(2,128)(2,1)} %param.9) | copy-start | bytes 6148
  1.4 0.7 %copy-start.1 = (f32[1,1,1024]{2,1,0:T(1,128)S(1)}, f32[1,1,1024]{2,1,0:T(1,128)}, u32[]{:S(2)}) copy-start(f32[1,1,1024]{2,1,0:T(1,128)} %param.10) | copy-start | bytes 12292
  3.6 7.5 %collective-permute-start = (bf16[144,256]{1,0:T(8,128)(2,1)S(1)}, bf16[144,256]{1,0:T(8,128)(2,1)S(1)}, u32[]{:S(2)}, u32[]{:S(2)}) collective-permute-start(bf16[144,256]{1,0:T(8,128)(2,1)S(1)} %get-tuple-element.26), channel_id=1, source_target_pairs={{0,16},{16,0},{32,48},{48,32},{64,80},{80,64},{96,112},{112,96},{1... | collective-permute-start | bytes 221192 | tf_op jit(solution)/shard_map/ppermute | solution.py:532
  3.7 7.6 %collective-permute-start.1 = (bf16[144,256]{1,0:T(8,128)(2,1)S(1)}, bf16[144,256]{1,0:T(8,128)(2,1)S(1)}, u32[]{:S(2)}, u32[]{:S(2)}) collective-permute-start(bf16[144,256]{1,0:T(8,128)(2,1)S(1)} %get-tuple-element.27), channel_id=1, source_target_pairs={{16,32},{32,16},{48,64},{64,48},{80,96},{96,80},{112,128},{128,112... | collective-permute-start | bytes 221192 | tf_op jit(solution)/shard_map/ppermute | solution.py:533
  13.4 8.4 %collective-permute-start.2 = (bf16[864,128]{1,0:T(8,128)(2,1)S(1)}, bf16[864,128]{1,0:T(8,128)(2,1)S(1)}, u32[]{:S(2)}, u32[]{:S(2)}) collective-permute-start(bf16[864,128]{1,0:T(8,128)(2,1)S(1)} %get-tuple-element.29), channel_id=1, source_target_pairs={{0,1},{1,0},{2,3},{3,2},{4,5},{5,4},{6,7},{7,6},{8,9},{9,8},{10,11... | collective-permute-start | bytes 663560 | tf_op jit(solution)/shard_map/ppermute | solution.py:532
  14.8 9.9 %collective-permute-start.3 = (bf16[864,128]{1,0:T(8,128)(2,1)S(1)}, bf16[864,128]{1,0:T(8,128)(2,1)S(1)}, u32[]{:S(2)}, u32[]{:S(2)}) collective-permute-start(bf16[864,128]{1,0:T(8,128)(2,1)S(1)} %get-tuple-element.30), channel_id=1, source_target_pairs={{1,2},{2,1},{3,4},{4,3},{5,6},{6,5},{7,8},{8,7},{9,10},{10,9},{11,... | collective-permute-start | bytes 663560 | tf_op jit(solution)/shard_map/ppermute | solution.py:533

commit v4 on v3

--- a/solution.py
+++ b/solution.py
@@ -54,11 +54,11 @@
 
 
 def stencil_rows(first):
-    cell = first + lax.broadcasted_iota(jnp.int32, (COLS, CELLS), 0)
+    cell = (first & (CELLS - 1)) + lax.broadcasted_iota(jnp.int32, (COLS, CELLS), 0)
     lane = lax.broadcasted_iota(jnp.int32, (COLS, CELLS), 1)
-    side = first // CELLS - 1
-    near = jnp.abs(((cell & (CELLS - 1)) >> 4) - (lane >> 4)) <= 1
-    beside = jnp.abs(side * PATCH + (cell & (PATCH - 1)) - (lane & (PATCH - 1))) <= 1
+    near = jnp.abs((cell >> 4) - (lane >> 4)) <= 1
+    apart = jnp.abs((cell & (PATCH - 1)) - (lane & (PATCH - 1)))
+    beside = apart <= 1 if first < CELLS else apart == PATCH - 1
     return jnp.where(near & beside, 1.0, 0.0).astype(BF16)
 
 
@@ -124,14 +124,15 @@
             out_ref[pl.ds(m * 16, 16), pl.ds(b * CELLS, CELLS)] = both
 
 
-def strip_kernel(background_ref, pack_ref, held, even_ref, odd_ref, tails_ref, mask_ref, lines, sems):
+def strip_kernel(background_ref, pack_ref, value_ref, err_ref,
+                 held, even_ref, odd_ref, tails_ref, mask_ref, lines, sems):
     lon_odd = (lax.axis_index("lon") & 1) == 1
     copies = fetch_field(background_ref, 0, held, sems)
-    slots = (pack_ref.shape[1] - (ROWS + 1) * COLS) // 3
+    slots = value_ref.shape[1]
     halves = []
     for g in range(2):
         rows = [
-            jnp.broadcast_to(pack_ref[:, pl.ds(3 * slots + (g * 8 + r) * COLS, COLS)], (8, COLS))
+            jnp.broadcast_to(pack_ref[:, pl.ds(slots + (g * 8 + r) * COLS, COLS)].astype(F32), (8, COLS))
             for r in range(8)
         ]
         halves.append(swap_groups(rows))
@@ -140,12 +141,12 @@
     for b in range(PATCHES):
         mask = jnp.where(which == b, jnp.concatenate([halves[0][b], halves[1][b]], axis=1), mask)
     mask_ref[...] = mask
-    cell = pack_ref[:, pl.ds(0, slots)].astype(jnp.int32)
-    count = pack_ref[:, pl.ds(3 * slots + ROWS * COLS, COLS)][:, 0:1].astype(jnp.int32)
+    cell = pack_ref[:, pl.ds(0, slots)]
+    count = pack_ref[:, pl.ds(slots + ROWS * COLS, COLS)][:, 0:1]
     used = lax.broadcasted_iota(jnp.int32, (1, slots), 1) < count
-    err = pack_ref[:, pl.ds(2 * slots, slots)]
+    err = err_ref[...]
     inverse = jnp.where(used, 1.0 / (err * err), 0.0)
-    value = jnp.where(used, pack_ref[:, pl.ds(slots, slots)], 0.0)
+    value = jnp.where(used, value_ref[...].astype(F32), 0.0)
     column = cell & (COLS - 1)
     block = column >> 4
     place = ((cell >> 7) << 4) + (column & (PATCH - 1))
@@ -185,7 +186,7 @@
 
 
 def block_kernel(held, tails_ref, blocks_ref, table_ref, lines):
-    for first in range(0, 3 * CELLS, COLS):
+    for first in range(0, 2 * CELLS, COLS):
         table_ref[pl.ds(first, COLS), :] = stencil_rows(first)
     widen_lines((), held, lines)
     to_blocks(lines, blocks_ref)
@@ -196,10 +197,10 @@
     return pltpu.roll(piece, lanes % COLS, 1) if lanes % COLS else piece
 
 
-def quarters(pieces, offset, lane):
-    tile = shift(pieces[0], -offset)
+def quarters(pieces, lane):
+    tile = pieces[0]
     for q in range(1, len(pieces)):
-        tile = jnp.where((lane >> 5) == q, shift(pieces[q], 32 * q - offset), tile)
+        tile = jnp.where((lane >> 5) == q, shift(pieces[q], 32 * q), tile)
     return tile
 
 
@@ -215,9 +216,13 @@
     wide[:, pl.ds(span + 2 * CELLS, CELLS)] = jnp.where(lon_odd, two, one)
 
     tail_row = lax.broadcasted_iota(jnp.int32, (EXTRA, CELLS), 0)
+    column = lax.broadcasted_iota(jnp.int32, (MEMBERS, CELLS), 1) & (PATCH - 1)
+    rows = pl.ds(0, MEMBERS)
     for e in range(PATCHES + 2):
+        left, own, right = (wide[rows, pl.ds((e + k) * CELLS, CELLS)] for k in range(3))
+        beside = jnp.where(column == PATCH - 1, left, jnp.where(column == 0, right, jnp.zeros_like(own)))
         summed = jnp.dot(
-            wide[pl.ds(0, MEMBERS), pl.ds(e * CELLS, 3 * CELLS)], table_ref[...], preferred_element_type=F32
+            jnp.concatenate([own, beside], axis=1), table_ref[...], preferred_element_type=F32
         )
         mean = summed * (1.0 / 9.0)
         average = jnp.sum(mean, axis=0, keepdims=True) * (1.0 / MEMBERS)
@@ -228,48 +233,48 @@
             tail_row == 0, innovation, jnp.where(tail_row == 1, tail[0:1], 0.0)
         ).astype(BF16)
 
+    write_message(pert, wide, even_ref, lat_odd)
+    write_message(pert, wide, odd_ref, jnp.logical_not(lat_odd))
+
+
+def write_message(pert, wide, out_ref, upward):
     lane = lax.broadcasted_iota(jnp.int32, (MEMBERS, COLS), 1)
     tail_lane = lax.broadcasted_iota(jnp.int32, (EXTRA, COLS), 1)
-    rims, rim_tails = [], []
-    for part, offset in ((0, 0), (1, COLS - 32)):
-        tiles, tails = [], []
-        for t in range(3):
-            some = range(4 * t, min(4 * t + 4, PATCHES + 2))
-            places = [pl.ds((e + 1) * CELLS + part * COLS, COLS) for e in some]
-            tiles.append(quarters([wide[pl.ds(0, MEMBERS), place] for place in places], offset, lane))
-            tail = [wide[pl.ds(MEMBERS, EXTRA), place].astype(F32) for place in places]
-            tails.append(quarters(tail, offset, tail_lane)[0:2])
-        half = MEMBERS // 2
-        tiles[2] = jnp.where(lane[:half] < 64, tiles[2][:half], shift(tiles[2][half:], 64))
-        rims.append(tiles)
-        rim_tails.append(jnp.concatenate(tails + [jnp.zeros((EXTRA - 6, COLS), F32)], axis=0).astype(BF16))
+
+    def near_rows(rows, e):
+        first, last = (wide[rows, pl.ds((e + 1) * CELLS + part * COLS, COLS)] for part in range(2))
+        return jnp.where(upward, first, shift(last, 32))
+
+    tiles, tails = [], []
+    for t in range(3):
+        some = range(4 * t, min(4 * t + 4, PATCHES + 2))
+        tiles.append(quarters([near_rows(pl.ds(0, MEMBERS), e) for e in some], lane))
+        tail = [near_rows(pl.ds(MEMBERS, EXTRA), e).astype(F32) for e in some]
+        tails.append(quarters(tail, tail_lane)[0:2])
+    half = MEMBERS // 2
+    tiles[2] = jnp.where(lane[:half] < 64, tiles[2][:half], shift(tiles[2][half:], 64))
+    tiles.append(jnp.concatenate(tails + [jnp.zeros((EXTRA - 6, COLS), F32)], axis=0).astype(BF16))
     start = RIMS
-    for t in range(3):
-        size = rims[0][t].shape[0]
-        even_ref[pl.ds(start, size), :] = jnp.where(lat_odd, rims[0][t], rims[1][t])
-        odd_ref[pl.ds(start, size), :] = jnp.where(lat_odd, rims[1][t], rims[0][t])
-        start += size
-    even_ref[pl.ds(start, EXTRA), :] = jnp.where(lat_odd, rim_tails[0], rim_tails[1])
-    odd_ref[pl.ds(start, EXTRA), :] = jnp.where(lat_odd, rim_tails[1], rim_tails[0])
+    for tile in tiles:
+        out_ref[pl.ds(start, tile.shape[0]), :] = tile
+        start += tile.shape[0]
 
     r = lax.broadcasted_iota(jnp.int32, (MEMBERS, MEMBERS), 0)
     c = lax.broadcasted_iota(jnp.int32, (MEMBERS, MEMBERS), 1)
     lower = r >= c
     same = r == c
-    base = (PATCHES // 2) * MEMBERS
     above, _, below = tapers()
-    for out_ref, near, far in ((even_ref, above, below), (odd_ref, below, above)):
-        taper = jnp.where(lat_odd, near, far)
-        forcings, diagonals = [], []
-        for pair in range(PATCHES // 2):
-            first, forcing = patch_gram(pert, window_of(2 * pair), taper, same)
-            forcings.append(forcing)
-            second, forcing = patch_gram(pert, window_of(2 * pair + 1), taper, same)
-            forcings.append(forcing)
-            diagonals.append(jnp.sum(jnp.where(same, second, 0.0), axis=0, keepdims=True))
-            out_ref[pl.ds(pair * MEMBERS, MEMBERS), :] = jnp.where(lower, first, second).astype(BF16)
-        tail = forcings + diagonals + [jnp.zeros((4, MEMBERS), F32)]
-        out_ref[pl.ds(base, 16), :] = jnp.concatenate(tail, axis=0).astype(BF16)
+    taper = jnp.where(upward, above, below)
+    forcings, diagonals = [], []
+    for pair in range(PATCHES // 2):
+        first, forcing = patch_gram(pert, window_of(2 * pair), taper, same)
+        forcings.append(forcing)
+        second, forcing = patch_gram(pert, window_of(2 * pair + 1), taper, same)
+        forcings.append(forcing)
+        diagonals.append(jnp.sum(jnp.where(same, second, 0.0), axis=0, keepdims=True))
+        out_ref[pl.ds(pair * MEMBERS, MEMBERS), :] = jnp.where(lower, first, second).astype(BF16)
+    tail = forcings + diagonals + [jnp.zeros((4, MEMBERS), F32)]
+    out_ref[pl.ds((PATCHES // 2) * MEMBERS, 16), :] = jnp.concatenate(tail, axis=0).astype(BF16)
 
 
 def patch_gram(pert, lanes, taper, same):
@@ -422,6 +427,11 @@
     base = (PATCHES // 2) * MEMBERS
     tail = first_ref[pl.ds(base, 16), :].astype(F32) + second_ref[pl.ds(base, 16), :].astype(F32)
     norms, rim_forcings = [], []
+    for p in range(PATCHES):
+        lanes = pl.ds(p // 2 * COLS, 2 * COLS)
+        rim_gram, rim_forcing = patch_gram(pert, lanes, rim_taper(p % 2), r == c)
+        rim_forcings.append(rim_forcing)
+        spread[0, :, pl.ds(p * MEMBERS, MEMBERS)] = rim_gram
     for pair in range(PATCHES // 2):
         rows = pl.ds(pair * MEMBERS, MEMBERS)
         mixed = first_ref[rows, :].astype(F32) + second_ref[rows, :].astype(F32)
@@ -433,10 +443,7 @@
         )
         for k in range(2):
             p = 2 * pair + k
-            lanes = pl.ds((p - k) // 2 * COLS, 2 * COLS)
-            rim_gram, rim_forcing = patch_gram(pert, lanes, rim_taper(k), r == c)
-            rim_forcings.append(rim_forcing)
-            system = gram_ref[p] + gains[k] + rim_gram
+            system = gram_ref[p] + gains[k] + spread[0, :, pl.ds(p * MEMBERS, MEMBERS)]
             total = jnp.sum(jnp.sum(system * system, axis=0, keepdims=True), axis=1, keepdims=True)
             norm = jnp.sqrt(total)
             norms.append(norm)
@@ -541,9 +548,9 @@
     field = pltpu.VMEM((MEMBERS, ROWS, COLS), BF16)
     lines_shape = (MEMBERS * ROWS, COLS)
     copies = pltpu.SemaphoreType.DMA
-    parts = [array.reshape(1, -1).astype(F32) for array in (obs_cell, obs_value, obs_err, land, obs_count)]
-    room = 3 * slots + (ROWS + 1) * COLS
-    pack, start = 0.0, 0
+    parts = [array.reshape(1, -1) for array in (obs_cell, land, obs_count)]
+    room = slots + (ROWS + 1) * COLS
+    pack, start = 0, 0
     for part in parts:
         pack = pack + jnp.pad(part, ((0, 0), (start, room - start - part.shape[1])))
         start += part.shape[1]
@@ -558,13 +565,13 @@
         ],
         [pltpu.VMEM(lines_shape, F32), copies((PARTS,))],
         10**7, 2 * 10**6,
-        background, pack,
+        background, pack, obs_value.reshape(1, slots), obs_err.reshape(1, slots),
         far=(0,),
     )
     neighbours = exchange(even, odd, "lon", True)
     blocks, table = call(
         block_kernel,
-        [shape((CHANNELS, span), BF16), shape((3 * CELLS, CELLS), BF16)],
+        [shape((CHANNELS, span), BF16), shape((2 * CELLS, CELLS), BF16)],
         [pltpu.VMEM(lines_shape, F32)],
         10**8, 4 * 10**6,
         held, tails,

time: 32.9 us -> 30.8 us (0.936)
  Pallas kernels: 17 us -> 15.3 us
  local copies, waits for them, and re-layouts: 0.69 us -> 0.03 us
    pallas_call x5, Pallas kernels: 17 us -> 15.3 us  [call(): pl.pallas_call(kernel, out_shape=out_shape, in_specs=[anywhere if i in fa...]
    add x1, other arithmetic: 0.01 us -> 0.72 us  [body(): pack = pack + jnp.pad(part, ((0, 0), (start, room - start - part.shape[1])))]
    convert_element_type x2 -> x0, other arithmetic: 0.69 us -> none  [body(): array.reshape(1, -1).astype(F32)]
    unnamed x6, local copies, waits for them, and re-layouts: 0.69 us -> 0.03 us
  transfers between devices with their start and end apart: 4 -> 4, of which waited for: 3 -> 3; matrix products, arithmetic and copies ran while one was open for 0% -> 0% of each run, Pallas kernels for 17% -> 18%
where the time goes in v4:
time: 30.8 us; the launch traced here: 30.6 us
  Pallas kernels  15.3 us (50%)
  starting transfers between devices  9.41 us (31%)
  waiting for transfers between devices  4.17 us (14%)
  between operations  0.89 us (3%)
  other arithmetic  0.72 us (2%)
    pallas_call x5, Pallas kernels, call(): pl.pallas_call(kernel, out_shape=out_shape, in_specs=[anywhere if i in fa...  15.3 us
    ppermute x2, starting transfers between devices, exchange(): lax.ppermute(odd, axis, pairs_across(size, wrap))  7.86 us
    ppermute x2, waiting for transfers between devices, exchange(): lax.ppermute(odd, axis, pairs_across(size, wrap))  3.36 us
    ppermute x2, starting transfers between devices, exchange(): lax.ppermute(even, axis, pairs_inside(size))  1.55 us
    ppermute x2, waiting for transfers between devices, exchange(): lax.ppermute(even, axis, pairs_inside(size))  0.81 us
    add x1, other arithmetic, body(): pack = pack + jnp.pad(part, ((0, 0), (start, room - start - part.shape[1])))  0.72 us
  transfers between devices with their start and end apart: 4, of which 3 were waited for; matrix products, arithmetic and copies ran while one was open for 0% of the time, Pallas kernels for 18%

profile of v4, /device:TPU:128, one launch (start us, length us, event | category | flops | bytes accessed | tf_op | source)
XLA Modules:
  0.0 30.6 jit_solution(4016085107134188436)
XLA Ops:
  0.0 0.0 copy-start.2
  0.7 0.0 copy-done.2
  0.7 0.0 copy-start
  0.7 0.0 copy-start.1
  0.7 0.7 %pad_add_fusion.pack_ref = s32[1,3200]{1,0:T(1,128)S(1)} fusion(s32[1,1]{1,0:T(1,128)S(6)} %copy.7, s32[1,2048]{1,0:T(1,128)} %bitcast.6, s32[1,1024]{1,0:T(1,128)S(1)} %bitcast.7), kind=kLoop, calls=%fused_computation | loop fusion | flops 6400 | bytes 25092 | tf_op jit(solution)/shard_map/add | solution.py:555
  1.4 0.0 copy-done
  1.4 0.0 copy-done.1
  1.4 1.6 %shard_map.64 = (bf16[128,16,128]{2,1,0:T(8,128)(2,1)S(1)}, bf16[144,256]{1,0:T(8,128)(2,1)S(1)}, bf16[144,256]{1,0:T(8,128)(2,1)S(1)}, bf16[16,2048]{1,0:T(8,128)(2,1)S(1)}, f32[8,256]{1,0:T(8,128)S(1)}) custom-call(bf16[2,128,16,128]{3,2,1,0:T(8,128)(2,1)} %background_ref.3, s32[1,3200]{1,0:T(1,128)S(1)} %pad_add_fusion.pack_ref, ...), custom_call_target="tpu_custom_call" | custom-call | flops 10000000 | bytes 2000000 | tf_op jit(solution)/shard_map/pallas_call | solution.py:510
  3.0 0.1 collective-permute-start
  3.1 5.6 %collective-permute-start.1 = (bf16[144,256]{1,0:T(8,128)(2,1)S(1)}, bf16[144,256]{1,0:T(8,128)(2,1)S(1)}, u32[]{:S(2)}, u32[]{:S(2)}) collective-permute-start(bf16[144,256]{1,0:T(8,128)(2,1)S(1)} %get-tuple-element.27), channel_id=1, source_target_pairs={{16,32},{32,16},{48,64},{64,48},{80,96},{96,80},{112,128},{128,112... | collective-permute-start | bytes 221192 | tf_op jit(solution)/shard_map/ppermute | solution.py:540
  8.7 1.6 %shard_map.65 = (bf16[144,2048]{1,0:T(8,128)(2,1)S(1)}, bf16[512,256]{1,0:T(8,128)(2,1)S(1)}) custom-call(bf16[128,16,128]{2,1,0:T(8,128)(2,1)S(1)} %get-tuple-element.23.held, bf16[16,2048]{1,0:T(8,128)(2,1)S(1)} %get-tuple-element.24.tails_ref), custom_call_target="tpu_custom_call" | custom-call | flops 100000000 | bytes 4000000 | tf_op jit(solution)/shard_map/pallas_call | solution.py:510
  10.3 0.0 collective-permute-done.first_ref
  10.3 0.4 %collective-permute-done.1.second_ref = bf16[144,256]{1,0:T(8,128)(2,1)S(1)} collective-permute-done((bf16[144,256]{1,0:T(8,128)(2,1)S(1)}, bf16[144,256]{1,0:T(8,128)(2,1)S(1)}, u32[]{:S(2)}, u32[]{:S(2)}) %collective-permute-start.1) | collective-permute-done | bytes 73760 | tf_op jit(solution)/shard_map/ppermute | solution.py:540
  10.7 2.1 %shard_map.66 = (bf16[864,128]{1,0:T(8,128)(2,1)S(1)}, bf16[864,128]{1,0:T(8,128)(2,1)S(1)}, bf16[144,2560]{1,0:T(8,128)(2,1)S(1)}, bf16[144,3072]{1,0:T(8,128)(2,1)S(1)}) custom-call(bf16[144,2048]{1,0:T(8,128)(2,1)S(1)} %get-tuple-element.25.blocks_ref, bf16[144,256]{1,0:T(8,128)(2,1)S(1)} %collective-permute-done.first_ref, ...), custom_call_target="tpu_custom_call" | custom-call | flops 1000000000 | bytes 3000000 | tf_op jit(solution)/shard_map/pallas_call | solution.py:510
  12.8 1.5 %collective-permute-start.2 = (bf16[864,128]{1,0:T(8,128)(2,1)S(1)}, bf16[864,128]{1,0:T(8,128)(2,1)S(1)}, u32[]{:S(2)}, u32[]{:S(2)}) collective-permute-start(bf16[864,128]{1,0:T(8,128)(2,1)S(1)} %get-tuple-element.29), channel_id=1, source_target_pairs={{0,1},{1,0},{2,3},{3,2},{4,5},{5,4},{6,7},{7,6},{8,9},{9,8},{10,11... | collective-permute-start | bytes 663560 | tf_op jit(solution)/shard_map/ppermute | solution.py:539
  14.3 2.3 %collective-permute-start.3 = (bf16[864,128]{1,0:T(8,128)(2,1)S(1)}, bf16[864,128]{1,0:T(8,128)(2,1)S(1)}, u32[]{:S(2)}, u32[]{:S(2)}) collective-permute-start(bf16[864,128]{1,0:T(8,128)(2,1)S(1)} %get-tuple-element.30), channel_id=1, source_target_pairs={{1,2},{2,1},{3,4},{4,3},{5,6},{6,5},{7,8},{8,7},{9,10},{10,9},{11,... | collective-permute-start | bytes 663560 | tf_op jit(solution)/shard_map/ppermute | solution.py:540
  16.6 3.8 %shard_map.67 = (f32[8,128,128]{2,1,0:T(8,128)S(1)}, f32[8,128]{1,0:T(8,128)S(1)}, bf16[128,4096]{1,0:T(8,128)(2,1)S(1)}, bf16[128,4096]{1,0:T(8,128)(2,1)S(1)},...) custom-call(bf16[144,2560]{1,0:T(8,128)(2,1)S(1)} %get-tuple-element.31.pert, ...), custom_call_target="tpu_custom_call" | custom-call | flops 1000000000 | bytes 5000000 | tf_op jit(solution)/shard_map/pallas_call | solution.py:510
  20.4 0.8 %collective-permute-done.2.first_ref = bf16[864,128]{1,0:T(8,128)(2,1)S(1)} collective-permute-done((bf16[864,128]{1,0:T(8,128)(2,1)S(1)}, bf16[864,128]{1,0:T(8,128)(2,1)S(1)}, u32[]{:S(2)}, u32[]{:S(2)}) %collective-permute-start.2) | collective-permute-done | bytes 221216 | tf_op jit(solution)/shard_map/ppermute | solution.py:539
  21.2 3.0 %collective-permute-done.3.second_ref = bf16[864,128]{1,0:T(8,128)(2,1)S(1)} collective-permute-done((bf16[864,128]{1,0:T(8,128)(2,1)S(1)}, bf16[864,128]{1,0:T(8,128)(2,1)S(1)}, u32[]{:S(2)}, u32[]{:S(2)}) %collective-permute-start.3) | collective-permute-done | bytes 221216 | tf_op jit(solution)/shard_map/ppermute | solution.py:540
  24.2 6.2 %shard_map.68 = bf16[2,128,16,128]{3,2,1,0:T(8,128)(2,1)} custom-call(bf16[864,128]{1,0:T(8,128)(2,1)S(1)} %collective-permute-done.2.first_ref, bf16[864,128]{1,0:T(8,128)(2,1)S(1)} %collective-permute-done.3.second_ref, f32[8,128,128]{2,1,0:T(8,128)S(1)} %get-tuple-element.34.gram_ref, f32[8,128]{1,0:T(8,128)S(1)} %get-tuple-element.35.force_ref, ...), custom_call_target="tpu_custom_call" | custom-call | flops 2000000000 | bytes 5000000 | tf_op jit(solution)/shard_map/pallas_call | solution.py:510
Async XLA Ops:
  0.0 0.7 %copy-start.2 = (s32[1,1,1024]{2,1,0:T(1,128)S(1)}, s32[1,1,1024]{2,1,0:T(1,128)}, u32[]{:S(2)}) copy-start(s32[1,1,1024]{2,1,0:T(1,128)} %param.7) | copy-start | bytes 12292
  0.7 0.7 %copy-start = (bf16[1,1,1024]{2,1,0:T(2,128)(2,1)S(1)}, bf16[1,1,1024]{2,1,0:T(2,128)(2,1)}, u32[]{:S(2)}) copy-start(bf16[1,1,1024]{2,1,0:T(2,128)(2,1)} %param.9) | copy-start | bytes 6148
  0.7 0.7 %copy-start.1 = (f32[1,1,1024]{2,1,0:T(1,128)S(1)}, f32[1,1,1024]{2,1,0:T(1,128)}, u32[]{:S(2)}) copy-start(f32[1,1,1024]{2,1,0:T(1,128)} %param.10) | copy-start | bytes 12292
  3.0 7.3 %collective-permute-start = (bf16[144,256]{1,0:T(8,128)(2,1)S(1)}, bf16[144,256]{1,0:T(8,128)(2,1)S(1)}, u32[]{:S(2)}, u32[]{:S(2)}) collective-permute-start(bf16[144,256]{1,0:T(8,128)(2,1)S(1)} %get-tuple-element.26), channel_id=1, source_target_pairs={{0,16},{16,0},{32,48},{48,32},{64,80},{80,64},{96,112},{112,96},{1... | collective-permute-start | bytes 221192 | tf_op jit(solution)/shard_map/ppermute | solution.py:539
  3.1 7.6 %collective-permute-start.1 = (bf16[144,256]{1,0:T(8,128)(2,1)S(1)}, bf16[144,256]{1,0:T(8,128)(2,1)S(1)}, u32[]{:S(2)}, u32[]{:S(2)}) collective-permute-start(bf16[144,256]{1,0:T(8,128)(2,1)S(1)} %get-tuple-element.27), channel_id=1, source_target_pairs={{16,32},{32,16},{48,64},{64,48},{80,96},{96,80},{112,128},{128,112... | collective-permute-start | bytes 221192 | tf_op jit(solution)/shard_map/ppermute | solution.py:540
  12.8 8.4 %collective-permute-start.2 = (bf16[864,128]{1,0:T(8,128)(2,1)S(1)}, bf16[864,128]{1,0:T(8,128)(2,1)S(1)}, u32[]{:S(2)}, u32[]{:S(2)}) collective-permute-start(bf16[864,128]{1,0:T(8,128)(2,1)S(1)} %get-tuple-element.29), channel_id=1, source_target_pairs={{0,1},{1,0},{2,3},{3,2},{4,5},{5,4},{6,7},{7,6},{8,9},{9,8},{10,11... | collective-permute-start | bytes 663560 | tf_op jit(solution)/shard_map/ppermute | solution.py:539
  14.3 9.9 %collective-permute-start.3 = (bf16[864,128]{1,0:T(8,128)(2,1)S(1)}, bf16[864,128]{1,0:T(8,128)(2,1)S(1)}, u32[]{:S(2)}, u32[]{:S(2)}) collective-permute-start(bf16[864,128]{1,0:T(8,128)(2,1)S(1)} %get-tuple-element.30), channel_id=1, source_target_pairs={{1,2},{2,1},{3,4},{4,3},{5,6},{6,5},{7,8},{8,7},{9,10},{10,9},{11,... | collective-permute-start | bytes 663560 | tf_op jit(solution)/shard_map/ppermute | solution.py:540

commit v5 on v4

--- a/solution.py
+++ b/solution.py
@@ -85,6 +85,22 @@
                 mixed[i + step] = jnp.where(high, second, pltpu.roll(first, COLS - width, 1))
         arrays = mixed
     return arrays
+
+
+def shift(piece, lanes):
+    return pltpu.roll(piece, lanes % COLS, 1) if lanes % COLS else piece
+
+
+def turn_groups(block, p):
+    return jnp.concatenate([shift(block[:, :COLS], PATCH * p), shift(block[:, COLS:], PATCH * p)], axis=1)
+
+
+def turned_lines(arrays):
+    group = lax.broadcasted_iota(jnp.int32, arrays[0].shape, 1) >> 4
+    for step in (1, 2, 4):
+        odd = (group & step) != 0
+        arrays = [jnp.where(odd, arrays[(i + step) % 8], arrays[i]) for i in range(8)]
+    return [shift(arrays[-r % 8], -PATCH * r) for r in range(8)]
 
 
 def fetch(source, target, sem):
@@ -193,10 +209,6 @@
     blocks_ref[pl.ds(MEMBERS, EXTRA), :] = tails_ref[...]
 
 
-def shift(piece, lanes):
-    return pltpu.roll(piece, lanes % COLS, 1) if lanes % COLS else piece
-
-
 def quarters(pieces, lane):
     tile = pieces[0]
     for q in range(1, len(pieces)):
@@ -321,9 +333,10 @@
             mean = jnp.sum(raw, axis=0, keepdims=True) * (1.0 / MEMBERS)
             place = pl.ds((2 * p + v) * CELLS, CELLS)
             coarse = mean.astype(BF16).astype(F32)
-            departure_ref[:, place] = jnp.where(land, raw - mean, 0.0).astype(BF16)
-            base_ref[:, place] = jnp.where(land, coarse, raw).astype(BF16)
-            rest_ref[:, place] = jnp.broadcast_to(jnp.where(land, mean - coarse, 0.0), (8, CELLS))
+            departure_ref[:, place] = turn_groups(jnp.where(land, raw - mean, 0.0).astype(BF16), p)
+            base_ref[:, place] = turn_groups(jnp.where(land, coarse, raw).astype(BF16), p)
+            rest = jnp.broadcast_to(jnp.where(land, mean - coarse, 0.0), (8, CELLS))
+            rest_ref[:, place] = turn_groups(rest, p)
 
 
 def split(a):
@@ -489,7 +502,7 @@
         for m in range(MEMBERS // 16):
             rows = pl.ds(m * 16, 16)
             for g in range(2):
-                lines = swap_groups(
+                lines = turned_lines(
                     [spread[v, rows, pl.ds(b * CELLS + g * COLS, COLS)] for b in range(PATCHES)]
                 )
                 for k in range(8):

time: 30.8 us -> 29.8 us (0.968)
  the two profiles are of different devices: /device:TPU:128 before, /device:TPU:102 now
where the time goes in v5:
time: 29.8 us; the launch traced here: 29.3 us
  Pallas kernels  15.3 us (51%)
  starting transfers between devices  10.6 us (36%)
  waiting for transfers between devices  1.87 us (6%)
  between operations  0.75 us (3%)
  other arithmetic  0.72 us (2%)
    pallas_call x5, Pallas kernels, call(): pl.pallas_call(kernel, out_shape=out_shape, in_specs=[anywhere if i in fa...  15.3 us
    ppermute x2, starting transfers between devices, exchange(): lax.ppermute(odd, axis, pairs_across(size, wrap))  9.62 us
    ppermute x2, waiting for transfers between devices, exchange(): lax.ppermute(odd, axis, pairs_across(size, wrap))  1.86 us
    ppermute x2, starting transfers between devices, exchange(): lax.ppermute(even, axis, pairs_inside(size))  1 us
    add x1, other arithmetic, body(): pack = pack + jnp.pad(part, ((0, 0), (start, room - start - part.shape[1])))  0.72 us
  transfers between devices with their start and end apart: 4, of which 1 were waited for; matrix products, arithmetic and copies ran while one was open for 0% of the time, Pallas kernels for 21%

profile of v5, /device:TPU:102, one launch (start us, length us, event | category | flops | bytes accessed | tf_op | source)
XLA Modules:
  0.0 29.3 jit_solution(2519571173358968221)
XLA Ops:
  0.0 0.0 copy-start.2
  0.7 0.0 copy-done.2
  0.7 0.0 copy-start
  0.7 0.0 copy-start.1
  0.7 0.7 %pad_add_fusion.pack_ref = s32[1,3200]{1,0:T(1,128)S(1)} fusion(s32[1,1]{1,0:T(1,128)S(6)} %copy.7, s32[1,2048]{1,0:T(1,128)} %bitcast.6, s32[1,1024]{1,0:T(1,128)S(1)} %bitcast.7), kind=kLoop, calls=%fused_computation | loop fusion | flops 6400 | bytes 25092 | tf_op jit(solution)/shard_map/add | solution.py:568
  1.4 0.0 copy-done
  1.4 0.0 copy-done.1
  1.4 1.6 %shard_map.64 = (bf16[128,16,128]{2,1,0:T(8,128)(2,1)S(1)}, bf16[144,256]{1,0:T(8,128)(2,1)S(1)}, bf16[144,256]{1,0:T(8,128)(2,1)S(1)}, bf16[16,2048]{1,0:T(8,128)(2,1)S(1)}, f32[8,256]{1,0:T(8,128)S(1)}) custom-call(bf16[2,128,16,128]{3,2,1,0:T(8,128)(2,1)} %background_ref.3, s32[1,3200]{1,0:T(1,128)S(1)} %pad_add_fusion.pack_ref, ...), custom_call_target="tpu_custom_call" | custom-call | flops 10000000 | bytes 2000000 | tf_op jit(solution)/shard_map/pallas_call | solution.py:523
  3.0 0.1 collective-permute-start
  3.1 4.0 %collective-permute-start.1 = (bf16[144,256]{1,0:T(8,128)(2,1)S(1)}, bf16[144,256]{1,0:T(8,128)(2,1)S(1)}, u32[]{:S(2)}, u32[]{:S(2)}) collective-permute-start(bf16[144,256]{1,0:T(8,128)(2,1)S(1)} %get-tuple-element.27), channel_id=1, source_target_pairs={{16,32},{32,16},{48,64},{64,48},{80,96},{96,80},{112,128},{128,112... | collective-permute-start | bytes 221192 | tf_op jit(solution)/shard_map/ppermute | solution.py:553
  7.1 1.6 %shard_map.65 = (bf16[144,2048]{1,0:T(8,128)(2,1)S(1)}, bf16[512,256]{1,0:T(8,128)(2,1)S(1)}) custom-call(bf16[128,16,128]{2,1,0:T(8,128)(2,1)S(1)} %get-tuple-element.23.held, bf16[16,2048]{1,0:T(8,128)(2,1)S(1)} %get-tuple-element.24.tails_ref), custom_call_target="tpu_custom_call" | custom-call | flops 100000000 | bytes 4000000 | tf_op jit(solution)/shard_map/pallas_call | solution.py:523
  8.7 0.0 collective-permute-done.first_ref
  8.7 1.9 %collective-permute-done.1.second_ref = bf16[144,256]{1,0:T(8,128)(2,1)S(1)} collective-permute-done((bf16[144,256]{1,0:T(8,128)(2,1)S(1)}, bf16[144,256]{1,0:T(8,128)(2,1)S(1)}, u32[]{:S(2)}, u32[]{:S(2)}) %collective-permute-start.1) | collective-permute-done | bytes 73760 | tf_op jit(solution)/shard_map/ppermute | solution.py:553
  10.6 2.1 %shard_map.66 = (bf16[864,128]{1,0:T(8,128)(2,1)S(1)}, bf16[864,128]{1,0:T(8,128)(2,1)S(1)}, bf16[144,2560]{1,0:T(8,128)(2,1)S(1)}, bf16[144,3072]{1,0:T(8,128)(2,1)S(1)}) custom-call(bf16[144,2048]{1,0:T(8,128)(2,1)S(1)} %get-tuple-element.25.blocks_ref, bf16[144,256]{1,0:T(8,128)(2,1)S(1)} %collective-permute-done.first_ref, ...), custom_call_target="tpu_custom_call" | custom-call | flops 1000000000 | bytes 3000000 | tf_op jit(solution)/shard_map/pallas_call | solution.py:523
  12.7 0.9 %collective-permute-start.2 = (bf16[864,128]{1,0:T(8,128)(2,1)S(1)}, bf16[864,128]{1,0:T(8,128)(2,1)S(1)}, u32[]{:S(2)}, u32[]{:S(2)}) collective-permute-start(bf16[864,128]{1,0:T(8,128)(2,1)S(1)} %get-tuple-element.29), channel_id=1, source_target_pairs={{0,1},{1,0},{2,3},{3,2},{4,5},{5,4},{6,7},{7,6},{8,9},{9,8},{10,11... | collective-permute-start | bytes 663560 | tf_op jit(solution)/shard_map/ppermute | solution.py:552
  13.6 5.7 %collective-permute-start.3 = (bf16[864,128]{1,0:T(8,128)(2,1)S(1)}, bf16[864,128]{1,0:T(8,128)(2,1)S(1)}, u32[]{:S(2)}, u32[]{:S(2)}) collective-permute-start(bf16[864,128]{1,0:T(8,128)(2,1)S(1)} %get-tuple-element.30), channel_id=1, source_target_pairs={{1,2},{2,1},{3,4},{4,3},{5,6},{6,5},{7,8},{8,7},{9,10},{10,9},{11,... | collective-permute-start | bytes 663560 | tf_op jit(solution)/shard_map/ppermute | solution.py:553
  19.3 4.5 %shard_map.67 = (f32[8,128,128]{2,1,0:T(8,128)S(1)}, f32[8,128]{1,0:T(8,128)S(1)}, bf16[128,4096]{1,0:T(8,128)(2,1)S(1)}, bf16[128,4096]{1,0:T(8,128)(2,1)S(1)},...) custom-call(bf16[144,2560]{1,0:T(8,128)(2,1)S(1)} %get-tuple-element.31.pert, ...), custom_call_target="tpu_custom_call" | custom-call | flops 1000000000 | bytes 5000000 | tf_op jit(solution)/shard_map/pallas_call | solution.py:523
  23.8 0.0 collective-permute-done.2.first_ref
  23.9 0.0 collective-permute-done.3.second_ref
  23.9 5.4 %shard_map.68 = bf16[2,128,16,128]{3,2,1,0:T(8,128)(2,1)} custom-call(bf16[864,128]{1,0:T(8,128)(2,1)S(1)} %collective-permute-done.2.first_ref, bf16[864,128]{1,0:T(8,128)(2,1)S(1)} %collective-permute-done.3.second_ref, f32[8,128,128]{2,1,0:T(8,128)S(1)} %get-tuple-element.34.gram_ref, f32[8,128]{1,0:T(8,128)S(1)} %get-tuple-element.35.force_ref, ...), custom_call_target="tpu_custom_call" | custom-call | flops 2000000000 | bytes 5000000 | tf_op jit(solution)/shard_map/pallas_call | solution.py:523
Async XLA Ops:
  0.0 0.7 %copy-start.2 = (s32[1,1,1024]{2,1,0:T(1,128)S(1)}, s32[1,1,1024]{2,1,0:T(1,128)}, u32[]{:S(2)}) copy-start(s32[1,1,1024]{2,1,0:T(1,128)} %param.7) | copy-start | bytes 12292
  0.7 0.7 %copy-start = (bf16[1,1,1024]{2,1,0:T(2,128)(2,1)S(1)}, bf16[1,1,1024]{2,1,0:T(2,128)(2,1)}, u32[]{:S(2)}) copy-start(bf16[1,1,1024]{2,1,0:T(2,128)(2,1)} %param.9) | copy-start | bytes 6148
  0.7 0.7 %copy-start.1 = (f32[1,1,1024]{2,1,0:T(1,128)S(1)}, f32[1,1,1024]{2,1,0:T(1,128)}, u32[]{:S(2)}) copy-start(f32[1,1,1024]{2,1,0:T(1,128)} %param.10) | copy-start | bytes 12292
  3.0 5.7 %collective-permute-start = (bf16[144,256]{1,0:T(8,128)(2,1)S(1)}, bf16[144,256]{1,0:T(8,128)(2,1)S(1)}, u32[]{:S(2)}, u32[]{:S(2)}) collective-permute-start(bf16[144,256]{1,0:T(8,128)(2,1)S(1)} %get-tuple-element.26), channel_id=1, source_target_pairs={{0,16},{16,0},{32,48},{48,32},{64,80},{80,64},{96,112},{112,96},{1... | collective-permute-start | bytes 221192 | tf_op jit(solution)/shard_map/ppermute | solution.py:552
  3.1 7.5 %collective-permute-start.1 = (bf16[144,256]{1,0:T(8,128)(2,1)S(1)}, bf16[144,256]{1,0:T(8,128)(2,1)S(1)}, u32[]{:S(2)}, u32[]{:S(2)}) collective-permute-start(bf16[144,256]{1,0:T(8,128)(2,1)S(1)} %get-tuple-element.27), channel_id=1, source_target_pairs={{16,32},{32,16},{48,64},{64,48},{80,96},{96,80},{112,128},{128,112... | collective-permute-start | bytes 221192 | tf_op jit(solution)/shard_map/ppermute | solution.py:553
  12.7 11.1 %collective-permute-start.2 = (bf16[864,128]{1,0:T(8,128)(2,1)S(1)}, bf16[864,128]{1,0:T(8,128)(2,1)S(1)}, u32[]{:S(2)}, u32[]{:S(2)}) collective-permute-start(bf16[864,128]{1,0:T(8,128)(2,1)S(1)} %get-tuple-element.29), channel_id=1, source_target_pairs={{0,1},{1,0},{2,3},{3,2},{4,5},{5,4},{6,7},{7,6},{8,9},{9,8},{10,11... | collective-permute-start | bytes 663560 | tf_op jit(solution)/shard_map/ppermute | solution.py:552
  13.6 10.2 %collective-permute-start.3 = (bf16[864,128]{1,0:T(8,128)(2,1)S(1)}, bf16[864,128]{1,0:T(8,128)(2,1)S(1)}, u32[]{:S(2)}, u32[]{:S(2)}) collective-permute-start(bf16[864,128]{1,0:T(8,128)(2,1)S(1)} %get-tuple-element.30), channel_id=1, source_target_pairs={{1,2},{2,1},{3,4},{4,3},{5,6},{6,5},{7,8},{8,7},{9,10},{10,9},{11,... | collective-permute-start | bytes 663560 | tf_op jit(solution)/shard_map/ppermute | solution.py:553

commit v6 on v5

--- a/solution.py
+++ b/solution.py
@@ -195,8 +195,10 @@
             for r in range(8):
                 row = lines[pl.ds(m * 256 + g * 8 + r, 16, stride=16), :].astype(BF16)
                 here = group == r
-                west = jnp.where(here, pltpu.roll(row, PATCH * r, 1) if r else row, west)
-                east = jnp.where(here, pltpu.roll(row, PATCH * (r + 1), 1) if r < 7 else row, east)
+                turned = shift(row, PATCH * r)
+                west = jnp.where(here, turned, west)
+                east = jnp.where(group == (r + 7) % 8, turned, east)
+            east = shift(east, PATCH)
             even_ref[pl.ds(m * 16, 16), pl.ds(g * COLS, COLS)] = jnp.where(lon_odd, west, east)
             odd_ref[pl.ds(m * 16, 16), pl.ds(g * COLS, COLS)] = jnp.where(lon_odd, east, west)
 

time: 29.8 us -> 29.9 us (level)
  no operation moved by 1% of the time
where the time goes in v6:
time: 29.9 us; the launch traced here: 29.4 us
  Pallas kernels  15.4 us (52%)
  starting transfers between devices  10.6 us (35%)
  waiting for transfers between devices  1.87 us (6%)
  between operations  0.75 us (3%)
  other arithmetic  0.72 us (2%)
    pallas_call x5, Pallas kernels, call(): pl.pallas_call(kernel, out_shape=out_shape, in_specs=[anywhere if i in fa...  15.4 us
    ppermute x2, starting transfers between devices, exchange(): lax.ppermute(odd, axis, pairs_across(size, wrap))  9.62 us
    ppermute x2, waiting for transfers between devices, exchange(): lax.ppermute(odd, axis, pairs_across(size, wrap))  1.86 us
    ppermute x2, starting transfers between devices, exchange(): lax.ppermute(even, axis, pairs_inside(size))  1.01 us
    add x1, other arithmetic, body(): pack = pack + jnp.pad(part, ((0, 0), (start, room - start - part.shape[1])))  0.72 us
  transfers between devices with their start and end apart: 4, of which 1 were waited for; matrix products, arithmetic and copies ran while one was open for 0% of the time, Pallas kernels for 21%

profile of v6, /device:TPU:102, one launch (start us, length us, event | category | flops | bytes accessed | tf_op | source)
XLA Modules:
  0.0 29.4 jit_solution(15919949902417387447)
XLA Ops:
  0.0 0.0 copy-start.2
  0.7 0.0 copy-done.2
  0.7 0.0 copy-start
  0.7 0.0 copy-start.1
  0.7 0.7 %pad_add_fusion.pack_ref = s32[1,3200]{1,0:T(1,128)S(1)} fusion(s32[1,1]{1,0:T(1,128)S(6)} %copy.7, s32[1,2048]{1,0:T(1,128)} %bitcast.6, s32[1,1024]{1,0:T(1,128)S(1)} %bitcast.7), kind=kLoop, calls=%fused_computation | loop fusion | flops 6400 | bytes 25092 | tf_op jit(solution)/shard_map/add | solution.py:570
  1.4 0.0 copy-done
  1.4 0.0 copy-done.1
  1.4 1.6 %shard_map.64 = (bf16[128,16,128]{2,1,0:T(8,128)(2,1)S(1)}, bf16[144,256]{1,0:T(8,128)(2,1)S(1)}, bf16[144,256]{1,0:T(8,128)(2,1)S(1)}, bf16[16,2048]{1,0:T(8,128)(2,1)S(1)}, f32[8,256]{1,0:T(8,128)S(1)}) custom-call(bf16[2,128,16,128]{3,2,1,0:T(8,128)(2,1)} %background_ref.3, s32[1,3200]{1,0:T(1,128)S(1)} %pad_add_fusion.pack_ref, ...), custom_call_target="tpu_custom_call" | custom-call | flops 10000000 | bytes 2000000 | tf_op jit(solution)/shard_map/pallas_call | solution.py:525
  3.1 0.1 collective-permute-start
  3.2 4.0 %collective-permute-start.1 = (bf16[144,256]{1,0:T(8,128)(2,1)S(1)}, bf16[144,256]{1,0:T(8,128)(2,1)S(1)}, u32[]{:S(2)}, u32[]{:S(2)}) collective-permute-start(bf16[144,256]{1,0:T(8,128)(2,1)S(1)} %get-tuple-element.27), channel_id=1, source_target_pairs={{16,32},{32,16},{48,64},{64,48},{80,96},{96,80},{112,128},{128,112... | collective-permute-start | bytes 221192 | tf_op jit(solution)/shard_map/ppermute | solution.py:555
  7.1 1.6 %shard_map.65 = (bf16[144,2048]{1,0:T(8,128)(2,1)S(1)}, bf16[512,256]{1,0:T(8,128)(2,1)S(1)}) custom-call(bf16[128,16,128]{2,1,0:T(8,128)(2,1)S(1)} %get-tuple-element.23.held, bf16[16,2048]{1,0:T(8,128)(2,1)S(1)} %get-tuple-element.24.tails_ref), custom_call_target="tpu_custom_call" | custom-call | flops 100000000 | bytes 4000000 | tf_op jit(solution)/shard_map/pallas_call | solution.py:525
  8.8 0.0 collective-permute-done.first_ref
  8.8 1.9 %collective-permute-done.1.second_ref = bf16[144,256]{1,0:T(8,128)(2,1)S(1)} collective-permute-done((bf16[144,256]{1,0:T(8,128)(2,1)S(1)}, bf16[144,256]{1,0:T(8,128)(2,1)S(1)}, u32[]{:S(2)}, u32[]{:S(2)}) %collective-permute-start.1) | collective-permute-done | bytes 73760 | tf_op jit(solution)/shard_map/ppermute | solution.py:555
  10.7 2.1 %shard_map.66 = (bf16[864,128]{1,0:T(8,128)(2,1)S(1)}, bf16[864,128]{1,0:T(8,128)(2,1)S(1)}, bf16[144,2560]{1,0:T(8,128)(2,1)S(1)}, bf16[144,3072]{1,0:T(8,128)(2,1)S(1)}) custom-call(bf16[144,2048]{1,0:T(8,128)(2,1)S(1)} %get-tuple-element.25.blocks_ref, bf16[144,256]{1,0:T(8,128)(2,1)S(1)} %collective-permute-done.first_ref, ...), custom_call_target="tpu_custom_call" | custom-call | flops 1000000000 | bytes 3000000 | tf_op jit(solution)/shard_map/pallas_call | solution.py:525
  12.8 0.9 %collective-permute-start.2 = (bf16[864,128]{1,0:T(8,128)(2,1)S(1)}, bf16[864,128]{1,0:T(8,128)(2,1)S(1)}, u32[]{:S(2)}, u32[]{:S(2)}) collective-permute-start(bf16[864,128]{1,0:T(8,128)(2,1)S(1)} %get-tuple-element.29), channel_id=1, source_target_pairs={{0,1},{1,0},{2,3},{3,2},{4,5},{5,4},{6,7},{7,6},{8,9},{9,8},{10,11... | collective-permute-start | bytes 663560 | tf_op jit(solution)/shard_map/ppermute | solution.py:554
  13.7 5.7 %collective-permute-start.3 = (bf16[864,128]{1,0:T(8,128)(2,1)S(1)}, bf16[864,128]{1,0:T(8,128)(2,1)S(1)}, u32[]{:S(2)}, u32[]{:S(2)}) collective-permute-start(bf16[864,128]{1,0:T(8,128)(2,1)S(1)} %get-tuple-element.30), channel_id=1, source_target_pairs={{1,2},{2,1},{3,4},{4,3},{5,6},{6,5},{7,8},{8,7},{9,10},{10,9},{11,... | collective-permute-start | bytes 663560 | tf_op jit(solution)/shard_map/ppermute | solution.py:555
  19.4 4.5 %shard_map.67 = (f32[8,128,128]{2,1,0:T(8,128)S(1)}, f32[8,128]{1,0:T(8,128)S(1)}, bf16[128,4096]{1,0:T(8,128)(2,1)S(1)}, bf16[128,4096]{1,0:T(8,128)(2,1)S(1)},...) custom-call(bf16[144,2560]{1,0:T(8,128)(2,1)S(1)} %get-tuple-element.31.pert, ...), custom_call_target="tpu_custom_call" | custom-call | flops 1000000000 | bytes 5000000 | tf_op jit(solution)/shard_map/pallas_call | solution.py:525
  23.9 0.0 collective-permute-done.2.first_ref
  23.9 0.0 collective-permute-done.3.second_ref
  23.9 5.4 %shard_map.68 = bf16[2,128,16,128]{3,2,1,0:T(8,128)(2,1)} custom-call(bf16[864,128]{1,0:T(8,128)(2,1)S(1)} %collective-permute-done.2.first_ref, bf16[864,128]{1,0:T(8,128)(2,1)S(1)} %collective-permute-done.3.second_ref, f32[8,128,128]{2,1,0:T(8,128)S(1)} %get-tuple-element.34.gram_ref, f32[8,128]{1,0:T(8,128)S(1)} %get-tuple-element.35.force_ref, ...), custom_call_target="tpu_custom_call" | custom-call | flops 2000000000 | bytes 5000000 | tf_op jit(solution)/shard_map/pallas_call | solution.py:525
Async XLA Ops:
  0.0 0.7 %copy-start.2 = (s32[1,1,1024]{2,1,0:T(1,128)S(1)}, s32[1,1,1024]{2,1,0:T(1,128)}, u32[]{:S(2)}) copy-start(s32[1,1,1024]{2,1,0:T(1,128)} %param.7) | copy-start | bytes 12292
  0.7 0.7 %copy-start = (bf16[1,1,1024]{2,1,0:T(2,128)(2,1)S(1)}, bf16[1,1,1024]{2,1,0:T(2,128)(2,1)}, u32[]{:S(2)}) copy-start(bf16[1,1,1024]{2,1,0:T(2,128)(2,1)} %param.9) | copy-start | bytes 6148
  0.7 0.7 %copy-start.1 = (f32[1,1,1024]{2,1,0:T(1,128)S(1)}, f32[1,1,1024]{2,1,0:T(1,128)}, u32[]{:S(2)}) copy-start(f32[1,1,1024]{2,1,0:T(1,128)} %param.10) | copy-start | bytes 12292
  3.1 5.7 %collective-permute-start = (bf16[144,256]{1,0:T(8,128)(2,1)S(1)}, bf16[144,256]{1,0:T(8,128)(2,1)S(1)}, u32[]{:S(2)}, u32[]{:S(2)}) collective-permute-start(bf16[144,256]{1,0:T(8,128)(2,1)S(1)} %get-tuple-element.26), channel_id=1, source_target_pairs={{0,16},{16,0},{32,48},{48,32},{64,80},{80,64},{96,112},{112,96},{1... | collective-permute-start | bytes 221192 | tf_op jit(solution)/shard_map/ppermute | solution.py:554
  3.2 7.5 %collective-permute-start.1 = (bf16[144,256]{1,0:T(8,128)(2,1)S(1)}, bf16[144,256]{1,0:T(8,128)(2,1)S(1)}, u32[]{:S(2)}, u32[]{:S(2)}) collective-permute-start(bf16[144,256]{1,0:T(8,128)(2,1)S(1)} %get-tuple-element.27), channel_id=1, source_target_pairs={{16,32},{32,16},{48,64},{64,48},{80,96},{96,80},{112,128},{128,112... | collective-permute-start | bytes 221192 | tf_op jit(solution)/shard_map/ppermute | solution.py:555
  12.8 11.1 %collective-permute-start.2 = (bf16[864,128]{1,0:T(8,128)(2,1)S(1)}, bf16[864,128]{1,0:T(8,128)(2,1)S(1)}, u32[]{:S(2)}, u32[]{:S(2)}) collective-permute-start(bf16[864,128]{1,0:T(8,128)(2,1)S(1)} %get-tuple-element.29), channel_id=1, source_target_pairs={{0,1},{1,0},{2,3},{3,2},{4,5},{5,4},{6,7},{7,6},{8,9},{9,8},{10,11... | collective-permute-start | bytes 663560 | tf_op jit(solution)/shard_map/ppermute | solution.py:554
  13.7 10.2 %collective-permute-start.3 = (bf16[864,128]{1,0:T(8,128)(2,1)S(1)}, bf16[864,128]{1,0:T(8,128)(2,1)S(1)}, u32[]{:S(2)}, u32[]{:S(2)}) collective-permute-start(bf16[864,128]{1,0:T(8,128)(2,1)S(1)} %get-tuple-element.30), channel_id=1, source_target_pairs={{1,2},{2,1},{3,4},{4,3},{5,6},{6,5},{7,8},{8,7},{9,10},{10,9},{11,... | collective-permute-start | bytes 663560 | tf_op jit(solution)/shard_map/ppermute | solution.py:555
